TPU v7x, 32 devices: a whole 2x2x4 slice. The times are simulated.
32 devices in a mesh: ctx: 8 (over y, x, core), fsdp: 4 (over z).
Axes of the slice: x: 2, y: 2, z: 4, core: 2. Of those that a mesh axis runs over, the one named last changes fastest.
Arguments:
- inputs: bfloat16 [4, 1024, 2304], P('fsdp', 'ctx'), may hold values from -6 to 6
- cotangent: bfloat16 [4, 1024, 2304], P('fsdp', 'ctx'), may hold values from -6 to 6
- weights_in: float32 [2304, 16, 256], P('ctx', 'fsdp'), may hold values from -0.20833333 to 0.20833333
- weights_out: float32 [2304, 8, 256], P('ctx', 'fsdp'), may hold values from -0.125 to 0.125
- ffn_weights: float32 [2304, 3, 9216], P('ctx', None, 'fsdp'), may hold values from -0.125 to 0.125
- norm_gains: float32 [4, 2304], replicated, may hold values from -0.5 to 0.5
- momentum_in: float32 [2304, 16, 256], P('ctx', 'fsdp'), may hold values from -256 to 256
- momentum_out: float32 [2304, 8, 256], P('ctx', 'fsdp'), may hold values from -256 to 256
- ffn_momentum: float32 [2304, 3, 9216], P('ctx', None, 'fsdp'), may hold values from -192 to 192
- gain_first: float32 [4, 2304], replicated, may hold values from -32 to 32
- gain_second: float32 [4, 2304], replicated, may hold values from 204.8 to 819.2
- stretch_order: int32 [16], replicated, may hold values from 0 to 15, each once
Outputs:
- outputs: bfloat16 [4, 1024, 2304], P('fsdp', 'ctx')
- input_grad: float32 [4, 1024, 2304], P('fsdp', 'ctx')
- new_weights_in: float32 [2304, 16, 256], P('ctx', 'fsdp')
- new_weights_out: float32 [2304, 8, 256], P('ctx', 'fsdp')
- new_ffn_weights: float32 [2304, 3, 9216], P('ctx', None, 'fsdp')
- new_momentum_in: float32 [2304, 16, 256], P('ctx', 'fsdp')
- new_momentum_out: float32 [2304, 8, 256], P('ctx', 'fsdp')
- new_ffn_momentum: float32 [2304, 3, 9216], P('ctx', None, 'fsdp')
- new_norm_gains: float32 [4, 2304], replicated
- new_gain_first: float32 [4, 2304], replicated
- new_gain_second: float32 [4, 2304], replicated
Inputs may be any that keep to these rules, and one draw needn't show every extreme that they name: stretch_order is a permutation: every stretch of a sequence stands in exactly one storage slot.
All inputs are finite; a program needn't handle non-finite values.
Results may differ from a plain program's by a relative error of at most 0.025.
Values may be sent and summed in bfloat16 or wider, within the bound.
A program may use at most 320 MiB of HBM per device.

v0:
```python
import math

import jax
import jax.numpy as jnp
from jax import lax
from jax.sharding import PartitionSpec as P

QUERY_HEADS = 8
KEY_VALUE_HEADS = 4
FBLK = 128
ITERS = 5
STEP = 10


SOFT_CAP = 50.0
EXP_SHIFT = 20.0
NORM_EPS = 1e-06
ROPE_THETA = 10000.0
MOMENTUM_DECAY = 0.95
LEARN_RATE = 0.3
WEIGHT_DECAY = 0.01
BETA_ONE = 0.9
BETA_TWO = 0.95
GAIN_RATE = 0.3
ADAM_EPS = 1e-08
NEWTON_A = 3.4445
NEWTON_B = -4.775
NEWTON_C = 2.0315
GELU_SCALE = 0.7978845608028654
GELU_CUBE = 0.044715
PRECISE = lax.Precision.HIGHEST


def rms_scale(values):
    return lax.rsqrt(jnp.mean(values * values, -1, keepdims=True) + NORM_EPS)


def gelu_tanh(values):
    inner = GELU_SCALE * (values + GELU_CUBE * values * values * values)
    return 0.5 * values * (1.0 + jnp.tanh(inner))


def gelu_slope(values):
    inner = GELU_SCALE * (values + GELU_CUBE * values * values * values)
    squashed = jnp.tanh(inner)
    return 0.5 * (1.0 + squashed) + 0.5 * values * (1.0 - squashed * squashed) * GELU_SCALE * (
        1.0 + 3.0 * GELU_CUBE * values * values
    )


def positions_of(row_index, stretch_order, stretch_rows):
    stretch_slot = row_index // stretch_rows
    slot_table = jnp.arange(stretch_order.shape[0], dtype=jnp.int32)
    picked = jnp.sum(
        jnp.where(stretch_slot[:, None] == slot_table[None, :], stretch_order[None, :], 0), axis=1
    )
    return picked * stretch_rows + row_index % stretch_rows


def rope_tables(places, width):
    half_width = width // 2
    frequency = ROPE_THETA ** (-(2.0 * jnp.arange(half_width, dtype=jnp.float32)) / width)
    angles = places.astype(jnp.float32)[:, None] * frequency[None, :]
    return (jnp.cos(angles), jnp.sin(angles))


def apply_rotation(values, cosine_lookup, sine_lookup):
    half_width = values.shape[-1] // 2
    first_half = values[..., :half_width]
    second_half = values[..., half_width:]
    cosine_part = cosine_lookup[:, None, :]
    sine_part = sine_lookup[:, None, :]
    return jnp.concatenate(
        [
            first_half * cosine_part - second_half * sine_part,
            second_half * cosine_part + first_half * sine_part,
        ],
        -1,
    )


def newton_step(matrices, gram_matrix):
    polynomial = NEWTON_B * gram_matrix + NEWTON_C * jnp.einsum(
        "jef,jfg->jeg", gram_matrix, gram_matrix, precision=PRECISE
    )
    return NEWTON_A * matrices + jnp.einsum("jef,jfd->jed", polynomial, matrices, precision=PRECISE)


def self_gram(matrices):
    return jnp.einsum("jed,jfd->jef", matrices, matrices, precision=PRECISE)


def gram_pair(head_part, ffn_part):
    return (
        lax.psum(self_gram(head_part).astype(jnp.bfloat16), "ctx").astype(jnp.float32),
        lax.psum(self_gram(ffn_part).astype(jnp.bfloat16), "ctx").astype(jnp.float32),
    )


def normalize(matrices, gram_matrix):
    diag_sum = jnp.sum(jnp.diagonal(gram_matrix, axis1=1, axis2=2), -1)
    factor = 1.0 / (jnp.sqrt(diag_sum) + 1e-07)
    return (matrices * factor[:, None, None], gram_matrix * (factor * factor)[:, None, None])


def local(
    inputs,
    cotangent,
    weights_in,
    weights_out,
    ffn_weights,
    norm_gains,
    momentum_in,
    momentum_out,
    ffn_momentum,
    gain_first,
    gain_second,
    stretch_order,
):
    sequence_count, count_of_rows, model_width = inputs.shape
    stretch_rows = count_of_rows // 2
    in_local = weights_in.shape[1]
    local_rows = weights_in.shape[0]
    head_extent = weights_in.shape[2]
    ffn_local = ffn_weights.shape[2]
    block_count = ffn_local // FBLK
    query_group_width = QUERY_HEADS // KEY_VALUE_HEADS
    input_matrix_count = QUERY_HEADS + 2 * KEY_VALUE_HEADS
    token_count = sequence_count * count_of_rows
    context_index = lax.axis_index("ctx")
    shard_index = lax.axis_index("fsdp")
    context_size = lax.axis_size("ctx")
    own_places = positions_of(
        context_index * count_of_rows + jnp.arange(count_of_rows, dtype=jnp.int32),
        stretch_order,
        stretch_rows,
    )
    cosine_lookup, sine_lookup = rope_tables(own_places, head_extent)
    query_scale = head_extent ** (-0.5)
    in_cut, out_cut, ffn_low = (
        lax.all_gather(weights_in.astype(jnp.bfloat16), "ctx", axis=0, tiled=True),
        lax.all_gather(weights_out.astype(jnp.bfloat16), "ctx", axis=0, tiled=True),
        lax.all_gather(ffn_weights.astype(jnp.bfloat16), "ctx", axis=0, tiled=True),
    )
    w_in, w_out = (
        lax.all_gather(in_cut, "fsdp", axis=1, tiled=True),
        lax.all_gather(out_cut, "fsdp", axis=1, tiled=True),
    )
    flat_in = inputs.astype(jnp.float32).reshape(token_count, model_width)
    inv_pre = rms_scale(flat_in)
    normed = flat_in * inv_pre
    normed_low = (normed * (1.0 + norm_gains[0])).astype(jnp.bfloat16)
    projection_result = jnp.einsum(
        "td,dje->tje", normed_low, w_in, preferred_element_type=jnp.float32
    )
    projection_result = projection_result.reshape(
        sequence_count, count_of_rows, input_matrix_count, head_extent
    )
    query_reduced = (
        apply_rotation(projection_result[:, :, :QUERY_HEADS], cosine_lookup, sine_lookup)
        * query_scale
    ).astype(jnp.bfloat16)
    query_reduced = query_reduced.reshape(
        sequence_count, count_of_rows, KEY_VALUE_HEADS, query_group_width, head_extent
    )
    key_reduced = apply_rotation(
        projection_result[:, :, QUERY_HEADS : QUERY_HEADS + KEY_VALUE_HEADS],
        cosine_lookup,
        sine_lookup,
    ).astype(jnp.bfloat16)
    value_reduced = projection_result[:, :, QUERY_HEADS + KEY_VALUE_HEADS :].astype(jnp.bfloat16)
    key_all, value_all = (
        lax.all_gather(key_reduced, "ctx", axis=1, tiled=True),
        lax.all_gather(value_reduced, "ctx", axis=1, tiled=True),
    )
    block_devices = math.gcd(context_size, max(1, 512 // count_of_rows))
    key_span = block_devices * count_of_rows
    key_blocks_count = context_size // block_devices

    def key_mask(first_row, row_span):
        key_places = positions_of(
            first_row + jnp.arange(row_span, dtype=jnp.int32), stretch_order, stretch_rows
        )
        return key_places[None, :] <= own_places[:, None]

    def block_slices(block_id):
        first_row = block_id * key_span
        key_piece = lax.dynamic_slice_in_dim(key_all, first_row, key_span, 1)
        value_piece = lax.dynamic_slice_in_dim(value_all, first_row, key_span, 1)
        return (first_row, key_piece, value_piece)

    def attend(block_id, carried):
        first_row, key_piece, value_piece = block_slices(block_id)
        visible_mask = key_mask(first_row, key_span)
        row_total, numerator = carried
        scores = jnp.einsum(
            "srkge,snke->skgrn", query_reduced, key_piece, preferred_element_type=jnp.float32
        )
        exponent = jnp.where(
            visible_mask, jnp.exp(SOFT_CAP * jnp.tanh(scores / SOFT_CAP) - EXP_SHIFT), 0.0
        )
        row_total = row_total + jnp.sum(exponent, -1)
        numerator = numerator + jnp.einsum(
            "skgrn,snke->srkge",
            exponent.astype(jnp.bfloat16),
            value_piece,
            preferred_element_type=jnp.float32,
        )
        return (row_total, numerator)

    empty_running_total = jnp.zeros(
        (sequence_count, KEY_VALUE_HEADS, query_group_width, count_of_rows), jnp.float32
    )
    empty_numerator = jnp.zeros(
        (sequence_count, count_of_rows, KEY_VALUE_HEADS, query_group_width, head_extent),
        jnp.float32,
    )
    row_total, numerator = lax.fori_loop(
        0, key_blocks_count, attend, (empty_running_total, empty_numerator)
    )
    total_rows = jnp.transpose(row_total, (0, 3, 1, 2))[..., None]
    attended = numerator / total_rows
    attended_low = attended.astype(jnp.bfloat16).reshape(token_count, QUERY_HEADS, head_extent)
    branch = jnp.einsum("the,dhe->td", attended_low, w_out, preferred_element_type=jnp.float32)
    inv_post = rms_scale(branch)
    post_hat = branch * inv_post
    mixed = flat_in + post_hat * (1.0 + norm_gains[1])
    inv_mid = rms_scale(mixed)
    mid_hat = mixed * inv_mid
    mid_low = (mid_hat * (1.0 + norm_gains[2])).astype(jnp.bfloat16)
    mid_rows, cot_rows = (
        lax.all_gather(mid_low, "fsdp", axis=0, tiled=True),
        lax.all_gather(cotangent.reshape(token_count, model_width), "fsdp", axis=0, tiled=True),
    )
    gate_up = jnp.einsum(
        "td,dmf->tmf", mid_rows, ffn_low[:, :2], preferred_element_type=jnp.float32
    )
    gate_act = gelu_tanh(gate_up[:, 0])
    hidden_low = (gate_act * gate_up[:, 1]).astype(jnp.bfloat16)
    ffn_partial = jnp.einsum(
        "tf,df->td", hidden_low, ffn_low[:, 2], preferred_element_type=jnp.float32
    )
    ffn_branch = lax.psum(ffn_partial, "fsdp")
    inv_late = rms_scale(ffn_branch)
    late_hat = ffn_branch * inv_late
    own_late = lax.dynamic_slice_in_dim(late_hat, shard_index * token_count, token_count, 0)
    outputs = (
        (mixed + own_late * (1.0 + norm_gains[3]))
        .astype(jnp.bfloat16)
        .reshape(sequence_count, count_of_rows, model_width)
    )
    upstream = cotangent.reshape(token_count, model_width).astype(jnp.float32)
    gain_late_grad = jnp.sum(upstream * own_late, 0)
    late_scaled = cot_rows.astype(jnp.float32) * (1.0 + norm_gains[3])
    late_grad = inv_late * (
        late_scaled - late_hat * jnp.mean(late_scaled * late_hat, -1, keepdims=True)
    )
    late_low = late_grad.astype(jnp.bfloat16)
    hidden_grad = jnp.einsum(
        "td,df->tf", late_low, ffn_low[:, 2], preferred_element_type=jnp.float32
    )
    pair_low = jnp.stack(
        [hidden_grad * gate_up[:, 1] * gelu_slope(gate_up[:, 0]), hidden_grad * gate_act], 1
    ).astype(jnp.bfloat16)
    mid_grad = lax.psum_scatter(
        jnp.einsum("tmf,dmf->td", pair_low, ffn_low[:, :2], preferred_element_type=jnp.float32),
        "fsdp",
        scatter_dimension=0,
        tiled=True,
    )
    gain_mid_grad = jnp.sum(mid_grad * mid_hat, 0)
    mid_scaled = mid_grad * (1.0 + norm_gains[2])
    mixed_grad = upstream + inv_mid * (
        mid_scaled - mid_hat * jnp.mean(mid_scaled * mid_hat, -1, keepdims=True)
    )
    gain_post_grad = jnp.sum(mixed_grad * post_hat, 0)
    hat_grad = mixed_grad * (1.0 + norm_gains[1])
    branch_grad = inv_post * (
        hat_grad - post_hat * jnp.mean(hat_grad * post_hat, -1, keepdims=True)
    )
    branch_low = branch_grad.astype(jnp.bfloat16)
    attended_gradient = jnp.einsum(
        "td,dhe->the", branch_low, w_out, preferred_element_type=jnp.float32
    )
    attended_gradient = attended_gradient.reshape(
        sequence_count, count_of_rows, KEY_VALUE_HEADS, query_group_width, head_extent
    )
    numerator_low = (attended_gradient / total_rows).astype(jnp.bfloat16)
    row_term = jnp.sum(attended_gradient * attended, -1) / total_rows[..., 0]
    row_gap = jnp.transpose(row_term, (0, 2, 3, 1))[..., None]

    def query_side(block_id, query_acc):
        first_row, key_piece, value_piece = block_slices(block_id)
        visible_mask = key_mask(first_row, key_span)
        scores = jnp.einsum(
            "srkge,snke->skgrn", query_reduced, key_piece, preferred_element_type=jnp.float32
        )
        squashed = jnp.tanh(scores / SOFT_CAP)
        exponent = jnp.where(visible_mask, jnp.exp(SOFT_CAP * squashed - EXP_SHIFT), 0.0)
        pulled = jnp.einsum(
            "srkge,snke->skgrn", numerator_low, value_piece, preferred_element_type=jnp.float32
        )
        score_low = (exponent * (pulled - row_gap) * (1.0 - squashed * squashed)).astype(
            jnp.bfloat16
        )
        return query_acc + jnp.einsum(
            "skgrn,snke->srkge", score_low, key_piece, preferred_element_type=jnp.float32
        )

    query_grad = lax.fori_loop(0, key_blocks_count, query_side, jnp.zeros_like(empty_numerator))
    all_terms = lax.all_gather(row_term, "ctx", axis=1, tiled=True)
    query_piece = lax.all_gather(query_reduced, "ctx", axis=1, tiled=True)
    grad_piece = lax.all_gather(numerator_low, "ctx", axis=1, tiled=True)
    row_span = query_piece.shape[1]
    query_places = positions_of(jnp.arange(row_span, dtype=jnp.int32), stretch_order, stretch_rows)
    visible_mask = own_places[None, :] <= query_places[:, None]
    piece_gap = jnp.transpose(all_terms, (0, 2, 3, 1))[..., None]
    scores = jnp.einsum(
        "snkge,srke->skgnr", query_piece, key_reduced, preferred_element_type=jnp.float32
    )
    squashed = jnp.tanh(scores / SOFT_CAP)
    exponent = jnp.where(visible_mask, jnp.exp(SOFT_CAP * squashed - EXP_SHIFT), 0.0)
    pulled = jnp.einsum(
        "snkge,srke->skgnr", grad_piece, value_reduced, preferred_element_type=jnp.float32
    )
    score_low = (exponent * (pulled - piece_gap) * (1.0 - squashed * squashed)).astype(jnp.bfloat16)
    value_acc = jnp.einsum(
        "skgnr,snkge->srke",
        exponent.astype(jnp.bfloat16),
        grad_piece,
        preferred_element_type=jnp.float32,
    )
    key_acc = jnp.einsum(
        "skgnr,snkge->srke", score_low, query_piece, preferred_element_type=jnp.float32
    )
    query_pre = apply_rotation(
        query_grad.reshape(sequence_count, count_of_rows, QUERY_HEADS, head_extent) * query_scale,
        cosine_lookup,
        -sine_lookup,
    )
    key_pre = apply_rotation(key_acc, cosine_lookup, -sine_lookup)
    projected_grad = jnp.concatenate([query_pre, key_pre, value_acc], 2).astype(jnp.bfloat16)
    projected_grad = projected_grad.reshape(token_count, input_matrix_count, head_extent)
    normed_grad = jnp.einsum(
        "tje,dje->td", projected_grad, w_in, preferred_element_type=jnp.float32
    )
    gain_pre_grad = jnp.sum(normed_grad * normed, 0)
    pre_hat_grad = normed_grad * (1.0 + norm_gains[0])
    input_grad = mixed_grad + inv_pre * (
        pre_hat_grad - normed * jnp.mean(pre_hat_grad * normed, -1, keepdims=True)
    )
    input_grad = input_grad.reshape(sequence_count, count_of_rows, model_width)
    gain_grad = lax.psum(
        jnp.stack([gain_pre_grad, gain_post_grad, gain_mid_grad, gain_late_grad]), ("ctx", "fsdp")
    )
    in_width = input_matrix_count * head_extent
    out_width = QUERY_HEADS * head_extent
    grad_a = jnp.einsum(
        "td,tje->dje", normed_low, projected_grad, preferred_element_type=jnp.float32
    )
    grad_b = jnp.einsum("td,tje->dje", branch_low, attended_low, preferred_element_type=jnp.float32)
    grad_c = jnp.einsum("td,tmf->dmf", mid_rows, pair_low, preferred_element_type=jnp.float32)
    grad_d = jnp.einsum("td,tf->df", late_low, hidden_low, preferred_element_type=jnp.float32)
    row_sums = lax.psum_scatter(
        jnp.concatenate(
            [
                grad_a.reshape(lax.axis_size("ctx") * local_rows, in_width),
                grad_b.reshape(lax.axis_size("ctx") * local_rows, out_width),
                grad_c.reshape(lax.axis_size("ctx") * local_rows, 2 * ffn_local),
                grad_d,
            ],
            1,
        ).astype(jnp.bfloat16),
        "ctx",
        scatter_dimension=0,
        tiled=True,
    ).astype(jnp.float32)
    in_grad, out_grad = (
        lax.psum_scatter(
            row_sums[:, :in_width]
            .reshape(local_rows, input_matrix_count, head_extent)
            .astype(jnp.bfloat16),
            "fsdp",
            scatter_dimension=1,
            tiled=True,
        ).astype(jnp.float32),
        lax.psum_scatter(
            row_sums[:, in_width : in_width + out_width]
            .reshape(local_rows, QUERY_HEADS, head_extent)
            .astype(jnp.bfloat16),
            "fsdp",
            scatter_dimension=1,
            tiled=True,
        ).astype(jnp.float32),
    )
    ffn_grad = row_sums[:, in_width + out_width :].reshape(local_rows, 3, ffn_local)
    momentum_new_in = MOMENTUM_DECAY * momentum_in + in_grad
    momentum_new_out = MOMENTUM_DECAY * momentum_out + out_grad
    momentum_new_ffn = MOMENTUM_DECAY * ffn_momentum + ffn_grad
    head_update = jnp.concatenate(
        [in_grad + MOMENTUM_DECAY * momentum_new_in, out_grad + MOMENTUM_DECAY * momentum_new_out],
        1,
    )
    ffn_update = ffn_grad + MOMENTUM_DECAY * momentum_new_ffn
    head_matrices = jnp.transpose(head_update, (1, 2, 0))
    ffn_blocks = jnp.transpose(ffn_update.reshape(local_rows, 3 * block_count, FBLK), (1, 2, 0))
    head_gram, ffn_gram = gram_pair(head_matrices, ffn_blocks)
    head_matrices, head_gram = normalize(head_matrices, head_gram)
    ffn_blocks, ffn_gram = normalize(ffn_blocks, ffn_gram)
    for iteration in range(ITERS):
        if iteration > 0:
            head_gram, ffn_gram = gram_pair(head_matrices, ffn_blocks)
        head_matrices = newton_step(head_matrices, head_gram)
        ffn_blocks = newton_step(ffn_blocks, ffn_gram)
    head_part = jnp.transpose(head_matrices, (2, 0, 1))
    ffn_part = jnp.transpose(ffn_blocks, (2, 0, 1)).reshape(local_rows, 3, ffn_local)
    shrink = 1.0 - LEARN_RATE * WEIGHT_DECAY
    head_rate = LEARN_RATE * (model_width / head_extent) ** 0.5
    ffn_rate = LEARN_RATE * (model_width / FBLK) ** 0.5
    new_weights_in = weights_in * shrink - head_rate * head_part[:, :in_local]
    new_weights_out = weights_out * shrink - head_rate * head_part[:, in_local:]
    new_ffn_weights = ffn_weights * shrink - ffn_rate * ffn_part
    new_gain_first = BETA_ONE * gain_first + (1.0 - BETA_ONE) * gain_grad
    new_gain_second = BETA_TWO * gain_second + (1.0 - BETA_TWO) * gain_grad * gain_grad
    corrected_one = new_gain_first / (1.0 - BETA_ONE**STEP)
    corrected_two = new_gain_second / (1.0 - BETA_TWO**STEP)
    new_norm_gains = norm_gains - GAIN_RATE * corrected_one / (jnp.sqrt(corrected_two) + ADAM_EPS)
    return (
        outputs,
        input_grad,
        new_weights_in,
        new_weights_out,
        new_ffn_weights,
        momentum_new_in,
        momentum_new_out,
        momentum_new_ffn,
        new_norm_gains,
        new_gain_first,
        new_gain_second,
    )


def solution(mesh):
    return jax.shard_map(
        local,
        mesh=mesh,
        in_specs=(
            P("fsdp", "ctx", None),
            P("fsdp", "ctx", None),
            P("ctx", "fsdp", None),
            P("ctx", "fsdp", None),
            P("ctx", None, "fsdp"),
            P(),
            P("ctx", "fsdp", None),
            P("ctx", "fsdp", None),
            P("ctx", None, "fsdp"),
            P(),
            P(),
            P(),
        ),
        out_specs=(
            P("fsdp", "ctx", None),
            P("fsdp", "ctx", None),
            P("ctx", "fsdp", None),
            P("ctx", "fsdp", None),
            P("ctx", None, "fsdp"),
            P("ctx", "fsdp", None),
            P("ctx", "fsdp", None),
            P("ctx", None, "fsdp"),
            P(),
            P(),
            P(),
        ),
        check_vma=False,
    )
```

profile of v0, /device:TPU:0, one launch (start us, length us, event | category | flops | bytes accessed | tf_op | source)
XLA Modules:
  0.0 2535.8 jit_solution(3155411035599779007)
XLA Ops:
  9.6 42.6 %all-gather.13.cloned.1.call-done = bf16[2304,4,256]{2,0,1:T(8,128)(2,1)} async-done(((bf16[288,4,256]{2,0,1:T(8,128)(2,1)}), bf16[2304,4,256]{2,0,1:T(8,128)(2,1)}) %all-gather.13.cloned.1.call-update) | async-done | bytes 4718608 | tf_op jit(solution)/shard_map/all_gather | solution.py:141
  55.5 320.9 %all-gather.15.cloned.1.call-done = bf16[2304,16,256]{2,0,1:T(8,128)(2,1)} async-done(((bf16[2304,4,256]{2,0,1:T(8,128)(2,1)}), bf16[2304,16,256]{2,0,1:T(8,128)(2,1)}) %all-gather.15.cloned.1.call-update) | async-done | bytes 18874384 | tf_op jit(solution)/shard_map/all_gather | solution.py:146
  376.4 7.8 convolution_bitcast_fusion.4
  386.0 20.7 all-gather.21.cloned.1.call-done
  408.2 28.7 %all-gather.17.cloned.1.call-done = bf16[1,1024,4,256]{3,1,2,0:T(8,128)(2,1)} async-done(((bf16[1,128,4,256]{3,1,2,0:T(8,128)(2,1)}), bf16[1,1024,4,256]{3,1,2,0:T(8,128)(2,1)}) %all-gather.17.cloned.1.call-update) | async-done | bytes 2097168 | tf_op jit(solution)/shard_map/all_gather | solution.py:173
  437.0 30.3 %all-gather.19.cloned.1.call-done = bf16[1,1024,4,256]{3,1,2,0:T(8,128)(2,1)} async-done(((bf16[1,128,4,256]{3,1,2,0:T(8,128)(2,1)}), bf16[1,1024,4,256]{3,1,2,0:T(8,128)(2,1)}) %all-gather.19.cloned.1.call-update) | async-done | bytes 2097168 | tf_op jit(solution)/shard_map/all_gather | solution.py:174
  467.2 9.1 while.34
  476.9 158.5 %all-gather.23.cloned.1.call-done = bf16[2304,8,256]{2,0,1:T(8,128)(2,1)} async-done(((bf16[2304,2,256]{2,0,1:T(8,128)(2,1)}), bf16[2304,8,256]{2,0,1:T(8,128)(2,1)}) %all-gather.23.cloned.1.call-update) | async-done | bytes 9437200 | tf_op jit(solution)/shard_map/all_gather | solution.py:147
  635.5 6.9 multiply_reduce_fusion.6
  644.9 5.6 convert_element_type.205
  650.8 42.9 %all-gather.25.cloned.1.call-done = bf16[512,2304]{1,0:T(8,128)(2,1)} async-done(((bf16[128,2304]{1,0:T(8,128)(2,1)}), bf16[512,2304]{1,0:T(8,128)(2,1)}) %all-gather.25.cloned.1.call-update) | async-done | bytes 2359312 | tf_op jit(solution)/shard_map/all_gather | solution.py:232
  693.7 154.9 %all-gather.27.cloned.1.call-done = bf16[2304,3,2304]{2,0,1:T(8,128)(2,1)} async-done(((bf16[288,3,2304]{2,0,1:T(8,128)(2,1)}), bf16[2304,3,2304]{2,0,1:T(8,128)(2,1)}) %all-gather.27.cloned.1.call-update) | async-done | bytes 31850512 | tf_op jit(solution)/shard_map/all_gather | solution.py:143
  848.6 18.2 fusion.51
  866.8 15.6 fusion.56
  884.3 170.3 %all-reduce.12.cloned.1.call-done = f32[512,2304]{1,0:T(8,128)} async-done(((f32[512,2304]{1,0:T(8,128)}), f32[512,2304]{1,0:T(8,128)}) %all-reduce.12.cloned.1.call-update) | async-done | bytes 4718608 | tf_op jit(solution)/shard_map/psum | solution.py:243
  1057.3 48.2 %all-gather.33.cloned.1.call-done = bf16[1,512,2304]{2,1,0:T(8,128)(2,1)} async-done(((bf16[1,128,2304]{2,1,0:T(8,128)(2,1)}), bf16[1,512,2304]{2,1,0:T(8,128)(2,1)}) %all-gather.33.cloned.1.call-update) | async-done | bytes 2359312 | tf_op jit(solution)/shard_map/all_gather | solution.py:233
  1113.9 12.2 fusion.140
  1128.3 15.8 fusion.67
  1146.2 5.7 fusion.98
  1151.9 79.7 %reduce-scatter.5.cloned.1.call-done = f32[128,2304]{1,0:T(8,128)} async-done(((f32[512,2304]{1,0:T(8,128)}), f32[128,2304]{1,0:T(8,128)}) %reduce-scatter.5.cloned.1.call-update) | async-done | bytes 1179664 | tf_op jit(solution)/shard_map/reduce_scatter | solution.py:265
  1237.8 5.2 fusion.280
  1244.9 14.1 convolution_convert_fusion.2
  1259.0 15.4 copy.147
  1274.4 17.1 convolution_convert_fusion
  1291.4 28.4 %copy.146 = bf16[2304,4608]{1,0:T(8,128)(2,1)} copy(bf16[2304,4608]{0,1:T(8,128)(2,1)} %bitcast.530) | data formatting | bytes 42467328 | tf_op jit(solution)/shard_map/reshape | solution.py:369
  1319.8 12.5 while.35
  1333.9 5.1 convolution_convert_fusion.3
  1339.0 13.1 copy.145
  1352.1 8.9 all_gather.47
  1361.9 7.6 fusion.229
  1376.3 9.2 convolution_convert_fusion.1
  1385.5 40.1 %pad_maximum_fusion = bf16[2304,13056]{1,0:T(8,128)(2,1)} fusion(bf16[2304,2304]{1,0:T(8,128)(2,1)} %copy.147, bf16[2304,4608]{1,0:T(8,128)(2,1)} %copy.146, bf16[2304,2048]{1,0:T(8,128)(2,1)} %copy.145, bf16[2304,4096]{1,0:T(8,128)(2,1)} %convolution_convert_fusion.1), kind=kLoop, calls=%fused_computation.74 | loop fusion | flops 240648192 | bytes 120324096 | tf_op jit(solution)/shard_map/concatenate | solution.py:365
  1425.7 337.1 %reduce-scatter.7.cloned.1.call-done = bf16[288,13056]{1,0:T(8,128)(2,1)} async-done(((bf16[2304,13056]{1,0:T(8,128)(2,1)}), bf16[288,13056]{1,0:T(8,128)(2,1)}) %reduce-scatter.7.cloned.1.call-update) | async-done | bytes 7520272 | tf_op jit(solution)/shard_map/reduce_scatter | solution.py:364
  1768.6 5.9 slice_convert_fusion
  1774.5 12.3 reshape.723
  1786.8 18.8 fusion.53
  1805.7 13.4 reshape.711
  1819.0 32.8 %fusion.182 = bf16[54,128,128]{2,1,0:T(8,128)(2,1)} fusion(f32[288,54,128]{2,1,0:T(8,128)} %reshape.711), kind=kOutput, calls=%fused_computation.243 | convolution fusion | flops 3058532352 | bytes 9732096 | tf_op jit(solution)/shard_map/jed,jfd->jef/dot_general | solution.py:90
  1861.7 64.5 %all-reduce.22.cloned.1.call-done = (bf16[6,256,256]{2,1,0:T(8,128)(2,1)}, bf16[54,128,128]{2,1,0:T(8,128)(2,1)}) async-done(((bf16[6,256,256]{2,1,0:T(8,128)(2,1)}, bf16[54,128,128]{2,1,0:T(8,128)(2,1)}), (bf16[6,256,256]{2,1,0:T(8,128)(2,1)}, bf16[54,128,128]{2,1,0:T(8,128)(2,1)})) %all-reduce.22.cloned.1.call-update) | async-done | bytes 2555920 | tf_op jit(solution)/shard_map/psum | solution.py:95
  1926.2 15.7 copy.152
  1962.7 5.9 fusion.125
  1968.6 26.7 %multiply_add_fusion.4 = (f32[54,128,288]{1,2,0:T(8,128)}, f32[54,128,288]{1,2,0:T(8,128)}) fusion(f32[288,54,128]{2,1,0:T(8,128)} %reshape.711, f32[54]{0:T(128)S(1)} %get-tuple-element.632, f32[54,128,128]{2,1,0:T(8,128)} %fusion.125, f32[54]{0:T(128)S(1)} %get-tuple-element.631, bf16[54,128,128]{2,1,0:T(8,128)(2,1)S(1)} %copy-done.11), kind=kOutput, calls=%fused_computation.107 | convolution fusion | flops 3070033920 | bytes 29196720 | tf_op jit(solution)/shard_map/jef,jfd->jed/dot_general | solution.py:86
  1995.2 23.9 convolution_convert_fusion.6
  2019.5 63.8 %all-reduce.20.cloned.1.call-done = (bf16[6,256,256]{2,1,0:T(8,128)(2,1)}, bf16[54,128,128]{2,1,0:T(8,128)(2,1)}) async-done(((bf16[6,256,256]{2,1,0:T(8,128)(2,1)}, bf16[54,128,128]{2,1,0:T(8,128)(2,1)}), (bf16[6,256,256]{2,1,0:T(8,128)(2,1)}, bf16[54,128,128]{2,1,0:T(8,128)(2,1)})) %all-reduce.20.cloned.1.call-update) | async-done | bytes 2555920 | tf_op jit(solution)/shard_map/psum | solution.py:95
  2085.1 5.5 multiply_add_fusion.13
  2098.2 23.2 multiply_add_fusion.3
  2121.4 24.0 convolution_convert_fusion.5
  2146.2 63.3 %all-reduce.18.cloned.1.call-done = (bf16[6,256,256]{2,1,0:T(8,128)(2,1)}, bf16[54,128,128]{2,1,0:T(8,128)(2,1)}) async-done(((bf16[6,256,256]{2,1,0:T(8,128)(2,1)}, bf16[54,128,128]{2,1,0:T(8,128)(2,1)}), (bf16[6,256,256]{2,1,0:T(8,128)(2,1)}, bf16[54,128,128]{2,1,0:T(8,128)(2,1)})) %all-reduce.18.cloned.1.call-update) | async-done | bytes 2555920 | tf_op jit(solution)/shard_map/psum | solution.py:95
  2214.7 5.1 convolution_convert_fusion.8
  2220.5 9.6 fusion.112
  2230.1 25.2 convolution_convert_fusion.4
  2256.4 14.7 fusion.247
  2271.1 39.8 %psum.95 = f32[4,2304]{1,0:T(4,128)S(1)} all-reduce(f32[4,2304]{1,0:T(4,128)S(1)} %pad_maximum_fusion.10), channel_id=1, replica_groups=mesh['ctx'=8,'fsdp'=4] {'ctx','fsdp'}, use_global_device_ids=true, to_apply=%region_39.40 | all-reduce | flops 9216 | bytes 73728 | tf_op jit(solution)/shard_map/psum | solution.py:353
  2311.6 8.4 all-reduce.16.cloned.1.call-done
  2325.6 5.4 convolution_convert_fusion.7
  2333.4 12.5 fusion.107
  2345.9 34.1 %fusion.181 = bf16[54,128,128]{2,1,0:T(8,128)(2,1)} fusion(f32[54,128,288]{1,2,0:T(8,128)} %fusion.107, f32[54,128,288]{1,2,0:T(8,128)} %fusion.112, f32[54,128,288]{1,2,0:T(8,128)} %get-tuple-element.679), kind=kOutput, calls=%fused_computation.242 | convolution fusion | flops 3066494976 | bytes 25657344 | tf_op jit(solution)/shard_map/jed,jfd->jef/dot_general | solution.py:90
  2384.7 9.0 copy.165
  2396.8 47.3 %all-reduce.14.cloned.1.call-done = (bf16[6,256,256]{2,1,0:T(8,128)(2,1)}, bf16[54,128,128]{2,1,0:T(8,128)(2,1)}) async-done(((bf16[6,256,256]{2,1,0:T(8,128)(2,1)}, bf16[54,128,128]{2,1,0:T(8,128)(2,1)}), (bf16[6,256,256]{2,1,0:T(8,128)(2,1)}, bf16[54,128,128]{2,1,0:T(8,128)(2,1)})) %all-reduce.14.cloned.1.call-update) | async-done | bytes 2555920 | tf_op jit(solution)/shard_map/psum | solution.py:95
  2446.3 6.4 bitcast_add_fusion.6
  2458.7 29.2 %fusion.57 = f32[288,54,128]{2,0,1:T(8,128)} fusion(f32[54,128,288]{1,2,0:T(8,128)} %fusion.107, f32[54,128,288]{1,2,0:T(8,128)} %fusion.112, f32[54,128,288]{1,2,0:T(8,128)} %get-tuple-element.680, f32[54,128,288]{1,2,0:T(8,128)} %get-tuple-element.676, f32[288,54,128]{2,1,0:T(8,128)} %reshape.711, f32[54]{0:T(128)S(1)} %get-tuple-element.632, ...), kind=kOutput, calls=%fused_computation.92 | convolution fusion | flops 3093037056 | bytes 61047000 | tf_op jit(solution)/shard_map/jef,jfd->jed/dot_general | solution.py:86
  2487.8 11.1 copy.159
  2498.9 12.6 mul.1053
  2511.5 12.5 fusion.54
  (332 shorter events, 150.7 us)
Async XLA Ops:
  7.2 45.0 %all-gather.13.cloned.1.call-start = ((), (), s32[]{:S(2)}) async-start(), calls=%async_computation.4 | async-start | bytes 5308416 | tf_op jit(solution)/shard_map/all_gather | solution.py:141
  9.5 366.8 %all-gather.15.cloned.1.call-start = ((), (), s32[]{:S(2)}) async-start(), calls=%async_computation.5 | async-start | bytes 23592960 | tf_op jit(solution)/shard_map/all_gather | solution.py:146
  52.2 354.6 %all-gather.21.cloned.1.call-start = ((), (), s32[]{:S(2)}) async-start(), calls=%async_computation.8 | async-start | bytes 2654208 | tf_op jit(solution)/shard_map/all_gather | solution.py:142
  54.0 383.0 %all-gather.17.cloned.1.call-start = ((), (), s32[]{:S(2)}) async-start(), calls=%async_computation.6 | async-start | bytes 2359296 | tf_op jit(solution)/shard_map/all_gather | solution.py:173
  54.3 329.9 %copy-start.50 = (f32[2304]{0:T(1024)}, f32[2304]{0:T(1024)S(1)}, u32[]{:S(2)}) copy-start(f32[2304]{0:T(1024)S(1)} %get-tuple-element.583) | copy-start | bytes 27652
  54.5 329.7 %copy-start.62 = (f32[128]{0:T(128)}, f32[128]{0:T(128)S(1)}, u32[]{:S(2)}) copy-start(f32[128]{0:T(128)S(1)} %add_rsqrt_fusion.3) | copy-start | bytes 1540
  55.5 351.4 %copy-start.43 = (f32[128,128]{1,0:T(8,128)}, f32[128,128]{1,0:T(8,128)S(1)}, u32[]{:S(2)}) copy-start(f32[128,128]{1,0:T(8,128)S(1)} %get-tuple-element.669) | copy-start | bytes 196612
  384.2 22.5 copy-start.23
  385.2 82.0 %all-gather.19.cloned.1.call-start = ((), (), s32[]{:S(2)}) async-start(), calls=%async_computation.7 | async-start | bytes 2359296 | tf_op jit(solution)/shard_map/all_gather | solution.py:174
  386.0 249.5 %all-gather.23.cloned.1.call-start = ((), (), s32[]{:S(2)}) async-start(), calls=%async_computation.9 | async-start | bytes 11796480 | tf_op jit(solution)/shard_map/all_gather | solution.py:147
  406.8 286.9 %all-gather.25.cloned.1.call-start = ((), (), s32[]{:S(2)}) async-start(), calls=%async_computation.10 | async-start | bytes 2949120 | tf_op jit(solution)/shard_map/all_gather | solution.py:232
  476.3 166.0 %copy-start.3 = (bf16[1,128,4,2,256]{4,1,3,2,0:T(8,128)(2,1)}, bf16[1,128,4,2,256]{4,1,3,2,0:T(8,128)(2,1)S(1)}, u32[]{:S(2)}) copy-start(bf16[1,128,4,2,256]{4,1,3,2,0:T(8,128)(2,1)S(1)} %get-tuple-element.905) | copy-start | bytes 1572868
  476.7 165.7 %copy-start.20 = (f32[1,128,4,2,256]{4,1,3,2,0:T(8,128)}, f32[1,128,4,2,256]{4,1,3,2,0:T(8,128)S(1)}, u32[]{:S(2)}) copy-start(f32[1,128,4,2,256]{4,1,3,2,0:T(8,128)S(1)} %copy.132) | copy-start | bytes 3145732
  476.9 165.5 %copy-start.29 = (bf16[1,128,4,2,256]{4,1,3,2,0:T(8,128)(2,1)}, bf16[1,128,4,2,256]{4,1,3,2,0:T(8,128)(2,1)S(1)}, u32[]{:S(2)}) copy-start(bf16[1,128,4,2,256]{4,1,3,2,0:T(8,128)(2,1)S(1)} %fusion.287) | copy-start | bytes 1572868
  644.8 203.7 %all-gather.27.cloned.1.call-start = ((), (), s32[]{:S(2)}) async-start(), calls=%async_computation.11 | async-start | bytes 35831808 | tf_op jit(solution)/shard_map/all_gather | solution.py:143
  650.5 404.1 %all-reduce.12.cloned.1.call-start = ((), (), s32[]{:S(2)}) async-start(), calls=%async_computation.12 | async-start | bytes 9437184 | tf_op jit(solution)/shard_map/psum | solution.py:243
  882.5 223.0 %all-gather.33.cloned.1.call-start = ((), (), s32[]{:S(2)}) async-start(), calls=%async_computation.19 | async-start | bytes 2949120 | tf_op jit(solution)/shard_map/all_gather | solution.py:233
  883.1 263.2 %all-gather.29.cloned.1.call-start = ((), (), s32[]{:S(2)}) async-start(), calls=%async_computation.14 | async-start | bytes 4718592 | tf_op jit(solution)/shard_map/all_gather | solution.py:312
  883.8 347.8 %reduce-scatter.5.cloned.1.call-start = ((), (), s32[]{:S(2)}) async-start(), calls=%async_computation.13 | async-start | bytes 5898240 | tf_op jit(solution)/shard_map/reduce_scatter | solution.py:265
  1105.5 6.5 copy-start.22
  1105.5 7.4 slice-start.8
  1105.5 7.9 slice-start.9
  1113.9 12.2 copy-start.39
  1144.2 217.1 %all-gather.31.cloned.1.call-start = ((), (), s32[]{:S(2)}) async-start(), calls=%async_computation.15 | async-start | bytes 4718592 | tf_op jit(solution)/shard_map/all_gather | solution.py:313
  1146.2 87.7 %copy-start.35 = (bf16[1,128,2304]{2,1,0:T(8,128)(2,1)S(1)}, bf16[1,128,2304]{2,1,0:T(8,128)(2,1)}, u32[]{:S(2)}) copy-start(bf16[1,128,2304]{2,1,0:T(8,128)(2,1)} %param.17) | copy-start | bytes 1769476
  1151.9 82.1 %copy-start.7 = (f32[128,2304]{1,0:T(8,128)S(1)}, f32[128,2304]{1,0:T(8,128)}, u32[]{:S(2)}) copy-start(f32[128,2304]{1,0:T(8,128)} %copy-done.6) | copy-start | bytes 3538948
  1237.5 5.5 copy-start.19
  1237.8 5.2 copy-start.21
  1244.2 518.6 %reduce-scatter.7.cloned.1.call-start = ((), (), s32[]{:S(2)}) async-start(), calls=%async_computation.16 | async-start | bytes 67682304 | tf_op jit(solution)/shard_map/reduce_scatter | solution.py:364
  1259.0 15.4 copy-start.67
  1291.4 28.4 %copy-start.4 = (bf16[1,128,4,2,256]{4,1,3,2,0:T(8,128)(2,1)S(1)}, bf16[1,128,4,2,256]{4,1,3,2,0:T(8,128)(2,1)}, u32[]{:S(2)}) copy-start(bf16[1,128,4,2,256]{4,1,3,2,0:T(8,128)(2,1)} %copy-done.3) | copy-start | bytes 1572868
  1339.0 22.1 copy-start.44
  1339.0 22.1 copy-start.47
  1361.3 13.2 copy-start.41
  1369.6 4.9 copy-start.46
  1425.6 426.3 %reduce-scatter.11.cloned.1.call-start = ((), (), s32[]{:S(2)}) async-start(), calls=%async_computation.18 | async-start | bytes 1474560 | tf_op jit(solution)/shard_map/reduce_scatter | solution.py:387
  1765.2 88.7 %reduce-scatter.9.cloned.1.call-start = ((), (), s32[]{:S(2)}) async-start(), calls=%async_computation.17 | async-start | bytes 2949120 | tf_op jit(solution)/shard_map/reduce_scatter | solution.py:379
  1768.5 157.6 %all-reduce.22.cloned.1.call-start = ((), (), s32[]{:S(2)}) async-start(), calls=%async_computation.24 | async-start | bytes 5111808 | tf_op jit(solution)/shard_map/psum | solution.py:95
  1819.0 32.9 %copy-start.48 = (f32[288,2,256]{2,1,0:T(2,128)S(1)}, f32[288,2,256]{2,1,0:T(2,128)}, u32[]{:S(2)}) copy-start(f32[288,2,256]{2,1,0:T(2,128)} %param.23) | copy-start | bytes 1769476
  1853.9 92.2 %copy-start.18 = (f32[288,2,256]{2,0,1:T(8,128)}, f32[288,2,256]{2,0,1:T(8,128)S(1)}, u32[]{:S(2)}) copy-start(f32[288,2,256]{2,0,1:T(8,128)S(1)} %get-tuple-element.662) | copy-start | bytes 1769476
  1861.6 221.6 %all-reduce.20.cloned.1.call-start = ((), (), s32[]{:S(2)}) async-start(), calls=%async_computation.23 | async-start | bytes 5111808 | tf_op jit(solution)/shard_map/psum | solution.py:95
  1926.2 18.1 copy-start.28
  1944.2 5.5 copy-start.65
  1949.8 6.3 copy-start.11
  2019.2 190.4 %all-reduce.18.cloned.1.call-start = ((), (), s32[]{:S(2)}) async-start(), calls=%async_computation.22 | async-start | bytes 5111808 | tf_op jit(solution)/shard_map/psum | solution.py:95
  2090.6 5.0 copy-start.14
  2145.5 174.4 %all-reduce.16.cloned.1.call-start = ((), (), s32[]{:S(2)}) async-start(), calls=%async_computation.21 | async-start | bytes 5111808 | tf_op jit(solution)/shard_map/psum | solution.py:95
  2211.4 8.4 copy-start.15
  2211.4 9.0 slice-start
  2214.7 5.7 slice-start.1
  2255.4 188.8 %all-reduce.14.cloned.1.call-start = ((), (), s32[]{:S(2)}) async-start(), calls=%async_computation.20 | async-start | bytes 5111808 | tf_op jit(solution)/shard_map/psum | solution.py:95
  2321.8 3.8 copy-start.1
  2321.8 11.6 slice-start.2
  2325.6 5.4 copy-start.16
  2325.6 5.4 copy-start.12
  2325.6 7.8 slice-start.3
  2384.7 9.0 copy-start.38
  2384.7 10.3 copy-start.32
  2395.0 51.0 %copy-start.66 = (f32[6]{0:T(128)S(1)}, f32[6]{0:T(128)}, u32[]{:S(2)}) copy-start(f32[6]{0:T(128)} %copy-done.65) | copy-start | bytes 76
  2446.3 6.4 copy-start.31
  2446.3 6.8 copy-start.37
  2452.7 6.0 slice-start.4
  2453.1 3.2 copy-start.10
  2455.0 3.7 slice-start.5
  (38 other events, 54.9 us)
Sparse Core Ops, SparseCore 0:
  10.5 41.6 all-gather.12
  53.7 322.5 all-gather.14
  378.8 27.8 all-gather.20
  409.1 27.8 all-gather.16
  439.3 27.8 all-gather.18
  468.7 166.7 all-gather.22
  645.0 48.6 all-gather.24
  696.1 152.3 all-gather.26
  882.6 171.9 all-reduce.11
  1056.0 49.4 all-gather.32
  1108.0 35.5 all-gather.28
  1146.3 85.2 reduce-scatter.4
  1244.3 37.2 all-gather.30
  1425.7 337.0 reduce-scatter.6
  1765.6 29.1 reduce-scatter.10
  1797.7 46.7 reduce-scatter.8
  1861.7 64.3 all-reduce.21
  2019.3 63.9 all-reduce.19
  2145.6 63.8 all-reduce.17
  2255.5 64.4 all-reduce.15
  2380.2 63.8 all-reduce.13
where the time goes:
time: 2550 us; the launch traced here: 2540 us
  waiting for transfers between devices  1680 us (66%)
  matrix products  492 us (19%)
  local copies, waits for them, and re-layouts  178 us (7%)
  other arithmetic  116 us (5%)
  blocking collectives  48.7 us (2%)
    reduce_scatter x1, waiting for transfers between devices, local(): lax.psum_scatter(jnp.concatenate([grad_a.reshape(lax.axis_size('ctx') * l...  337 us
    all_gather x1, waiting for transfers between devices, local(): lax.all_gather(in_cut, 'fsdp', axis=1, tiled=True)  321 us
    psum x5, waiting for transfers between devices, gram_pair(): lax.psum(self_gram(head_part).astype(jnp.bfloat16), 'ctx')  247 us
    psum x1, waiting for transfers between devices, local(): ffn_branch = lax.psum(ffn_partial, 'fsdp')  170 us
    dot_general x10, matrix products, self_gram(): return jnp.einsum('jed,jfd->jef', matrices, matrices, precision=PRECISE)  166 us
    all_gather x1, waiting for transfers between devices, local(): lax.all_gather(out_cut, 'fsdp', axis=1, tiled=True)  159 us
    all_gather x1, waiting for transfers between devices, local(): lax.all_gather(ffn_weights.astype(jnp.bfloat16), 'ctx', axis=0, tiled=True)  155 us
    dot_general x10, matrix products, newton_step(): jnp.einsum('jef,jfd->jed', polynomial, matrices, precision=PRECISE)  123 us
  transfers between devices with their start and end apart: 21, of which 17 were waited for; matrix products, arithmetic and copies ran while one was open for 12% of the time, Pallas kernels for 0%

commit v1 on v0

v1 whole, which is shorter than its diff:
```python
import functools

import jax
import jax.numpy as jnp
from jax import lax
from jax.experimental import pallas as pl
from jax.experimental.pallas import tpu as pltpu
from jax.sharding import PartitionSpec as P

QUERY_HEADS = 8
KEY_VALUE_HEADS = 4
FBLK = 128
ITERS = 5
STEP = 10

SOFT_CAP = 50.0
EXP_SHIFT = 20.0
NORM_EPS = 1e-06
ROPE_THETA = 10000.0
MOMENTUM_DECAY = 0.95
LEARN_RATE = 0.3
WEIGHT_DECAY = 0.01
BETA_ONE = 0.9
BETA_TWO = 0.95
GAIN_RATE = 0.3
ADAM_EPS = 1e-08
NEWTON_A = 3.4445
NEWTON_B = -4.775
NEWTON_C = 2.0315
GELU_SCALE = 0.7978845608028654
GELU_CUBE = 0.044715
LOW = jnp.bfloat16
FULL = jnp.float32
SHRINK = 1.0 - LEARN_RATE * WEIGHT_DECAY
VMEM_LIMIT = 60 * 1024 * 1024


def rms_scale(values):
    return lax.rsqrt(jnp.mean(values * values, -1, keepdims=True) + NORM_EPS)


def positions_of(row_index, stretch_order, stretch_rows):
    stretch_slot = row_index // stretch_rows
    slot_table = jnp.arange(stretch_order.shape[0], dtype=jnp.int32)
    picked = jnp.sum(
        jnp.where(stretch_slot[:, None] == slot_table[None, :], stretch_order[None, :], 0), axis=1
    )
    return picked * stretch_rows + row_index % stretch_rows


def rope_tables(places, width):
    half_width = width // 2
    frequency = ROPE_THETA ** (-(2.0 * jnp.arange(half_width, dtype=jnp.float32)) / width)
    angles = places.astype(jnp.float32)[:, None] * frequency[None, :]
    return (jnp.cos(angles), jnp.sin(angles))


def rotate(values, cosine, sine):
    half = values.shape[-1] // 2
    first, second = values[..., :half], values[..., half:]
    return jnp.concatenate([first * cosine - second * sine, second * cosine + first * sine], -1)


def batched(left, right, left_dim, right_dim):
    return lax.dot_general(
        left, right, (((left_dim,), (right_dim,)), ((0,), (0,))), preferred_element_type=FULL
    )


def dot(left, right, left_dim, right_dim):
    return lax.dot_general(
        left, right, (((left_dim,), (right_dim,)), ((), ())), preferred_element_type=FULL
    )


def gram_kernel(blocks, grad_ref, old_ref, *refs):
    new_ref, update_ref, gram_ref = refs[-3:]
    grad = grad_ref[...].astype(FULL)
    new = MOMENTUM_DECAY * old_ref[0] + grad
    new_ref[0] = new
    update = (grad + MOMENTUM_DECAY * new).astype(LOW)
    update_ref[0] = update
    for block in range(blocks):
        piece = update[:, block * FBLK : (block + 1) * FBLK]
        gram_ref[block] = dot(piece, piece, 0, 0)


def ffn_gram(grads, momentum, first, blocks, earlier):
    _, rows, width = momentum.shape
    per_step = 6 if (width // FBLK) % 6 == 0 else 3
    span = per_step * FBLK
    steps = width // span
    spec = pl.BlockSpec((1, rows, span), lambda m, b: (m + first, 0, b))
    return pl.pallas_call(
        functools.partial(gram_kernel, per_step),
        grid=(grads.shape[1] // width, steps),
        in_specs=[pl.BlockSpec((rows, span), lambda m, b: (0, m * steps + b)), spec]
        + [ANY_SPEC] * len(earlier),
        out_specs=[
            spec,
            spec,
            pl.BlockSpec((per_step, FBLK, FBLK), lambda m, b: ((m + first) * steps + b, 0, 0)),
        ],
        out_shape=[
            jax.ShapeDtypeStruct(momentum.shape, FULL),
            jax.ShapeDtypeStruct(momentum.shape, LOW),
            jax.ShapeDtypeStruct((blocks, FBLK, FBLK), FULL),
        ],
        input_output_aliases={2 + index: index for index in range(len(earlier))},
        compiler_params=pltpu.CompilerParams(vmem_limit_bytes=VMEM_LIMIT),
        name="ffn_gram",
    )(grads, momentum, *earlier)


def split(values):
    high = values.astype(LOW)
    return high, (values - high.astype(FULL)).astype(LOW)


def fine_dot(left, right):
    (high, low), (right_high, right_low) = left, right
    return jnp.dot(
        jnp.concatenate([high, high, low], 1),
        jnp.concatenate([right_high, right_low, right_high], 0),
        preferred_element_type=FULL,
    )


def polys_of(grams):
    size = grams[0].shape[0]
    rows, columns = grid_of(size)
    eye = (rows == columns).astype(FULL)
    factors, totals = [], [None] * len(grams)
    for index, gram in enumerate(grams):
        trace = jnp.sum(jnp.sum(gram * eye, 0, keepdims=True), 1, keepdims=True)
        factors.append(1.0 / (jnp.sqrt(trace) + 1e-07))
        grams[index] = gram * (factors[index] * factors[index])
    for step in range(ITERS):
        parts = [split(gram) for gram in grams]
        squares = [fine_dot(part, part) for part in parts]
        quads = [
            NEWTON_A * eye + NEWTON_B * gram + NEWTON_C * square
            for gram, square in zip(grams, squares)
        ]
        quad_parts = [split(quad) for quad in quads]
        totals = [
            quad if total is None else fine_dot(split(total), part)
            for total, quad, part in zip(totals, quads, quad_parts)
        ]
        if step < ITERS - 1:
            halves = [fine_dot(quad, part) for quad, part in zip(quad_parts, parts)]
            grams = [fine_dot(split(half), quad) for half, quad in zip(halves, quad_parts)]
    return [total * factor for total, factor in zip(totals, factors)]


def moved(update, poly):
    high, low = split(poly)
    return jnp.dot(
        jnp.concatenate([update, update], 1),
        jnp.concatenate([high, low], 0),
        preferred_element_type=FULL,
    )


def tile_of(size):
    return 768 if size % 768 == 0 else 384


def remote(source, target, send, receive, axis, to):
    return pltpu.make_async_remote_copy(
        src_ref=source,
        dst_ref=target,
        send_sem=send,
        recv_sem=receive,
        device_id={axis: to},
        device_id_type=pl.DeviceIdType.MESH,
    )


def greet(peers):
    barrier = pltpu.get_barrier_semaphore()
    for axis, to in peers:
        pl.semaphore_signal(
            barrier, inc=1, device_id={axis: to}, device_id_type=pl.DeviceIdType.MESH
        )
    pl.semaphore_wait(barrier, len(peers))


def line_greet(at, size):
    barrier = pltpu.get_barrier_semaphore()
    for ok, to in ((at > 0, at - 1), (at < size - 1, at + 1)):

        @pl.when(ok)
        def _(to=to):
            pl.semaphore_signal(
                barrier, inc=1, device_id={"fsdp": to}, device_id_type=pl.DeviceIdType.MESH
            )

    inside = (at > 0) & (at < size - 1)
    for ok, peers in ((inside, 2), (jnp.logical_not(inside), 1)):

        @pl.when(ok)
        def _(peers=peers):
            pl.semaphore_wait(barrier, peers)


class LineGather:
    def __init__(self, at, size, span, out, send, receive):
        self.at, self.size, self.span = at, size, span
        self.out, self.send_sem, self.receive_sem = out, send, receive

    def piece(self, owner, chunk):
        return self.out.at[owner, pl.ds(pl.multiple_of(chunk * self.span, self.span), self.span)]

    def copy(self, owner, chunk, side):
        piece = self.piece(owner, chunk)
        to = (self.at + (1 if side == 0 else self.size - 1)) % self.size
        return remote(
            piece,
            piece,
            self.send_sem.at[side, owner, chunk],
            self.receive_sem.at[owner, chunk],
            "fsdp",
            to,
        )

    def start(self, chunk):
        @pl.when(self.at < self.size - 1)
        def _():
            self.copy(self.at, chunk, 0).start()

        @pl.when(self.at > 0)
        def _():
            self.copy(self.at, chunk, 1).start()

    def forward(self, chunk, gap):
        at, size = self.at, self.size

        @pl.when(at >= gap)
        def _(owner=at - gap):
            copy = self.copy(owner, chunk, 0)
            copy.wait_recv()

            @pl.when(at < size - 1)
            def _():
                copy.start()

        @pl.when(at + gap < size)
        def _(owner=at + gap):
            copy = self.copy(owner, chunk, 1)
            copy.wait_recv()

            @pl.when(at > 0)
            def _():
                copy.start()

    def drain(self, chunk):
        at, size = self.at, self.size
        for gap in range(size):

            @pl.when((at >= gap) & (at < size - 1))
            def _(owner=at - gap):
                self.copy(owner, chunk, 0).wait_send()

            @pl.when((at + gap < size) & (at > 0))
            def _(owner=at + gap):
                self.copy(owner, chunk, 1).wait_send()


def cut_of(rows):
    return 16 * (-(-rows // 32)) if rows >= 32 else rows


class Square:
    def __init__(self, at, size):
        self.at, self.column = at, size // 4
        self.core, self.x, self.y = at % 2, (at // 2) % 2, at // 4
        self.sibling = at + 1 - 2 * self.core

    def device(self, j, turn, core=None):
        x = 1 - self.x if turn else self.x
        core = self.core if core is None else core
        return (((self.y + j) % self.column) * 2 + x) * 2 + core

    def others(self):
        return range(1, self.column)

    def back(self, j):
        return (self.column - j) % self.column


def ctx_peers(at, size):
    square = Square(at, size)
    peers = [square.sibling, square.device(0, True)]
    return [("ctx", to) for to in peers + [square.device(j, False) for j in square.others()]]


class CtxGather:
    def __init__(self, at, size, source, slot, axis, sems):
        self.square = Square(at, size)
        self.source, self.slot, self.axis = source, slot, axis
        self.send, self.receive, self.pass_send, self.pass_receive, self.own = sems
        rows = source.shape[axis]
        cut = cut_of(rows)
        self.halves = (0, 1) if cut < rows else (0,)
        self.bounds = ((0, cut), (cut, rows - cut))

    def half(self, view, h):
        first, count = self.bounds[h]
        return view.at[(slice(None),) * self.axis + (pl.ds(first, count),)]

    def block(self, j, turn, h, core=None):
        return self.half(self.slot(self.square.device(j, turn, core)), h)

    def copy(self, source, target, h, send, j, turn, to):
        return remote(
            source,
            target,
            self.send.at[h, send],
            self.receive.at[h, j, int(turn)],
            "ctx",
            to,
        )

    def direct(self, h, j):
        square = self.square
        return self.copy(
            self.half(self.source, h),
            self.half(self.slot(square.at), h),
            h,
            j,
            square.back(j),
            j == 0,
            square.device(j, j == 0),
        )

    def onward(self, h, j):
        square = self.square
        block = self.block(0, True, 0) if h == 0 else self.block(j, False, 1)
        to = square.device(j, False) if h == 0 else square.device(0, True)
        origin = square.back(j) if h == 0 else j
        return self.copy(block, block, h, square.column + j, origin, True, to)

    def arrival(self, h, j, turn):
        block = self.block(j, turn, h)
        return remote(
            block, block, self.send.at[h, 0], self.receive.at[h, j, int(turn)], "ctx", self.square.sibling
        )

    def across(self, h, j, turn):
        block = self.block(j, turn, h)
        sems = (self.pass_send.at[h, j, int(turn)], self.pass_receive.at[h, j, int(turn)])
        return remote(block, block, *sems, "ctx", self.square.sibling)

    def crossed(self, h, j, turn):
        block = self.block(j, turn, h, 1 - self.square.core)
        sems = (self.pass_send.at[h, j, int(turn)], self.pass_receive.at[h, j, int(turn)])
        return remote(block, block, *sems, "ctx", self.square.sibling)

    def mine(self, h):
        sems = (self.pass_send.at[h, 0, 0], self.pass_receive.at[h, 0, 0])
        target = self.half(self.slot(self.square.at), h)
        return remote(self.half(self.source, h), target, *sems, "ctx", self.square.sibling)

    def keep(self):
        return pltpu.make_async_copy(self.source, self.slot(self.square.at), self.own)

    def start(self):
        others, halves = self.square.others(), self.halves
        self.direct(0, 0).start()
        for j in others:
            self.direct(halves[-1], j).start()
        if len(halves) > 1:
            self.direct(1, 0).start()
            for j in others:
                self.direct(0, j).start()
        for h in halves:
            self.mine(h).start()
        self.keep().start()

    def land(self, h, j, turn):
        self.arrival(h, j, turn).wait_recv()
        self.across(h, j, turn).start()

    def forward(self):
        others, halves = self.square.others(), self.halves
        self.land(0, 0, True)
        for j in others:
            self.onward(0, j).start()
        if len(halves) > 1:
            for j in others:
                self.land(1, j, False)
                self.onward(1, j).start()

    def rest(self):
        others, halves = self.square.others(), self.halves
        if len(halves) > 1:
            self.land(1, 0, True)
        for j in others:
            self.land(0, j, False)
        for j in others:
            for h in halves:
                self.land(h, j, True)

    def finish(self):
        square, halves = self.square, self.halves
        for h in halves:
            for j in range(square.column):
                self.direct(h, j).wait_send()
                if j > 0:
                    self.onward(h, j).wait_send()
                for turn in (False, True):
                    self.crossed(h, j, turn).wait_recv()
                    if j > 0 or turn:
                        self.across(h, j, turn).wait_send()
            self.mine(h).wait_send()
        self.keep().wait()


def ctx_gather_sems(size):
    column = size // 4
    dma = pltpu.SemaphoreType.DMA
    return [dma((2, 2 * column)), dma((2, column, 2)), dma((2, column, 2)), dma((2, column, 2)), dma]


class CtxScatter:
    def __init__(self, at, size, part, first, hold, along_x, along_y, landed, sems):
        self.square = Square(at, size)
        self.part, self.first, self.hold = part, first, hold
        self.along_x, self.along_y, self.landed = along_x, along_y, landed
        self.near_send, self.near_receive, self.send, self.receive = sems
        self.step = 16 if first.dtype == LOW else 8
        rows = hold.shape[2]
        cut = cut_of(rows)
        self.bounds = ((0, cut), (cut, rows - cut))

    def index(self, j, turn):
        return j * 2 + int(turn)

    def near(self, j, turn):
        index = self.index(j, turn)
        return remote(
            self.part(self.square.device(j, turn, 1 - self.square.core)),
            self.first.at[index],
            self.near_send.at[index],
            self.near_receive.at[index],
            "ctx",
            self.square.sibling,
        )

    def half(self, view, h):
        return view.at[:, pl.ds(*self.bounds[h])]

    def far(self, kind, j):
        square, h = self.square, kind % 2
        if kind < 2:
            source = self.half(self.hold.at[self.index(j, True)], h)
            target = self.along_x.at[j - 1] if kind == 0 else self.along_y.at[square.back(j) - 1]
        elif kind < 4:
            source = self.half(self.hold.at[self.index(0, True)], h)
            target = self.half(self.landed.at[0], h)
        else:
            source = self.half(self.hold.at[self.index(j, False)], h)
            target = self.half(self.landed.at[square.back(j)], h)
        along_x = kind in (0, 2, 3)
        to = square.device(0, True) if along_x else square.device(j, False)
        return remote(
            source,
            target,
            self.send.at[kind, j],
            self.receive.at[kind, j if along_x else square.back(j)],
            "ctx",
            to,
        )

    def arrival(self, kind, j):
        h = kind % 2
        if kind < 2:
            block = (self.along_x if kind == 0 else self.along_y).at[j - 1]
        else:
            block = self.half(self.landed.at[0 if kind < 4 else j], h)
        return remote(
            block, block, self.send.at[kind, j], self.receive.at[kind, j], "ctx", self.square.sibling
        )

    def rows(self, first, count, body):
        def one(index, carried):
            offset = pl.multiple_of(index * self.step, self.step)
            for block in range(self.hold.shape[1]):
                body(block, offset)
            return carried

        lax.fori_loop(first // self.step, (first + count) // self.step, one, 0)

    def pair(self, j, turn):
        self.near(j, turn).wait_recv()
        index = self.index(j, turn)
        part = self.part(self.square.device(j, turn))

        def add(block, offset):
            rows = pl.ds(offset, self.step)
            total = part[block, rows, :].astype(FULL)
            total = total + self.first[index, block, rows, :].astype(FULL)
            self.hold[index, block, rows, :] = total.astype(self.hold.dtype)

        self.rows(0, self.hold.shape[2], add)

    def start(self):
        others = self.square.others()
        for j in others:
            self.near(j, True).start()
        self.near(0, True).start()
        for j in others:
            self.near(j, False).start()
        self.near(0, False).start()

    def diagonal(self):
        for j in self.square.others():
            self.pair(j, True)
            self.far(0, j).start()
            self.far(1, j).start()

    def neighbours(self):
        self.pair(0, True)
        self.far(2, 0).start()
        for j in self.square.others():
            self.pair(j, False)
            self.far(5, j).start()

    def add_passing(self, index, h, block_of):
        first, count = self.bounds[h]

        def add(block, offset):
            rows = pl.ds(offset, self.step)
            local = pl.ds(pl.multiple_of(offset - first, self.step), self.step)
            total = self.hold[index, block, rows, :].astype(FULL)
            for passing in block_of:
                total = total + passing[block, local, :].astype(FULL)
            self.hold[index, block, rows, :] = total.astype(self.hold.dtype)

        self.rows(first, count, add)

    def passing(self):
        others = self.square.others()
        for j in others:
            self.arrival(0, j).wait_recv()
            self.add_passing(self.index(j, False), 0, [self.along_x.at[j - 1]])
            self.far(4, j).start()
        for j in others:
            self.arrival(1, j).wait_recv()
        self.add_passing(self.index(0, True), 1, [self.along_y.at[j - 1] for j in others])
        self.far(3, 0).start()

    def finish(self, store):
        others = self.square.others()
        self.near(0, False).wait_recv()
        for kind in (2, 3):
            self.arrival(kind, 0).wait_recv()
        for j in others:
            for kind in (5, 4):
                self.arrival(kind, j).wait_recv()
        part = self.part(self.square.at)

        def add(block, offset):
            rows = pl.ds(offset, self.step)
            total = part[block, rows, :].astype(FULL) + self.first[0, block, rows, :].astype(FULL)
            for index in range(self.landed.shape[0]):
                total = total + self.landed[index, block, rows, :].astype(FULL)
            store(block, rows, total)

        self.rows(0, self.hold.shape[2], add)

    def drain(self):
        for j in range(self.square.column):
            for turn in (False, True):
                self.near(j, turn).wait_send()
        for kind in (2, 3):
            self.far(kind, 0).wait_send()
        for j in self.square.others():
            for kind in (0, 1, 4, 5):
                self.far(kind, j).wait_send()


SCATTER = 9


def ctx_scatter_scratch(size, blocks, rows, width, kind):
    chips, column = size // 2, size // 4
    cut = cut_of(rows)
    dma = pltpu.SemaphoreType.DMA
    return [
        pltpu.VMEM((chips, blocks, rows, width), kind),
        pltpu.VMEM((chips, blocks, rows, width), kind),
        pltpu.VMEM((column - 1, blocks, cut, width), kind),
        pltpu.VMEM((column - 1, blocks, rows - cut, width), kind),
        pltpu.VMEM((column, blocks, rows, width), kind),
        dma((chips,)),
        dma((chips,)),
        dma((6, column)),
        dma((6, column)),
    ]


def ctx_scatter(at, size, part, scratch):
    return CtxScatter(at, size, part, *scratch[:5], scratch[5:9])


def rows_of_ctx(ref):
    return lambda c: ref.at[pl.ds(c, 1)]


VMEM_SPEC = pl.BlockSpec(memory_space=pltpu.VMEM)
ANY_SPEC = pl.BlockSpec(memory_space=pl.ANY)


def head_places(fsdp):
    heads = QUERY_HEADS // fsdp
    pairs = max(1, KEY_VALUE_HEADS // fsdp)
    stored = (QUERY_HEADS + 2 * KEY_VALUE_HEADS) // fsdp
    places = []
    for user in range(fsdp):
        first = (user * heads) // (QUERY_HEADS // KEY_VALUE_HEADS)
        used = [user * heads + h for h in range(heads)]
        used += [QUERY_HEADS + first + p for p in range(pairs)]
        used += [QUERY_HEADS + KEY_VALUE_HEADS + first + p for p in range(pairs)]
        places.append([(matrix // stored, matrix % stored) for matrix in used])
    return places


def prepare_kernel(
    ctx, fsdp, in_ref, out_ref, ffn_ref, x_ref, gains, mine, out_all, ffn_low, normed, *scratch
):
    at, line_at = lax.axis_index("ctx"), lax.axis_index("fsdp")
    in_low, out_low, wide, wide_sem, move_send, move_receive = scratch[:6]
    places = head_places(fsdp)
    head = in_ref.shape[2]
    greet(ctx_peers(at, ctx) + [("fsdp", (line_at + k) % fsdp) for k in range(1, fsdp)])

    def move(user, slot):
        owner, index = places[user][slot]
        return remote(
            in_low.at[index],
            mine.at[:, pl.ds(slot * head, head)],
            move_send.at[user, slot],
            move_receive.at[slot],
            "fsdp",
            user,
        )

    def load(matrix):
        return pltpu.make_async_copy(
            ffn_ref.at[matrix], wide.at[matrix % 2], wide_sem.at[matrix % 2]
        )

    load(0).start()
    for index in range(in_ref.shape[1]):
        in_low[index] = in_ref[:, index, :].astype(LOW)
    for user in range(fsdp):
        for slot in range(len(places[0])):
            owner, index = places[user][slot]

            @pl.when(line_at == owner)
            def _(user=user, slot=slot, owner=owner, index=index):
                if user == owner:
                    mine[:, slot * head : (slot + 1) * head] = in_low[index]
                else:
                    move(user, slot).start()

    for index in range(out_ref.shape[1]):
        out_low[:, index * head : (index + 1) * head] = out_ref[:, index, :].astype(LOW)
    gather = CtxGather(at, ctx, out_low, lambda c: out_all.at[c], 0, scratch[6:11])
    gather.start()
    x = x_ref[...].astype(FULL)
    normed[...] = (x * rms_scale(x) * (1.0 + gains[0:1, :])).astype(LOW)
    for matrix in range(3):
        load(matrix).wait()
        if matrix < 2:
            load(matrix + 1).start()
        ffn_low[matrix] = wide[matrix % 2].astype(LOW)
    gather.forward()
    gather.rest()
    for user in range(fsdp):

        @pl.when(line_at == user)
        def _(user=user):
            for slot in range(len(places[0])):
                if places[user][slot][0] != user:
                    move(user, slot).wait_recv()

        for slot in range(len(places[0])):
            owner, index = places[user][slot]
            if user != owner:

                @pl.when(line_at == owner)
                def _(user=user, slot=slot):
                    move(user, slot).wait_send()

    gather.finish()


def prepare(weights_in, weights_out, ffn, x, gains, ctx, fsdp):
    local_rows, in_local, head = weights_in.shape
    out_local = weights_out.shape[1]
    mine = len(head_places(fsdp)[0])
    dma = pltpu.SemaphoreType.DMA
    return pl.pallas_call(
        functools.partial(prepare_kernel, ctx, fsdp),
        in_specs=[VMEM_SPEC] * 2 + [ANY_SPEC] + [VMEM_SPEC] * 2,
        out_specs=[VMEM_SPEC, ANY_SPEC, VMEM_SPEC, VMEM_SPEC],
        out_shape=[
            jax.ShapeDtypeStruct((local_rows, mine * head), LOW),
            jax.ShapeDtypeStruct((ctx, local_rows, out_local * head), LOW),
            jax.ShapeDtypeStruct(ffn.shape, LOW),
            jax.ShapeDtypeStruct(x.shape, LOW),
        ],
        scratch_shapes=[
            pltpu.VMEM((in_local, local_rows, head), LOW),
            pltpu.VMEM((local_rows, out_local * head), LOW),
            pltpu.VMEM((2,) + ffn.shape[1:], FULL),
            dma((2,)),
            dma((fsdp, mine)),
            dma((mine,)),
        ]
        + ctx_gather_sems(ctx),
        compiler_params=pltpu.CompilerParams(vmem_limit_bytes=VMEM_LIMIT, collective_id=0),
        name="prepare",
    )(weights_in, weights_out, ffn, x, gains)


def project_kernel(
    ctx, fsdp, span, heads, own, mine, cosine, sine, normed, in_all, query, key_all, value_all, *scratch
):
    at, line_at = lax.axis_index("ctx"), lax.axis_index("fsdp")
    key, value, low_send, low_receive = scratch[:4]
    tokens = own.shape[0]
    rows = key.shape[1]
    local_rows = mine.shape[0]
    head = 2 * cosine.shape[1]
    pairs = key.shape[2] // head
    chunks = tokens // span
    greet(ctx_peers(at, ctx) + [("fsdp", (line_at + k) % fsdp) for k in range(1, fsdp)])
    line = LineGather(line_at, fsdp, span, normed, low_send, low_receive)
    normed[line_at] = own[...]
    for chunk in range(chunks):
        line.start(chunk)
    step = 16

    def slot(c):
        return in_all.at[pl.ds(pl.multiple_of(c * local_rows, step), local_rows)]

    gather_in = CtxGather(at, ctx, mine, slot, 0, scratch[4:9])
    gather_in.start()
    for chunk in range(chunks):
        line.forward(chunk, 1)
    gather_in.forward()
    for gap in range(2, fsdp):
        for chunk in range(chunks):
            line.forward(chunk, gap)
    gather_in.rest()
    gather_in.finish()

    def projected(index, write, turn, scale):
        weights = in_all[:, index * head : (index + 1) * head]
        for sequence in range(fsdp):
            result = dot(normed[sequence], weights, 1, 0)
            if turn:
                first, second = result[:, : head // 2], result[:, head // 2 :]
                result = jnp.concatenate(
                    [
                        first * cosine[...] - second * sine[...],
                        second * cosine[...] + first * sine[...],
                    ],
                    1,
                )
            write(sequence, (result * scale).astype(LOW))

    per_device = tokens // rows
    for pair in range(pairs):
        columns = slice(pair * head, (pair + 1) * head)
        for matrix, target, turn in (
            (heads + pair, key, True),
            (heads + pairs + pair, value, False),
        ):

            def write(sequence, result, target=target, columns=columns):
                for inner in range(per_device):
                    target[sequence * per_device + inner, :, columns] = result[
                        inner * rows : (inner + 1) * rows
                    ]

            projected(matrix, write, turn, 1.0)

    keys = CtxGather(at, ctx, key, lambda c: key_all.at[:, c], 1, scratch[9:14])
    values = CtxGather(at, ctx, value, lambda c: value_all.at[:, c], 1, scratch[14:19])
    keys.start()
    values.start()
    for index in range(heads):

        def write(sequence, result, index=index):
            query[sequence * tokens : (sequence + 1) * tokens, index * head : (index + 1) * head] = result

        projected(index, write, True, head ** (-0.5))
    keys.forward()
    values.forward()
    keys.rest()
    values.rest()
    for chunk in range(chunks):
        line.drain(chunk)
    keys.finish()
    values.finish()


def project(own, mine, cosine, sine, sequences, heads, pairs, ctx, fsdp):
    tokens, width = own.shape
    local_rows = mine.shape[0]
    head = 2 * cosine.shape[1]
    rows = tokens // sequences
    chunks = 4
    dma = pltpu.SemaphoreType.DMA
    block = (fsdp * sequences, rows, pairs * head)
    spread = (fsdp * sequences, ctx, rows, pairs * head)
    return pl.pallas_call(
        functools.partial(project_kernel, ctx, fsdp, tokens // chunks, heads),
        in_specs=[VMEM_SPEC] * 4,
        out_specs=[VMEM_SPEC] * 3 + [ANY_SPEC] * 2,
        out_shape=[
            jax.ShapeDtypeStruct((fsdp, tokens, width), LOW),
            jax.ShapeDtypeStruct((ctx * local_rows, mine.shape[1]), LOW),
            jax.ShapeDtypeStruct((fsdp * tokens, heads * head), LOW),
            jax.ShapeDtypeStruct(spread, LOW),
            jax.ShapeDtypeStruct(spread, LOW),
        ],
        scratch_shapes=[
            pltpu.VMEM(block, LOW),
            pltpu.VMEM(block, LOW),
            dma((2, fsdp, chunks)),
            dma((fsdp, chunks)),
        ]
        + ctx_gather_sems(ctx) * 3,
        compiler_params=pltpu.CompilerParams(vmem_limit_bytes=VMEM_LIMIT, collective_id=1),
        name="project",
    )(own, mine, cosine, sine)


class LineExchange:
    def __init__(self, at, size, span, part, low_all, mid, scratch):
        self.at, self.size, self.span, self.part, self.mid = at, size, span, part, mid
        self.hold, self.landed, self.total, self.send, self.receive = scratch[:5]
        self.chunks = part.shape[1] // span
        self.low_all = low_all
        if low_all is not None:
            self.line = LineGather(at, size, span, low_all, *scratch[5:7])
        self.steps = self.chunks + (size - 1) * (1 if low_all is None else 2)

    def hop(self, source, target, chunk, side):
        to = (self.at + (1 if side == 0 else self.size - 1)) % self.size
        rows = pl.ds(pl.multiple_of(chunk * self.span, self.span), self.span)
        return remote(
            source.at[target, rows],
            self.landed.at[side, target, rows],
            self.send.at[target, chunk],
            self.receive.at[side, target, chunk],
            "fsdp",
            to,
        )

    def pass_on(self, target, chunk, side):
        rows = pl.ds(pl.multiple_of(chunk * self.span, self.span), self.span)
        origin = self.at == 0 if side == 0 else self.at == self.size - 1

        @pl.when(origin)
        def _():
            self.hop(self.part, target, chunk, side).start()

        @pl.when(jnp.logical_not(origin))
        def _():
            self.hop(self.part, target, chunk, side).wait_recv()
            added = self.part[target, rows, :].astype(FULL)
            added = added + self.landed[side, target, rows, :].astype(FULL)
            self.hold[target, rows, :] = added.astype(LOW)
            self.hop(self.hold, target, chunk, side).start()

    def step(self, index):
        at, size, chunks = self.at, self.size, self.chunks
        for gap in range(size - 1, 0, -1):
            chunk = index - at

            @pl.when((at + gap < size) & (chunk >= 0) & (chunk < chunks))
            def _(target=at + gap, chunk=chunk):
                self.pass_on(target, chunk, 0)

            chunk = index - (size - 1 - at)

            @pl.when((at >= gap) & (chunk >= 0) & (chunk < chunks))
            def _(target=at - gap, chunk=chunk):
                self.pass_on(target, chunk, 1)

        chunk = index - (size - 1)

        @pl.when((chunk >= 0) & (chunk < chunks))
        def _():
            rows = pl.ds(pl.multiple_of(chunk * self.span, self.span), self.span)
            self.total[...] = self.part[at, rows, :].astype(FULL)
            for side, ok in ((0, at > 0), (1, at < size - 1)):

                @pl.when(ok)
                def _(side=side):
                    self.hop(self.part, at, chunk, side).wait_recv()
                    self.total[...] += self.landed[side, at, rows, :].astype(FULL)

            low = self.mid(chunk, rows, self.total[...])
            if self.low_all is not None:
                self.low_all[at, rows, :] = low
                self.line.start(chunk)

        if self.low_all is not None:
            for gap in range(1, size):
                chunk = index - (size - 1) - gap

                @pl.when((chunk >= 0) & (chunk < chunks))
                def _(gap=gap, chunk=chunk):
                    self.line.forward(chunk, gap)

    def run(self, first, last):
        def one(index, carried):
            self.step(index)
            return carried

        lax.fori_loop(first, last, one, 0)

    def drain(self):
        at, size = self.at, self.size

        def one(chunk, carried):
            for gap in range(1, size):

                @pl.when(at + gap < size)
                def _(target=at + gap):
                    self.hop(self.part, target, chunk, 0).wait_send()

                @pl.when(at >= gap)
                def _(target=at - gap):
                    self.hop(self.part, target, chunk, 1).wait_send()

            if self.low_all is not None:
                self.line.drain(chunk)
            return carried

        lax.fori_loop(0, self.chunks, one, 0)


def line_span(tokens):
    return 16


def line_scratch(fsdp, tokens, width, gather):
    span = line_span(tokens)
    chunks = tokens // span
    dma = pltpu.SemaphoreType.DMA
    return [
        pltpu.VMEM((fsdp, tokens, width), LOW),
        pltpu.VMEM((2, fsdp, tokens, width), LOW),
        pltpu.VMEM((span, width), FULL),
        dma((fsdp, chunks)),
        dma((2, fsdp, chunks)),
    ] + ([dma((2, fsdp, chunks)), dma((fsdp, chunks))] if gather else [])


def exchange_kernel(mid, size, inputs, part, *refs):
    at = lax.axis_index("fsdp")
    ins, gains, low_all, refs = refs[:inputs], refs[inputs], refs[inputs + 1], refs[inputs + 2 :]
    outs, scratch = refs[:-7], refs[-7:]
    line_greet(at, size)
    line = LineExchange(
        at,
        size,
        line_span(part.shape[1]),
        part,
        low_all,
        lambda chunk, rows, total: mid(chunk, rows, total, ins, gains, outs),
        scratch,
    )
    line.run(0, line.steps)
    line.drain()


def exchange(part, ins, gains, mid, out_shape, fsdp, collective_id, name):
    _, tokens, width = part.shape
    return pl.pallas_call(
        functools.partial(exchange_kernel, mid, fsdp, len(ins)),
        in_specs=[VMEM_SPEC] * (len(ins) + 2),
        out_specs=[VMEM_SPEC] * (len(out_shape) + 1),
        out_shape=[jax.ShapeDtypeStruct(part.shape, LOW)] + out_shape,
        scratch_shapes=line_scratch(fsdp, tokens, width, True),
        compiler_params=pltpu.CompilerParams(
            vmem_limit_bytes=VMEM_LIMIT, collective_id=collective_id
        ),
        name=name,
    )(part, *ins, gains)


class Forward:
    def __init__(self, mid, weights, hidden, gate_factor, up_factor, part, scratch):
        self.weights, self.part = weights, part
        self.outs = (hidden, gate_factor, up_factor)
        self.mid, self.hidden, self.pair, self.down, self.pair_sem, self.down_sem = scratch
        self.sequences, self.tokens, _ = mid.shape
        self.half = self.tokens // 2
        self.span, self.reach = self.pair.shape[3], self.down.shape[1]
        self.tiles = weights.shape[2] // self.span
        self.ends = weights.shape[1] // self.reach
        self.count = self.tiles + self.ends
        for half in range(2):
            for sequence in range(self.sequences):
                rows = slice(sequence * self.half, (sequence + 1) * self.half)
                self.mid[half, rows, :] = mid[sequence, half * self.half : (half + 1) * self.half, :]

    def fetch_pair(self, half, tile):
        slot = (half * self.tiles + tile) % 2
        columns = pl.ds(pl.multiple_of(tile * self.span, self.span), self.span)
        return pltpu.make_async_copy(
            self.weights.at[pl.ds(0, 2), :, columns], self.pair.at[slot], self.pair_sem.at[slot]
        )

    def fetch_down(self, half, tile):
        slot = (half * self.ends + tile) % 2
        rows = pl.ds(pl.multiple_of(tile * self.reach, self.reach), self.reach)
        return pltpu.make_async_copy(
            self.weights.at[2, rows], self.down.at[slot], self.down_sem.at[slot]
        )

    def fetch(self, index):
        half, tile = index // self.count, index % self.count

        @pl.when(tile < self.tiles)
        def _():
            self.fetch_pair(half, tile).start()

        @pl.when(tile >= self.tiles)
        def _():
            self.fetch_down(half, tile - self.tiles).start()

    def rows(self, half):
        return pl.ds(pl.multiple_of(half * self.half, 16), self.half)

    def run(self, index):
        half, tile = index // self.count, index % self.count

        @pl.when(index + 1 < 2 * self.count)
        def _():
            self.fetch(index + 1)

        @pl.when(tile < self.tiles)
        def _():
            self.fetch_pair(half, tile).wait()
            slot = (half * self.tiles + tile) % 2
            mid = self.mid[half]
            gate = dot(mid, self.pair[slot, 0], 1, 0)
            up = dot(mid, self.pair[slot, 1], 1, 0)
            columns = pl.ds(pl.multiple_of(tile * self.span, self.span), self.span)
            results = [value.astype(LOW) for value in activate(gate, up)]
            self.hidden[half, :, columns] = results[0]
            for out, value in zip(self.outs, results):
                for sequence in range(self.sequences):
                    out[sequence, self.rows(half), columns] = value[
                        sequence * self.half : (sequence + 1) * self.half
                    ]

        @pl.when(tile >= self.tiles)
        def _():
            end = tile - self.tiles
            self.fetch_down(half, end).wait()
            slot = (half * self.ends + end) % 2
            value = dot(self.hidden[half], self.down[slot], 1, 1).astype(LOW)
            columns = pl.ds(pl.multiple_of(end * self.reach, self.reach), self.reach)
            for sequence in range(self.sequences):
                self.part[sequence, self.rows(half), columns] = value[
                    sequence * self.half : (sequence + 1) * self.half
                ]


def activate(gate, up):
    square = gate * gate
    squashed = jnp.tanh(GELU_SCALE * gate * (1.0 + GELU_CUBE * square))
    half = 0.5 + 0.5 * squashed
    act = gate * half
    slope = half + act * (1.0 - squashed) * (GELU_SCALE + 3.0 * GELU_SCALE * GELU_CUBE * square)
    return act * up, up * slope, act


def late_kernel(
    size, mid, mixed, cotangent, gains, weights, late, out, gain, hidden, gate_factor, up_factor, *scratch
):
    at = lax.axis_index("fsdp")
    line_greet(at, size)
    part = scratch[0]
    line = LineExchange(
        at,
        size,
        line_span(part.shape[1]),
        part,
        late,
        lambda chunk, rows, total: late_mid(
            chunk, rows, total, (mixed, cotangent), gains, (out, gain)
        ),
        scratch[1:8],
    )
    forward = Forward(mid, weights, hidden, gate_factor, up_factor, part, scratch[8:])
    forward.fetch(0)

    def one(index, carried):
        forward.run(index)
        return carried

    lax.fori_loop(0, forward.count, one, 0)
    ahead = line.chunks // 2 - 1
    share = -(-forward.count // ahead)

    def both(index, carried):
        line.step(index)

        def more(inner, carried):
            tile = forward.count + index * share + inner

            @pl.when(tile < 2 * forward.count)
            def _():
                forward.run(tile)

            return carried

        lax.fori_loop(0, share, more, 0)
        return carried

    lax.fori_loop(0, ahead, both, 0)
    line.run(ahead, line.steps)
    line.drain()


def late_exchange(mid, weights, mixed, cotangent, gains, collective_id):
    fsdp, tokens, width = mid.shape
    units = weights.shape[2]
    span, reach = tile_of(units), tile_of(width)
    rows = fsdp * tokens // 2
    dma = pltpu.SemaphoreType.DMA
    low = jax.ShapeDtypeStruct((fsdp, tokens, units), LOW)
    return pl.pallas_call(
        functools.partial(late_kernel, fsdp),
        in_specs=[VMEM_SPEC] * 4 + [ANY_SPEC],
        out_specs=[VMEM_SPEC] * 6,
        out_shape=[
            jax.ShapeDtypeStruct(mid.shape, LOW),
            jax.ShapeDtypeStruct((tokens, width), LOW),
            jax.ShapeDtypeStruct((1, width), FULL),
            low,
            low,
            low,
        ],
        scratch_shapes=[pltpu.VMEM(mid.shape, LOW)]
        + line_scratch(fsdp, tokens, width, True)
        + [
            pltpu.VMEM((2, rows, width), LOW),
            pltpu.VMEM((2, rows, units), LOW),
            pltpu.VMEM((2, 2, width, span), LOW),
            pltpu.VMEM((2, reach, units), LOW),
            dma((2,)),
            dma((2,)),
        ],
        compiler_params=pltpu.CompilerParams(
            vmem_limit_bytes=VMEM_LIMIT, collective_id=collective_id
        ),
        name="late_exchange",
    )(mid, mixed, cotangent, gains, weights)


class Backward:
    def __init__(self, late, mid, weights, gate_factor, up_factor, part, grads, scratch):
        self.weights, self.part, self.grads, self.mid = weights, part, grads, mid
        self.factors = (gate_factor, up_factor)
        self.late, self.turned, self.pairs, self.wide, self.tall, self.stage = scratch[:6]
        self.wide_sem, self.tall_sem, self.stage_sem, self.mid_sem = scratch[6:]
        self.sequences, self.tokens, self.width = late.shape
        self.half = self.tokens // 2
        self.span, self.reach = self.wide.shape[2], self.tall.shape[2]
        self.units = weights.shape[2]
        self.tiles = self.units // self.span
        self.ends = self.width // self.reach
        self.count = self.tiles + self.ends
        self.sums = 2 * self.units // self.stage.shape[2]
        for half in range(2):
            for sequence in range(self.sequences):
                rows = slice(sequence * self.half, (sequence + 1) * self.half)
                self.late[half, rows, :] = late[sequence, half * self.half : (half + 1) * self.half, :]

    def fetch_mid(self):
        return [
            pltpu.make_async_copy(
                self.mid.at[s, pl.ds(half * self.half, self.half)],
                self.late.at[half, pl.ds(s * self.half, self.half)],
                self.mid_sem.at[half * self.sequences + s],
            )
            for half in range(2)
            for s in range(self.sequences)
        ]

    def turn(self):
        rows = self.sequences * self.half
        for copy in self.fetch_mid():
            copy.wait()
        for half in range(2):
            for first in range(0, self.width, self.reach):
                block = self.late[half, :, first : first + self.reach]
                self.turned[first : first + self.reach, half * rows : (half + 1) * rows] = block.T

    def fetch_wide(self, half, tile):
        slot = (half * self.tiles + tile) % 2
        columns = pl.ds(pl.multiple_of(tile * self.span, self.span), self.span)
        return pltpu.make_async_copy(
            self.weights.at[2, :, columns], self.wide.at[slot], self.wide_sem.at[slot]
        )

    def fetch_tall(self, half, tile):
        slot = (half * self.ends + tile) % 2
        rows = pl.ds(pl.multiple_of(tile * self.reach, self.reach), self.reach)
        return pltpu.make_async_copy(
            self.weights.at[pl.ds(0, 2), rows], self.tall.at[slot], self.tall_sem.at[slot]
        )

    def fetch(self, index):
        half, tile = index // self.count, index % self.count

        @pl.when(tile < self.tiles)
        def _():
            self.fetch_wide(half, tile).start()

        @pl.when(tile >= self.tiles)
        def _():
            self.fetch_tall(half, tile - self.tiles).start()

    def run(self, index):
        half, tile = index // self.count, index % self.count
        rows = pl.ds(pl.multiple_of(half * self.half, 16), self.half)

        @pl.when(index + 1 < 2 * self.count)
        def _():
            self.fetch(index + 1)

        @pl.when(tile < self.tiles)
        def _():
            self.fetch_wide(half, tile).wait()
            slot = (half * self.tiles + tile) % 2
            hidden_grad = dot(self.late[half], self.wide[slot], 1, 0)
            columns = pl.ds(pl.multiple_of(tile * self.span, self.span), self.span)
            for side, factor in enumerate(self.factors):
                target = pl.ds(
                    pl.multiple_of(side * self.units + tile * self.span, self.span), self.span
                )
                for s in range(self.sequences):
                    own = slice(s * self.half, (s + 1) * self.half)
                    value = hidden_grad[own] * factor[s, rows, columns].astype(FULL)
                    self.pairs[half, own, target] = value.astype(LOW)

        @pl.when(tile >= self.tiles)
        def _():
            end = tile - self.tiles
            self.fetch_tall(half, end).wait()
            slot = (half * self.ends + end) % 2
            value = dot(self.pairs[half, :, : self.units], self.tall[slot, 0], 1, 1)
            value = value + dot(self.pairs[half, :, self.units :], self.tall[slot, 1], 1, 1)
            value = value.astype(LOW)
            columns = pl.ds(pl.multiple_of(end * self.reach, self.reach), self.reach)
            for s in range(self.sequences):
                self.part[s, rows, columns] = value[s * self.half : (s + 1) * self.half]

    def put(self, index):
        span = self.stage.shape[2]
        columns = pl.ds(pl.multiple_of(index * span, span), span)
        return pltpu.make_async_copy(
            self.stage.at[index % 2], self.grads.at[:, columns], self.stage_sem.at[index % 2]
        )

    def sum(self, index):
        @pl.when(index >= 2)
        def _():
            self.put(index - 2).wait()

        span = self.stage.shape[2]
        columns = pl.ds(pl.multiple_of(index * span, span), span)
        rows = self.sequences * self.half
        for first in range(0, self.width, 768):
            own = slice(first, first + 768)
            value = dot(self.turned[own, :rows], self.pairs[0, :, columns], 1, 0)
            value = value + dot(self.turned[own, rows:], self.pairs[1, :, columns], 1, 0)
            self.stage[index % 2, own, :] = value.astype(LOW)
        self.put(index).start()


def mid_kernel(
    size, late, mixed, branch, cotangent, gains, gate_factor, up_factor, mid, weights,
    low, mixed_grad, gain, grads, *scratch
):
    at = lax.axis_index("fsdp")
    line_greet(at, size)
    part = scratch[0]
    line = LineExchange(
        at,
        size,
        line_span(part.shape[1]),
        part,
        low,
        lambda chunk, rows, total: mid_mid(
            chunk, rows, total, (mixed, branch, cotangent), gains, (mixed_grad, gain)
        ),
        scratch[1:8],
    )
    backward = Backward(late, mid, weights, gate_factor, up_factor, part, grads, scratch[8:])
    backward.fetch(0)

    def one(index, carried):
        backward.run(index)
        return carried

    lax.fori_loop(0, backward.count, one, 0)
    ahead = line.chunks // 2 - 1
    share = -(-backward.count // ahead)

    def both(index, carried):
        line.step(index)

        def more(inner, carried):
            tile = backward.count + index * share + inner

            @pl.when(tile < 2 * backward.count)
            def _():
                backward.run(tile)

            return carried

        lax.fori_loop(0, share, more, 0)
        return carried

    lax.fori_loop(0, ahead, both, 0)
    for copy in backward.fetch_mid():
        copy.start()
    line.run(ahead, ahead + 1)
    backward.turn()
    portion = -(-backward.sums // (line.steps - ahead - 1))

    def rest(index, carried):
        line.step(index)

        def more(inner, carried):
            tile = (index - ahead - 1) * portion + inner

            @pl.when(tile < backward.sums)
            def _():
                backward.sum(tile)

            return carried

        lax.fori_loop(0, portion, more, 0)
        return carried

    lax.fori_loop(ahead + 1, line.steps, rest, 0)
    line.drain()
    backward.put(backward.sums - 2).wait()
    backward.put(backward.sums - 1).wait()


def mid_exchange(
    late, mid, mixed, branch, cotangent, gains, gate_factor, up_factor, weights, collective_id
):
    fsdp, tokens, width = mid.shape
    units = weights.shape[2]
    span, reach, stage = tile_of(units), 384, 384 if fsdp <= 4 else 256
    rows = fsdp * tokens // 2
    dma = pltpu.SemaphoreType.DMA
    return pl.pallas_call(
        functools.partial(mid_kernel, fsdp),
        in_specs=[VMEM_SPEC] * 7 + [ANY_SPEC] * 2,
        out_specs=[VMEM_SPEC] * 3 + [ANY_SPEC],
        out_shape=[
            jax.ShapeDtypeStruct(mid.shape, LOW),
            jax.ShapeDtypeStruct((tokens, width), FULL),
            jax.ShapeDtypeStruct((2, width), FULL),
            jax.ShapeDtypeStruct((width, 2 * units), LOW),
        ],
        scratch_shapes=[pltpu.VMEM(mid.shape, LOW)]
        + line_scratch(fsdp, tokens, width, True)
        + [
            pltpu.VMEM((2, rows, width), LOW),
            pltpu.VMEM((width, 2 * rows), LOW),
            pltpu.VMEM((2, rows, 2 * units), LOW),
            pltpu.VMEM((2, width, span), LOW),
            pltpu.VMEM((2, 2, reach, units), LOW),
            pltpu.VMEM((2, width, stage), LOW),
            dma((2,)),
            dma((2,)),
            dma((2,)),
            dma((2 * fsdp,)),
        ],
        compiler_params=pltpu.CompilerParams(
            vmem_limit_bytes=VMEM_LIMIT, collective_id=collective_id
        ),
        name="mid_exchange",
    )(late, mixed, branch, cotangent, gains, gate_factor, up_factor, mid, weights)


def row_sum(values):
    return jnp.sum(values, 0, keepdims=True)


def add_gain(ref, chunk, index, values):
    @pl.when(chunk == 0)
    def _():
        ref[index : index + 1, :] = row_sum(values)

    @pl.when(chunk > 0)
    def _():
        ref[index : index + 1, :] += row_sum(values)


def branch_mid(chunk, rows, branch, ins, gains, outs):
    (x,), (branch_out, mixed_out) = ins, outs
    branch_out[rows, :] = branch
    post_hat = branch * rms_scale(branch)
    mixed = x[rows, :].astype(FULL) + post_hat * (1.0 + gains[1:2, :])
    mixed_out[rows, :] = mixed
    return (mixed * rms_scale(mixed) * (1.0 + gains[2:3, :])).astype(LOW)


def late_mid(chunk, rows, ffn_branch, ins, gains, outs):
    (mixed, cotangent), (out, gain) = ins, outs
    inv_late = rms_scale(ffn_branch)
    late_hat = ffn_branch * inv_late
    scale = 1.0 + gains[3:4, :]
    out[rows, :] = (mixed[rows, :] + late_hat * scale).astype(LOW)
    upstream = cotangent[rows, :].astype(FULL)
    add_gain(gain, chunk, 0, upstream * late_hat)
    scaled = upstream * scale
    grad = inv_late * (scaled - late_hat * jnp.mean(scaled * late_hat, -1, keepdims=True))
    return grad.astype(LOW)


def mid_mid(chunk, rows, mid_grad, ins, gains, outs):
    (mixed, branch, cotangent), (mixed_grad_out, gain) = ins, outs
    mixed = mixed[rows, :]
    inv_mid = rms_scale(mixed)
    mid_hat = mixed * inv_mid
    add_gain(gain, chunk, 1, mid_grad * mid_hat)
    scaled = mid_grad * (1.0 + gains[2:3, :])
    mixed_grad = cotangent[rows, :].astype(FULL) + inv_mid * (
        scaled - mid_hat * jnp.mean(scaled * mid_hat, -1, keepdims=True)
    )
    mixed_grad_out[rows, :] = mixed_grad
    branch = branch[rows, :]
    inv_post = rms_scale(branch)
    post_hat = branch * inv_post
    add_gain(gain, chunk, 0, mixed_grad * post_hat)
    hat = mixed_grad * (1.0 + gains[1:2, :])
    grad = inv_post * (hat - post_hat * jnp.mean(hat * post_hat, -1, keepdims=True))
    return grad.astype(LOW)


def pre_mid(chunk, rows, normed_grad, ins, gains, outs):
    (x, mixed_grad), (out, gain) = ins, outs
    x = x[rows, :].astype(FULL)
    inv_pre = rms_scale(x)
    normed = x * inv_pre
    add_gain(gain, chunk, 0, normed_grad * normed)
    scaled = normed_grad * (1.0 + gains[0:1, :])
    out[rows, :] = mixed_grad[rows, :] + inv_pre * (
        scaled - normed * jnp.mean(scaled * normed, -1, keepdims=True)
    )


def pair_sums_kernel(ctx, key, value, key_sum, value_sum, *scratch):
    at = lax.axis_index("ctx")
    greet(ctx_peers(at, ctx))
    keys = ctx_scatter(at, ctx, lambda c: key.at[:, c], scratch)
    values = ctx_scatter(at, ctx, lambda c: value.at[:, c], scratch[SCATTER:])
    keys.start()
    values.start()
    keys.diagonal()
    values.diagonal()
    keys.neighbours()
    values.neighbours()
    keys.passing()
    values.passing()
    for scatter, out in ((keys, key_sum), (values, value_sum)):

        def store(block, rows, total, out=out):
            out[block, rows, :] = total

        scatter.finish(store)
    keys.drain()
    values.drain()


def scatter_pairs(key, value):
    sequences, ctx, rows, width = key.shape
    return pl.pallas_call(
        functools.partial(pair_sums_kernel, ctx),
        in_specs=[VMEM_SPEC] * 2,
        out_specs=[VMEM_SPEC] * 2,
        out_shape=[jax.ShapeDtypeStruct((sequences, rows, width), FULL)] * 2,
        scratch_shapes=ctx_scatter_scratch(ctx, sequences, rows, width, LOW) * 2,
        compiler_params=pltpu.CompilerParams(vmem_limit_bytes=VMEM_LIMIT, collective_id=2),
        name="scatter_pairs",
    )(key, value)


def tail_kernel(
    ctx, fsdp, in_part, out_part, pre_part, x, mixed_grad, gains, in_old, out_old, after, *refs
):
    at, line_at = lax.axis_index("ctx"), lax.axis_index("fsdp")
    in_new, out_new, update, gram, input_grad, gain = refs[:6]
    scratch = refs[6:]
    places = head_places(fsdp)
    mine = len(places[0])
    scratch, others = scratch[: 2 * SCATTER], scratch[2 * SCATTER :]
    mine_sum, arrived, move_send, move_receive, out_sum = others[:5]
    head = arrived.shape[-1]
    greet(ctx_peers(at, ctx) + [("fsdp", (line_at + k) % fsdp) for k in range(1, fsdp)])
    ins = ctx_scatter(at, ctx, rows_of_ctx(in_part), scratch)
    outs = ctx_scatter(at, ctx, rows_of_ctx(out_part), scratch[SCATTER:])
    line = LineExchange(
        line_at,
        fsdp,
        line_span(pre_part.shape[1]),
        pre_part,
        None,
        lambda chunk, rows, total: pre_mid(
            chunk, rows, total, (x, mixed_grad), gains, (input_grad, gain)
        ),
        others[5:10],
    )
    ins.start()
    outs.start()
    ins.diagonal()
    ins.neighbours()
    line.run(0, 3)
    ins.passing()
    outs.diagonal()
    outs.neighbours()
    line.run(3, 6)
    outs.passing()
    line.run(6, 8)

    def store_in(block, rows, total):
        mine_sum[rows, :] = total.astype(LOW)

    def store_out(block, rows, total):
        out_sum[rows, :] = total

    ins.finish(store_in)

    def copies_of(owner, index):
        return [
            (user, slot)
            for user in range(fsdp)
            for slot in range(mine)
            if places[user][slot] == (owner, index)
        ]

    def move(user, slot):
        owner, index = places[user][slot]
        copy = copies_of(owner, index).index((user, slot))
        return remote(
            mine_sum.at[:, pl.ds(slot * head, head)],
            arrived.at[index, copy],
            move_send.at[slot],
            move_receive.at[index, copy],
            "fsdp",
            owner,
        )

    for user in range(fsdp):
        for slot in range(mine):

            @pl.when(line_at == user)
            def _(user=user, slot=slot):
                owner, index = places[user][slot]
                if owner == user:
                    copy = copies_of(owner, index).index((user, slot))
                    arrived[index, copy] = mine_sum[:, slot * head : (slot + 1) * head]
                else:
                    move(user, slot).start()

    line.run(8, line.steps)
    outs.finish(store_out)

    def step_of(index, grad, old_ref, new_ref, at):
        new = MOMENTUM_DECAY * old_ref[:, at, :] + grad
        new_ref[:, at, :] = new
        low = (grad + MOMENTUM_DECAY * new).astype(LOW)
        update[index] = low
        gram[index] = dot(low, low, 0, 0)

    stored = in_old.shape[1]
    for index in range(out_old.shape[1]):
        grad = out_sum[:, index * head : (index + 1) * head]
        step_of(stored + index, grad, out_old, out_new, index)
    for index in range(stored + out_old.shape[1], gram.shape[0]):
        gram[index] = jnp.zeros((head, head), FULL)
    for owner in range(fsdp):

        @pl.when(line_at == owner)
        def _(owner=owner):
            for index in range(stored):
                for user, slot in copies_of(owner, index):
                    if user != owner:
                        move(user, slot).wait_recv()

    for index in range(stored):
        grad = arrived[index, 0].astype(FULL)
        for copy in range(1, arrived.shape[1]):
            more = arrived[index, copy].astype(FULL)
            paired = line_at * stored + index >= QUERY_HEADS
            grad = grad + jnp.where(paired, more, 0.0)
        step_of(index, grad, in_old, in_new, index)
    for user in range(fsdp):
        for slot in range(mine):
            if places[user][slot][0] != user:

                @pl.when(line_at == user)
                def _(user=user, slot=slot):
                    move(user, slot).wait_send()

    ins.drain()
    outs.drain()
    line.drain()


def tail(in_part, out_part, pre_part, x, mixed_grad, gains, in_old, out_old, after):
    _, stored, head = in_old.shape
    matrices = stored + out_old.shape[1]
    ctx, rows, in_width = in_part.shape
    out_width = out_part.shape[2]
    fsdp, tokens, width = pre_part.shape
    mine = len(head_places(fsdp)[0])
    copies = max(1, fsdp // KEY_VALUE_HEADS)
    dma = pltpu.SemaphoreType.DMA
    return pl.pallas_call(
        functools.partial(tail_kernel, ctx, fsdp),
        in_specs=[VMEM_SPEC] * 8 + [ANY_SPEC],
        out_specs=[VMEM_SPEC] * 6,
        out_shape=[
            jax.ShapeDtypeStruct(in_old.shape, FULL),
            jax.ShapeDtypeStruct(out_old.shape, FULL),
            jax.ShapeDtypeStruct((matrices, rows, head), LOW),
            jax.ShapeDtypeStruct((ctx * (-(-matrices // ctx)), head, head), FULL),
            jax.ShapeDtypeStruct((tokens, width), FULL),
            jax.ShapeDtypeStruct((1, width), FULL),
        ],
        scratch_shapes=ctx_scatter_scratch(ctx, 1, rows, in_width, LOW)
        + ctx_scatter_scratch(ctx, 1, rows, out_width, LOW)
        + [
            pltpu.VMEM((rows, in_width), LOW),
            pltpu.VMEM((stored, copies, rows, head), LOW),
            dma((mine,)),
            dma((stored, copies)),
            pltpu.VMEM((rows, out_width), FULL),
        ]
        + line_scratch(fsdp, tokens, width, False),
        compiler_params=pltpu.CompilerParams(vmem_limit_bytes=VMEM_LIMIT, collective_id=3),
        name="tail",
    )(in_part, out_part, pre_part, x, mixed_grad, gains, in_old, out_old, after)


def packed_rows(small, large):
    squares = -(-small // 2)
    return squares * FBLK + large * 2 * FBLK + 16 * (-(-(squares + large) // 16))


def grid_of(size):
    rows = lax.broadcasted_iota(jnp.int32, (size, size), 0)
    return rows, lax.broadcasted_iota(jnp.int32, (size, size), 1)


def pack_two(first, second):
    rows, columns = grid_of(FBLK)
    if second is None:
        return first, jnp.zeros((1, FBLK), FULL)
    diagonal = jnp.sum(jnp.where(rows == columns, second, 0.0), 0, keepdims=True)
    return jnp.where(rows <= columns, first, second), diagonal


def unpack_two(square, diagonal, both):
    rows, columns = grid_of(FBLK)
    if not both:
        return square, None
    turned = square.T
    first = jnp.where(rows <= columns, square, turned)
    second = jnp.where(rows > columns, square, jnp.where(rows < columns, turned, diagonal))
    return first, second


def pack_all(blocks, heads, write):
    small, large = blocks[0], heads[0]
    squares = -(-small // 2)
    edge = squares * FBLK + large * 2 * FBLK
    for index in range(squares):
        second = blocks[1](2 * index + 1) if 2 * index + 1 < small else None
        square, diagonal = pack_two(blocks[1](2 * index), second)
        write(index * FBLK, square)
        write(edge + index, diagonal)
    for index in range(large):
        head = heads[1](index)
        square, diagonal = pack_two(head[:FBLK, :FBLK], head[FBLK:, FBLK:])
        base = squares * FBLK + index * 2 * FBLK
        write(base, square)
        write(base + FBLK, head[:FBLK, FBLK:])
        write(edge + squares + index, diagonal)


def unpack_all(small, large, read):
    squares = -(-small // 2)
    edge = squares * FBLK + large * 2 * FBLK
    blocks, heads = [], []
    for index in range(squares):
        both = 2 * index + 1 < small
        first, second = unpack_two(read(index * FBLK, FBLK), read(edge + index, 1), both)
        blocks += [first, second] if both else [first]
    for index in range(large):
        base = squares * FBLK + index * 2 * FBLK
        first, second = unpack_two(read(base, FBLK), read(edge + squares + index, 1), True)
        corner = read(base + FBLK, FBLK)
        heads.append(
            jnp.concatenate(
                [
                    jnp.concatenate([first, corner], 1),
                    jnp.concatenate([corner.T, second], 1),
                ],
                0,
            )
        )
    return blocks, heads


def newton_kernel(
    ctx, fsdp, head_rate, ffn_rate, heads, blocks, gains, head_update, in_old, out_old, ffn_update,
    ffn_old, in_new, out_new, ffn_new, gains_all, *scratch
):
    at, line_at = lax.axis_index("ctx"), lax.axis_index("fsdp")
    small, large = blocks.shape[1], heads.shape[1]
    packed, gram, poly, poly_all, gains_line, gains_sum, gain_send, gain_receive = scratch[:8]
    update, weights, update_sem, weight_sem, out_sem = scratch[8:13]
    scratch = scratch[13:]
    matrices, _, width = weights.shape
    per_matrix = width // FBLK
    count = matrices * per_matrix
    greet(ctx_peers(at, ctx) + [("fsdp", (line_at + k) % fsdp) for k in range(1, fsdp)])

    def gain_copy(k):
        return remote(
            gains,
            gains_line.at[k],
            gain_send.at[k],
            gain_receive.at[k],
            "fsdp",
            (line_at + k) % fsdp,
        )

    def fetches(matrix):
        return [
            pltpu.make_async_copy(
                ffn_update.at[matrix], update.at[matrix], update_sem.at[matrix]
            ),
            pltpu.make_async_copy(ffn_old.at[matrix], weights.at[matrix], weight_sem.at[matrix]),
        ]

    for k in range(1, fsdp):
        gain_copy(k).start()
    edge = packed_rows(small, large) - 16 * (-(-(-(-small // 2) + large) // 16))

    def pack_for(index, carried):
        packed[index, edge:, :] = jnp.zeros((packed.shape[1] - edge, FBLK), FULL)

        def write(first, rows):
            packed[index, first : first + rows.shape[0], :] = rows

        pack_all((small, lambda i: blocks[index, i]), (large, lambda i: heads[index, i]), write)
        return carried

    lax.fori_loop(0, ctx, pack_for, 0)
    scatter = ctx_scatter(at, ctx, rows_of_ctx(packed), scratch)
    scatter.start()
    for matrix in range(matrices):
        for copy in fetches(matrix):
            copy.start()
    scatter.diagonal()
    scatter.neighbours()
    scatter.passing()
    total = gains[...]
    for k in range(1, fsdp):
        gain_copy(k).wait_recv()
        total = total + gains_line[k]
    gains_sum[...] = total
    scratch = scratch[SCATTER:]
    gather_gains = CtxGather(at, ctx, gains_sum, lambda c: gains_all.at[c], 0, scratch[:5])
    gather = CtxGather(at, ctx, poly, lambda c: poly_all.at[c], 0, scratch[5:10])

    def store(block, rows, total):
        gram[rows, :] = total

    scatter.finish(store)
    gather_gains.start()
    block_grams, head_grams = unpack_all(
        small, large, lambda first, count: gram[first : first + count, :]
    )
    head_polys, block_polys = polys_of(head_grams), polys_of(block_grams)
    poly[edge:, :] = jnp.zeros((poly.shape[0] - edge, FBLK), FULL)

    def write(first, rows):
        poly[first : first + rows.shape[0], :] = rows

    pack_all((small, lambda i: block_polys[i]), (large, lambda i: head_polys[i]), write)
    gather.start()
    for matrix in range(matrices):
        for copy in fetches(matrix):
            copy.wait()

    def place(block):
        matrix = block // per_matrix
        columns = pl.ds(pl.multiple_of((block % per_matrix) * FBLK, FBLK), FBLK)
        return matrix, columns

    def put(block):
        matrix, columns = place(block)
        return pltpu.make_async_copy(
            weights.at[matrix, :, columns], ffn_new.at[matrix, :, columns], out_sem.at[block]
        )

    def apply(source, first):
        found, _ = unpack_all(small, 0, lambda row, count: source(row, count))
        for index, found_poly in enumerate(found):
            block = first * small + index

            @pl.when(block < count)
            def _(block=block, found_poly=found_poly):
                matrix, columns = place(block)
                step = moved(update[matrix, :, columns], found_poly)
                weights[matrix, :, columns] = weights[matrix, :, columns] * SHRINK - ffn_rate * step
                put(block).start()

    shift = large * 2 * FBLK

    def reader(view):
        edge_small = -(-small // 2) * FBLK

        def read(row, count):
            row = row + shift if row >= edge_small else row
            return view[row : row + count, :]

        return read

    apply(reader(poly), at)
    gather_gains.forward()
    gather.forward()
    gather_gains.rest()
    gather.rest()
    square = gather.square
    for j in range(square.column):
        for turn in (False, True):
            if j > 0 or turn:
                device = square.device(j, turn)
                apply(reader(poly_all.at[device]), device)
    for k in range(1, fsdp):
        gain_copy(k).wait_send()
    gather_gains.finish()
    gather.finish()
    for j in range(square.column):
        for turn in (False, True):
            device = square.device(j, turn, 1 - square.core)
            apply(reader(poly_all.at[device]), device)
    stored = in_old.shape[1]
    for device in range(ctx):
        first = device * large
        if first < head_update.shape[0]:
            _, found = unpack_all(
                small, large, lambda row, count: poly_all[device, row : row + count, :]
            )
            for index in range(first, min(first + large, head_update.shape[0])):
                step = head_rate * moved(head_update[index], found[index - first])
                if index < stored:
                    in_new[:, index, :] = in_old[:, index, :] * SHRINK - step
                else:
                    out_new[:, index - stored, :] = out_old[:, index - stored, :] * SHRINK - step
    scatter.drain()

    def finish(block, carried):
        put(block).wait()
        return carried

    lax.fori_loop(0, count, finish, 0)


def newton(
    heads, blocks, gains, head_update, in_old, out_old, ffn_update, ffn_old, head_rate, ffn_rate, fsdp
):
    ctx, large = heads.shape[:2]
    small = blocks.shape[1]
    rows = packed_rows(small, large)
    dma = pltpu.SemaphoreType.DMA
    matrices = ffn_old.shape[0]
    return pl.pallas_call(
        functools.partial(newton_kernel, ctx, fsdp, head_rate, ffn_rate),
        in_specs=[VMEM_SPEC] * 6 + [ANY_SPEC] * 2,
        out_specs=[VMEM_SPEC] * 2 + [ANY_SPEC, VMEM_SPEC],
        out_shape=[
            jax.ShapeDtypeStruct(in_old.shape, FULL),
            jax.ShapeDtypeStruct(out_old.shape, FULL),
            jax.ShapeDtypeStruct(ffn_old.shape, FULL),
            jax.ShapeDtypeStruct((ctx,) + gains.shape, FULL),
        ],
        scratch_shapes=[
            pltpu.VMEM((ctx, rows, FBLK), FULL),
            pltpu.VMEM((rows, FBLK), FULL),
            pltpu.VMEM((rows, FBLK), FULL),
            pltpu.VMEM((ctx, rows, FBLK), FULL),
            pltpu.VMEM((fsdp,) + gains.shape, FULL),
            pltpu.VMEM(gains.shape, FULL),
            dma((fsdp,)),
            dma((fsdp,)),
            pltpu.VMEM(ffn_update.shape, LOW),
            pltpu.VMEM(ffn_old.shape, FULL),
            dma((matrices,)),
            dma((matrices,)),
            dma((ctx * small,)),
        ]
        + ctx_scatter_scratch(ctx, 1, rows, FBLK, FULL)
        + ctx_gather_sems(ctx) * 2,
        compiler_params=pltpu.CompilerParams(vmem_limit_bytes=VMEM_LIMIT, collective_id=4),
        name="newton",
    )(heads, blocks, gains, head_update, in_old, out_old, ffn_update, ffn_old)


def local(
    inputs,
    cotangent,
    weights_in,
    weights_out,
    ffn_weights,
    norm_gains,
    momentum_in,
    momentum_out,
    ffn_momentum,
    gain_first,
    gain_second,
    stretch_order,
):
    sequences, rows, width = inputs.shape
    stretch_rows = rows // 2
    local_rows, in_local, head = weights_in.shape
    out_local = weights_out.shape[1]
    ffn_local = ffn_weights.shape[2]
    ctx, fsdp = lax.axis_size("ctx"), lax.axis_size("fsdp")
    ctx_at = lax.axis_index("ctx")
    tokens = sequences * rows
    all_sequences = sequences * fsdp
    heads = QUERY_HEADS // fsdp
    pairs = max(1, KEY_VALUE_HEADS // fsdp)
    shared = heads // pairs
    mine = heads + 2 * pairs

    ffn_mine = jnp.transpose(ffn_weights, (1, 0, 2))

    flat = inputs.reshape(tokens, width)
    mine_in, w_out, ffn_cut, own_normed = prepare(
        weights_in, weights_out, ffn_mine, flat, norm_gains, ctx, fsdp
    )
    ffn_low = lax.all_gather(ffn_cut, "ctx", axis=1, tiled=True)
    own_places = positions_of(
        ctx_at * rows + jnp.arange(rows, dtype=jnp.int32), stretch_order, stretch_rows
    )
    all_places = positions_of(
        jnp.arange(ctx * rows, dtype=jnp.int32), stretch_order, stretch_rows
    )
    cosine, sine = rope_tables(own_places, head)
    normed_low, w_in, query, key_all, value_all = project(
        own_normed,
        mine_in,
        jnp.tile(cosine, (sequences, 1)),
        jnp.tile(sine, (sequences, 1)),
        sequences,
        heads,
        pairs,
        ctx,
        fsdp,
    )
    normed_low = normed_low.reshape(fsdp * tokens, width)
    w_out = w_out.reshape(width, out_local * head)
    cosine, sine = jnp.tile(cosine, (all_sequences, 1)), jnp.tile(sine, (all_sequences, 1))
    scale = head ** (-0.5)

    def column(values, index):
        return values[:, index * head : (index + 1) * head]

    def by_sequence(columns):
        return jnp.concatenate([c.reshape(all_sequences, rows, head) for c in columns], 1)

    def flat_heads(values, count):
        return [
            values[:, g * rows : (g + 1) * rows].reshape(all_sequences * rows, head)
            for g in range(count)
        ]

    def heads_of(pair):
        return range(pair * shared, (pair + 1) * shared)

    query = [by_sequence([column(query, h) for h in heads_of(pair)]) for pair in range(pairs)]
    key_all = key_all.reshape(all_sequences, ctx * rows, pairs * head)
    value_all = value_all.reshape(all_sequences, ctx * rows, pairs * head)
    key_of = [key_all[:, :, p * head : (p + 1) * head] for p in range(pairs)]
    value_of = [value_all[:, :, p * head : (p + 1) * head] for p in range(pairs)]
    visible = jnp.tile(all_places[None, :] <= own_places[:, None], (shared, 1))[None]
    exponent, slope, exponent_low, row_total, attended = [], [], [], [], []
    for p in range(pairs):
        scores = batched(query[p], key_of[p], 2, 2)
        squashed = jnp.tanh(scores / SOFT_CAP)
        exponent.append(jnp.where(visible, jnp.exp(SOFT_CAP * squashed - EXP_SHIFT), 0.0))
        slope.append(exponent[p] * (1.0 - squashed * squashed))
        row_total.append(jnp.sum(exponent[p], -1, keepdims=True))
        exponent_low.append(exponent[p].astype(LOW))
        attended.append(batched(exponent_low[p], value_of[p], 2, 1) / row_total[p])
    attended_low = jnp.concatenate(
        sum([flat_heads(attended[p].astype(LOW), shared) for p in range(pairs)], []), 1
    )

    def parts(values):
        return values.astype(LOW).reshape(fsdp, tokens, width)

    full_rows = jax.ShapeDtypeStruct((tokens, width), FULL)
    low_rows = jax.ShapeDtypeStruct((tokens, width), LOW)

    def gain_rows(count):
        return jax.ShapeDtypeStruct((count, width), FULL)

    upstream = cotangent.reshape(tokens, width)
    mid_low, branch, mixed = exchange(
        parts(dot(attended_low, w_out, 1, 1)),
        [flat],
        norm_gains,
        branch_mid,
        [full_rows, full_rows],
        fsdp,
        5,
        "branch_exchange",
    )

    late_low, outputs, gain_late, hidden_low, gate_factor, up_factor = late_exchange(
        mid_low, ffn_low, mixed, upstream, norm_gains, 6
    )
    down_grads = lax.psum_scatter(
        dot(
            late_low.reshape(fsdp * tokens, width),
            hidden_low.reshape(fsdp * tokens, ffn_local),
            0,
            0,
        ).astype(LOW),
        "ctx",
        scatter_dimension=0,
        tiled=True,
    )
    branch_low, mixed_grad, gain_middle, pair_part = mid_exchange(
        late_low, mid_low, mixed, branch, upstream, norm_gains, gate_factor, up_factor, ffn_low, 7
    )
    pair_grads = lax.psum_scatter(pair_part, "ctx", scatter_dimension=0, tiled=True)

    branch_low = branch_low.reshape(fsdp * tokens, width)
    attended_grad = dot(branch_low, w_out, 1, 0)
    query_grad, key_part, value_part = [], [], []
    for p in range(pairs):
        grad = by_sequence([column(attended_grad, h) for h in heads_of(p)])
        numerator_low = (grad / row_total[p]).astype(LOW)
        row_term = jnp.sum(grad * attended[p], -1, keepdims=True) / row_total[p]
        pulled = batched(numerator_low, value_of[p], 2, 2)
        score_low = (slope[p] * (pulled - row_term)).astype(LOW)
        query_grad += flat_heads(batched(score_low, key_of[p], 2, 1), shared)
        key_part.append(batched(score_low, query[p], 1, 1).astype(LOW))
        value_part.append(batched(exponent_low[p], numerator_low, 1, 1).astype(LOW))
    spread = (all_sequences, ctx, rows, pairs * head)
    key_grad, value_grad = scatter_pairs(
        jnp.concatenate(key_part, 2).reshape(spread), jnp.concatenate(value_part, 2).reshape(spread)
    )
    key_grad = key_grad.reshape(all_sequences * rows, pairs * head)
    value_grad = value_grad.reshape(all_sequences * rows, pairs * head)
    projected_grad = jnp.concatenate(
        [rotate(grad * scale, cosine, -sine) for grad in query_grad]
        + [rotate(column(key_grad, p), cosine, -sine) for p in range(pairs)]
        + [value_grad],
        1,
    ).astype(LOW)
    momentum = jnp.transpose(ffn_momentum, (1, 0, 2))
    small = -(-3 * (ffn_local // FBLK) // ctx)
    earlier = ffn_gram(down_grads, momentum, 2, ctx * small, [])
    momentum_new_in, momentum_new_out, head_update, head_gram, input_grad, gain_pre = tail(
        dot(normed_low, projected_grad, 0, 0).astype(LOW).reshape(ctx, local_rows, mine * head),
        dot(branch_low, attended_low, 0, 0).astype(LOW).reshape(ctx, local_rows, out_local * head),
        parts(dot(projected_grad, w_in, 1, 1)),
        flat,
        mixed_grad,
        norm_gains,
        momentum_in,
        momentum_out,
        earlier[2][-1, :8],
    )
    input_grad = input_grad.reshape(inputs.shape)
    outputs = outputs.reshape(inputs.shape)
    gain_parts = jnp.concatenate([gain_pre, gain_middle, gain_late], 0)

    new_ffn, ffn_update, block_gram = ffn_gram(pair_grads, momentum, 0, ctx * small, earlier)
    new_weights_in, new_weights_out, new_ffn_weights, gain_every = newton(
        head_gram.reshape(ctx, -1, head, head),
        block_gram.reshape(ctx, small, FBLK, FBLK),
        gain_parts,
        head_update,
        weights_in,
        weights_out,
        ffn_update,
        ffn_mine,
        LEARN_RATE * (width / head) ** 0.5,
        LEARN_RATE * (width / FBLK) ** 0.5,
        fsdp,
    )
    gain_grad = jnp.sum(gain_every, 0)
    new_gain_first = BETA_ONE * gain_first + (1.0 - BETA_ONE) * gain_grad
    new_gain_second = BETA_TWO * gain_second + (1.0 - BETA_TWO) * gain_grad * gain_grad
    corrected_one = new_gain_first / (1.0 - BETA_ONE**STEP)
    corrected_two = new_gain_second / (1.0 - BETA_TWO**STEP)
    new_norm_gains = norm_gains - GAIN_RATE * corrected_one / (jnp.sqrt(corrected_two) + ADAM_EPS)
    return (
        outputs,
        input_grad,
        new_weights_in,
        new_weights_out,
        jnp.transpose(new_ffn_weights, (1, 0, 2)),
        momentum_new_in,
        momentum_new_out,
        jnp.transpose(new_ffn, (1, 0, 2)),
        new_norm_gains,
        new_gain_first,
        new_gain_second,
    )


def solution(mesh):
    return jax.shard_map(
        local,
        mesh=mesh,
        in_specs=(
            P("fsdp", "ctx", None),
            P("fsdp", "ctx", None),
            P("ctx", "fsdp", None),
            P("ctx", "fsdp", None),
            P("ctx", None, "fsdp"),
            P(),
            P("ctx", "fsdp", None),
            P("ctx", "fsdp", None),
            P("ctx", None, "fsdp"),
            P(),
            P(),
            P(),
        ),
        out_specs=(
            P("fsdp", "ctx", None),
            P("fsdp", "ctx", None),
            P("ctx", "fsdp", None),
            P("ctx", "fsdp", None),
            P("ctx", None, "fsdp"),
            P("ctx", "fsdp", None),
            P("ctx", "fsdp", None),
            P("ctx", None, "fsdp"),
            P(),
            P(),
            P(),
        ),
        check_vma=False,
    )
```

time: 2550 us -> 688 us (0.27)
  waiting for transfers between devices: 1680 us -> 13.3 us
  Pallas kernels: 0 us -> 579 us
  matrix products: 492 us -> 44.6 us
  local copies, waits for them, and re-layouts: 178 us -> 20.1 us
  other arithmetic: 116 us -> 6.08 us
  blocking collectives: 48.7 us -> 0 us
    all_gather x11 -> x1, waiting for transfers between devices: 848 us -> 4.04 us  [local(): ffn_low = lax.all_gather(ffn_cut, 'ctx', axis=1, tiled=True)]
    pallas_call x0 -> x10, Pallas kernels: none -> 579 us  [the longest x1 105 us: mid_exchange(): pl.pallas_call(functools.partial(mid_kernel, fsdp), in_specs=[VMEM_SPEC]...]
    dot_general x53 -> x12, matrix products: 492 us -> 44.6 us  [the longest x6 28.2 us: dot(): lax.dot_general(left, right, (((left_dim,), (right_dim,)), ((), ())), pre...]
    psum x6 -> x0, waiting for transfers between devices: 418 us -> none  [the longest x5 247 us: gram_pair(): lax.psum(self_gram(head_part).astype(jnp.bfloat16), 'ctx')]
    reduce_scatter x4 -> x2, waiting for transfers between devices: 417 us -> 9.2 us  [the longest x1 9.2 us: local(): lax.psum_scatter(pair_part, 'ctx', scatter_dimension=0, tiled=True)]
    reshape x4 -> x0, local copies, waits for them, and re-layouts: 55 us -> none  [the longest x1 28.4 us: local(): grad_c.reshape(lax.axis_size('ctx') * local_rows, 2 * ffn_local)]
    psum x1 -> x0, blocking collectives: 39.8 us -> none  [local(): lax.psum(jnp.stack([gain_pre_grad, gain_post_grad, gain_mid_grad, gain_la...]
    concatenate x6 -> x1, other arithmetic: 41.1 us -> 1.35 us  [local(): gain_parts = jnp.concatenate([gain_pre, gain_middle, gain_late], 0)]
  transfers between devices with their start and end apart: 21 -> 3, of which waited for: 17 -> 2; matrix products, arithmetic and copies ran while one was open for 12% -> 6% of each run, Pallas kernels for 0% -> 57%
where the time goes in v1:
time: 688 us; the launch traced here: 678 us
  Pallas kernels  579 us (84%)
  matrix products  44.6 us (6%)
  local copies, waits for them, and re-layouts  20.1 us (3%)
  between operations  14.6 us (2%)
  waiting for transfers between devices  13.3 us (2%)
    pallas_call x1, Pallas kernels, mid_exchange(): pl.pallas_call(functools.partial(mid_kernel, fsdp), in_specs=[VMEM_SPEC]...  105 us
    pallas_call x1, Pallas kernels, late_exchange(): pl.pallas_call(functools.partial(late_kernel, fsdp), in_specs=[VMEM_SPEC]...  93.9 us
    pallas_call x1, Pallas kernels, project(): pl.pallas_call(functools.partial(project_kernel, ctx, fsdp, tokens // chu...  88.4 us
    pallas_call x1, Pallas kernels, tail(): pl.pallas_call(functools.partial(tail_kernel, ctx, fsdp), in_specs=[VMEM_...  87.6 us
    pallas_call x1, Pallas kernels, exchange(): pl.pallas_call(functools.partial(exchange_kernel, mid, fsdp, len(ins)), i...  75.1 us
    pallas_call x1, Pallas kernels, newton(): pl.pallas_call(functools.partial(newton_kernel, ctx, fsdp, head_rate, ffn...  63.7 us
    dot_general x6, matrix products, dot(): lax.dot_general(left, right, (((left_dim,), (right_dim,)), ((), ())), pre...  28.2 us
    pallas_call x1, Pallas kernels, scatter_pairs(): pl.pallas_call(functools.partial(pair_sums_kernel, ctx), in_specs=[VMEM_S...  26.5 us
  transfers between devices with their start and end apart: 3, of which 2 were waited for; matrix products, arithmetic and copies ran while one was open for 6% of the time, Pallas kernels for 57%

profile of v1, /device:TPU:0, one launch (start us, length us, event | category | flops | bytes accessed | tf_op | source)
XLA Modules:
  0.0 678.0 jit_solution(5959913055869074304)
XLA Ops:
  7.2 0.0 all-gather.2.cloned.1.call-start
  7.2 25.0 %prepare.1 = (bf16[288,1024]{1,0:T(8,128)(2,1)}, bf16[8,288,512]{2,1,0:T(8,128)(2,1)}, bf16[3,288,2304]{2,1,0:T(8,128)(2,1)}, bf16[128,2304]{1,0:T(8,128)(2,1)}) custom-call(f32[288,4,256]{2,1,0:T(4,128)} %in_old.3, f32[288,2,256]{2,1,0:T(2,128)} %out_old.3, f32[3,288,2304]{2,1,0:T(8,128)} %bitcast.104, bf16[128,2304]{1,0:T(8,128)(2,1)} %bitcast.110, ...), custom_call_target="tpu_custom_call" | custom-call | tf_op jit(solution)/shard_map/prepare/pallas_call | solution.py:706
  32.2 0.0 copy-start.13
  32.2 0.0 all-gather.2.cloned.1.call-update
  32.2 0.0 reduce-scatter.3.cloned.1.call-start
  32.3 0.5 copy-done.13
  32.8 0.1 select_reduce_fusion.1
  32.9 1.0 fusion.16
  33.9 88.4 %project.1 = (bf16[4,128,2304]{2,1,0:T(8,128)(2,1)}, bf16[2304,1024]{1,0:T(8,128)(2,1)}, bf16[512,512]{1,0:T(8,128)(2,1)}, bf16[4,8,128,256]{3,2,1,0:T(8,128)(2,1)}, bf16[4,8,128,256]{3,2,1,0:T(8,128)(2,1)}) custom-call(bf16[128,2304]{1,0:T(8,128)(2,1)} %get-tuple-element.51.own, bf16[288,1024]{1,0:T(8,128)(2,1)} %get-tuple-element.52.mine, ...), custom_call_target="tpu_custom_call" | custom-call | tf_op jit(solution)/shard_map/project/pallas_call | solution.py:822
  122.3 0.1 select_reduce_fusion
  122.4 0.1 broadcast_compare_fusion
  122.6 1.2 fusion.37
  123.8 0.1 tile.10
  123.9 4.2 fusion
  128.0 0.0 copy-start.19
  128.1 1.6 fusion.38
  129.7 0.5 copy-done.19
  130.2 1.0 copy-done.15
  131.2 2.8 convolution_convert_fusion.3
  134.1 75.1 %branch_exchange.1 = (bf16[4,128,2304]{2,1,0:T(8,128)(2,1)}, f32[128,2304]{1,0:T(8,128)}, f32[128,2304]{1,0:T(8,128)}) custom-call(bf16[4,128,2304]{2,1,0:T(8,128)(2,1)} %bitcast.114, bf16[128,2304]{1,0:T(8,128)(2,1)} %bitcast.111, f32[4,2304]{1,0:T(4,128)} %gains.7), custom_call_target="tpu_custom_call" | custom-call | tf_op jit(solution)/shard_map/branch_exchange/pallas_call | solution.py:989
  209.2 4.0 all-gather.2.cloned.1.call-done.weights
  213.3 93.9 %late_exchange.1 = (bf16[4,128,2304]{2,1,0:T(8,128)(2,1)}, bf16[128,2304]{1,0:T(8,128)(2,1)}, f32[1,2304]{1,0:T(1,128)}, bf16[4,128,2304]{2,1,0:T(8,128)(2,1)}, ...) custom-call(bf16[4,128,2304]{2,1,0:T(8,128)(2,1)} %get-tuple-element.57.mid, ...), custom_call_target="tpu_custom_call" | custom-call | tf_op jit(solution)/shard_map/late_exchange/pallas_call | solution.py:1146
  307.1 10.4 %bitcast_convert_fusion = bf16[2304,2304]{1,0:T(8,128)(2,1)} fusion(bf16[4,128,2304]{2,1,0:T(8,128)(2,1)} %get-tuple-element.62.late, bf16[4,128,2304]{2,1,0:T(8,128)(2,1)} %get-tuple-element.71), kind=kOutput, calls=%fused_computation | convolution fusion | flops 5441126400 | bytes 15335424 | tf_op jit(solution)/shard_map/dot_general | solution.py:71
  317.5 0.0 reduce-scatter.3.cloned.1.call-update
  317.5 0.0 reduce-scatter.5.cloned.1.call-start
  317.6 104.9 %mid_exchange.1 = (bf16[4,128,2304]{2,1,0:T(8,128)(2,1)}, f32[128,2304]{1,0:T(8,128)}, f32[2,2304]{1,0:T(2,128)}, bf16[2304,4608]{1,0:T(8,128)(2,1)}) custom-call(bf16[4,128,2304]{2,1,0:T(8,128)(2,1)} %get-tuple-element.62.late, f32[128,2304]{1,0:T(8,128)} %get-tuple-element.58.mixed, f32[128,2304]{1,0:T(8,128)} %get-tuple-element.63.branch, ...), custom_call_target="tpu_custom_call" | custom-call | tf_op jit(solution)/shard_map/mid_exchange/pallas_call | solution.py:1377
  422.5 0.0 reduce-scatter.5.cloned.1.call-update
  422.5 0.0 copy-start.20
  422.5 3.9 fusion.39
  426.4 0.1 fusion.35
  426.5 0.2 multiply_reduce_fusion
  426.7 0.0 copy-done.20
  426.8 1.3 copy-done.18
  428.1 2.7 multiply_convert_fusion
  430.8 2.3 convolution_convert_fusion.5
  433.1 3.2 convolution_convert_fusion.4
  436.3 26.5 %scatter_pairs.1 = (f32[4,128,256]{2,1,0:T(8,128)}, f32[4,128,256]{2,1,0:T(8,128)}) custom-call(bf16[4,8,128,256]{3,2,1,0:T(8,128)(2,1)} %bitcast.107, bf16[4,8,128,256]{3,2,1,0:T(8,128)(2,1)} %bitcast.122), custom_call_target="tpu_custom_call" | custom-call | tf_op jit(solution)/shard_map/scatter_pairs/pallas_call | solution.py:1501
  462.8 1.1 convert.28
  463.9 0.0 copy-start.4
  463.9 2.4 fusion.40
  466.3 0.1 slice_multiply_fusion
  466.4 0.0 copy-done.4
  466.4 0.0 copy-done.8
  466.4 0.2 fusion.14
  466.9 1.0 copy-done.16
  468.0 2.9 convolution_convert_fusion.2
  470.9 4.3 convolution_convert_fusion
  475.2 3.9 convolution_convert_fusion.1
  479.1 5.5 ffn_gram.2
  484.6 1.3 slice_bitcast_fusion.after
  485.9 87.6 %tail.1 = (f32[288,4,256]{2,1,0:T(4,128)}, f32[288,2,256]{2,1,0:T(2,128)}, bf16[6,288,256]{2,1,0:T(8,128)(2,1)}, f32[8,256,256]{2,1,0:T(8,128)}, f32[128,2304]{1,0:T(8,128)}, /*index=5*/f32[1,2304]{1,0:T(1,128)}) custom-call(bf16[8,288,1024]{2,1,0:T(8,128)(2,1)} %bitcast.113, bf16[8,288,512]{2,1,0:T(8,128)(2,1)} %bitcast.115, ...), custom_call_target="tpu_custom_call" | custom-call | tf_op jit(solution)/shard_map/tail/pallas_call | solution.py:1643
  573.5 1.3 pad_maximum_fusion.7.gains
  574.9 9.2 %reduce-scatter.5.cloned.1.call-done.grad_ref = bf16[288,4608]{1,0:T(8,128)(2,1)} async-done(((bf16[2304,4608]{1,0:T(8,128)(2,1)}), bf16[288,4608]{1,0:T(8,128)(2,1)}) %reduce-scatter.5.cloned.1.call-update) | async-done | bytes 2654224 | tf_op jit(solution)/shard_map/reduce_scatter | solution.py:2068
  584.1 8.7 %ffn_gram.3 = (f32[3,288,2304]{2,1,0:T(8,128)}, bf16[3,288,2304]{2,1,0:T(8,128)(2,1)}, f32[56,128,128]{2,1,0:T(8,128)}) custom-call(bf16[288,4608]{1,0:T(8,128)(2,1)} %reduce-scatter.5.cloned.1.call-done.grad_ref, f32[3,288,2304]{2,1,0:T(8,128)} %bitcast.103, ...), custom_call_target="tpu_custom_call", output_to_operand_aliasing={{0}: (2, {}), {1}: (3, {}), {2}: (4, {})} | custom-call | tf_op jit(solution)/shard_map/ffn_gram/pallas_call | solution.py:94
  592.8 63.7 %newton.1 = (f32[288,4,256]{2,1,0:T(4,128)}, f32[288,2,256]{2,1,0:T(2,128)}, f32[3,288,2304]{2,1,0:T(8,128)}, f32[8,4,2304]{2,1,0:T(4,128)}) custom-call(f32[8,1,256,256]{3,2,1,0:T(8,128)} %bitcast.119, f32[8,7,128,128]{3,2,1,0:T(8,128)} %bitcast.106, f32[4,2304]{1,0:T(4,128)} %pad_maximum_fusion.7.gains, ...), custom_call_target="tpu_custom_call" | custom-call | tf_op jit(solution)/shard_map/newton/pallas_call | solution.py:1906
  656.5 1.1 reduce_sum.49
  657.7 0.7 divide_subtract_fusion
  658.4 0.8 copy.51
  659.2 1.0 copy.52
  660.2 1.0 copy.53
  661.2 0.8 copy.54
  662.0 7.2 %copy.55 = f32[288,3,2304]{2,0,1:T(8,128)} copy(f32[288,3,2304]{2,0,1:T(8,128)} %bitcast.109) | data formatting | bytes 15925248
  669.2 1.0 copy.56
  670.2 0.8 copy.57
  (50 shorter events, 0.4 us)
Async XLA Ops:
  7.2 206.1 %all-gather.2.cloned.1.call-start = ((), (), s32[]{:S(2)}) async-start(), calls=%async_computation.2 | async-start | bytes 35831808 | tf_op jit(solution)/shard_map/all_gather | solution.py:1972
  32.2 0.7 copy-start.13
  32.2 446.9 %reduce-scatter.3.cloned.1.call-start = ((), (), s32[]{:S(2)}) async-start(), calls=%async_computation.3 | async-start | bytes 11943936 | tf_op jit(solution)/shard_map/reduce_scatter | solution.py:2054
  123.9 4.2 copy-start.17
  128.0 2.1 copy-start.19
  128.1 3.2 copy-start.15
  317.5 266.5 %reduce-scatter.5.cloned.1.call-start = ((), (), s32[]{:S(2)}) async-start(), calls=%async_computation.4 | async-start | bytes 23887872 | tf_op jit(solution)/shard_map/reduce_scatter | solution.py:2068
  422.5 4.2 copy-start.20
  426.4 1.6 copy-start.18
  463.9 2.5 copy-start.4
  463.9 2.5 copy-start.8
  466.3 1.7 copy-start.16
  468.0 2.9 copy-start.14
  468.0 7.2 %slice-start = ((s8[4718592]{0:T(1024)(128)(4,1)}), s8[4194304]{0:T(1024)(128)(4,1)S(1)}, s32[]{:S(2)}) async-start(s8[4718592]{0:T(1024)(128)(4,1)} %bitcast.147), calls=%async_computation.5 | async-start | bytes 8388608
  470.9 4.3 slice-start.1
  485.9 87.6 %copy-start.11 = (f32[2,2304]{1,0:T(2,128)S(1)}, f32[2,2304]{1,0:T(2,128)}, u32[]{:S(2)}) copy-start(f32[2,2304]{1,0:T(2,128)} %get-tuple-element.80) | copy-start | bytes 55300
  485.9 87.6 %copy-start.12 = (f32[1,2304]{1,0:T(1,128)S(1)}, f32[1,2304]{1,0:T(1,128)}, u32[]{:S(2)}) copy-start(f32[1,2304]{1,0:T(1,128)} %get-tuple-element.81) | copy-start | bytes 27652
  592.8 64.9 %copy-start = (f32[4,2304]{1,0:T(4,128)S(1)}, f32[4,2304]{1,0:T(4,128)}, u32[]{:S(2)}) copy-start(f32[4,2304]{1,0:T(4,128)} %gains.7) | copy-start | bytes 110596
  592.8 64.9 %copy-start.9 = (f32[4,2304]{1,0:T(4,128)S(1)}, f32[4,2304]{1,0:T(4,128)}, u32[]{:S(2)}) copy-start(f32[4,2304]{1,0:T(4,128)} %param.21) | copy-start | bytes 110596
  592.8 64.9 %copy-start.10 = (f32[4,2304]{1,0:T(4,128)S(1)}, f32[4,2304]{1,0:T(4,128)}, u32[]{:S(2)}) copy-start(f32[4,2304]{1,0:T(4,128)} %param.22) | copy-start | bytes 110596
  592.8 65.6 %copy-start.5 = (bf16[128,2304]{1,0:T(8,128)(2,1)S(1)}, bf16[128,2304]{1,0:T(8,128)(2,1)}, u32[]{:S(2)}) copy-start(bf16[128,2304]{1,0:T(8,128)(2,1)} %get-tuple-element.60) | copy-start | bytes 1769476
  592.8 66.4 %copy-start.2 = (f32[128,2304]{1,0:T(8,128)S(1)}, f32[128,2304]{1,0:T(8,128)}, u32[]{:S(2)}) copy-start(f32[128,2304]{1,0:T(8,128)} %get-tuple-element.73) | copy-start | bytes 3538948
  656.5 3.7 copy-start.3
  657.7 3.5 copy-start.7
  662.0 7.2 %copy-start.1 = (f32[288,4,256]{2,1,0:T(4,128)S(1)}, f32[288,4,256]{2,1,0:T(4,128)}, u32[]{:S(2)}) copy-start(f32[288,4,256]{2,1,0:T(4,128)} %get-tuple-element.137) | copy-start | bytes 3538948
  662.0 8.2 %copy-start.6 = (f32[288,2,256]{2,1,0:T(2,128)S(1)}, f32[288,2,256]{2,1,0:T(2,128)}, u32[]{:S(2)}) copy-start(f32[288,2,256]{2,1,0:T(2,128)} %get-tuple-element.138) | copy-start | bytes 1769476
Sparse Core Ops, SparseCore 0:
  32.3 180.8 all-gather.1
  317.7 80.4 reduce-scatter.2
  422.6 161.4 reduce-scatter.4

commit v2 on v1

--- a/solution.py
+++ b/solution.py
@@ -127,11 +127,13 @@
 
 
 def polys_of(grams):
-    size = grams[0].shape[0]
-    rows, columns = grid_of(size)
-    eye = (rows == columns).astype(FULL)
+    eyes = {}
+    for gram in grams:
+        rows, columns = grid_of(gram.shape[0])
+        eyes[gram.shape[0]] = (rows == columns).astype(FULL)
     factors, totals = [], [None] * len(grams)
     for index, gram in enumerate(grams):
+        eye = eyes[gram.shape[0]]
         trace = jnp.sum(jnp.sum(gram * eye, 0, keepdims=True), 1, keepdims=True)
         factors.append(1.0 / (jnp.sqrt(trace) + 1e-07))
         grams[index] = gram * (factors[index] * factors[index])
@@ -139,7 +141,7 @@
         parts = [split(gram) for gram in grams]
         squares = [fine_dot(part, part) for part in parts]
         quads = [
-            NEWTON_A * eye + NEWTON_B * gram + NEWTON_C * square
+            NEWTON_A * eyes[gram.shape[0]] + NEWTON_B * gram + NEWTON_C * square
             for gram, square in zip(grams, squares)
         ]
         quad_parts = [split(quad) for quad in quads]
@@ -999,21 +1001,57 @@
     )(part, *ins, gains)
 
 
+def spread(step, steps, work, body):
+    def one(index, carried):
+        body(index)
+        return carried
+
+    lax.fori_loop((step * work) // steps, ((step + 1) * work) // steps, one, 0)
+
+
+class Copies:
+    def __init__(self, copies):
+        self.copies = [pltpu.make_async_copy(*copy) for copy in copies]
+
+    def start(self):
+        for copy in self.copies:
+            copy.start()
+
+    def wait(self):
+        for copy in self.copies:
+            copy.wait()
+
+
 class Forward:
-    def __init__(self, mid, weights, hidden, gate_factor, up_factor, part, scratch):
-        self.weights, self.part = weights, part
-        self.outs = (hidden, gate_factor, up_factor)
-        self.mid, self.hidden, self.pair, self.down, self.pair_sem, self.down_sem = scratch
+    def __init__(self, mid, weights, results, part, scratch):
+        self.source, self.weights, self.results, self.part = mid, weights, results, part
+        self.mid, self.hidden, self.pair, self.down = scratch[:4]
+        self.pair_sem, self.down_sem, self.mid_sem, self.result_sem = scratch[4:8]
+        self.outs = scratch[8:]
         self.sequences, self.tokens, _ = mid.shape
         self.half = self.tokens // 2
         self.span, self.reach = self.pair.shape[3], self.down.shape[1]
         self.tiles = weights.shape[2] // self.span
         self.ends = weights.shape[1] // self.reach
         self.count = self.tiles + self.ends
+
+    def fetch_rows(self, half, s):
+        return pltpu.make_async_copy(
+            self.source.at[s, self.rows(half)],
+            self.mid.at[half, pl.ds(s * self.half, self.half)],
+            self.mid_sem.at[half, s],
+        )
+
+    def begin(self):
         for half in range(2):
-            for sequence in range(self.sequences):
-                rows = slice(sequence * self.half, (sequence + 1) * self.half)
-                self.mid[half, rows, :] = mid[sequence, half * self.half : (half + 1) * self.half, :]
+            for s in range(self.sequences):
+                self.fetch_rows(half, s).start()
+        self.fetch(0)
+
+    def give(self, index):
+        return pltpu.make_async_copy(
+            self.outs[index], self.results[index], self.result_sem.at[index]
+        )
 
     def fetch_pair(self, half, tile):
         slot = (half * self.tiles + tile) % 2
@@ -1049,6 +1087,11 @@
         @pl.when(index + 1 < 2 * self.count)
         def _():
             self.fetch(index + 1)
+
+        @pl.when(tile == 0)
+        def _():
+            for s in range(self.sequences):
+                self.fetch_rows(half, s).wait()
 
         @pl.when(tile < self.tiles)
         def _():
@@ -1089,11 +1132,12 @@
 
 
 def late_kernel(
-    size, mid, mixed, cotangent, gains, weights, late, out, gain, hidden, gate_factor, up_factor, *scratch
+    size, gains, mid, mixed_in, cotangent_in, weights,
+    late, out, gain, hidden, gate_factor, up_factor, *scratch
 ):
     at = lax.axis_index("fsdp")
     line_greet(at, size)
-    part = scratch[0]
+    part, line_parts, (mixed, cotangent, side_sem) = scratch[0], scratch[1:8], scratch[8:11]
     line = LineExchange(
         at,
         size,
@@ -1103,37 +1147,38 @@
         lambda chunk, rows, total: late_mid(
             chunk, rows, total, (mixed, cotangent), gains, (out, gain)
         ),
-        scratch[1:8],
-    )
-    forward = Forward(mid, weights, hidden, gate_factor, up_factor, part, scratch[8:])
-    forward.fetch(0)
+        line_parts,
+    )
+    forward = Forward(mid, weights, (hidden, gate_factor, up_factor), part, scratch[11:])
+    forward.begin()
+    sides = [
+        pltpu.make_async_copy(source, target, side_sem.at[index])
+        for index, (source, target) in enumerate(((mixed_in, mixed), (cotangent_in, cotangent)))
+    ]
+    for copy in sides:
+        copy.start()
 
     def one(index, carried):
         forward.run(index)
         return carried
 
     lax.fori_loop(0, forward.count, one, 0)
-    ahead = line.chunks // 2 - 1
-    share = -(-forward.count // ahead)
+    for copy in sides:
+        copy.wait()
+    ahead = line.chunks // 2
 
     def both(index, carried):
         line.step(index)
-
-        def more(inner, carried):
-            tile = forward.count + index * share + inner
-
-            @pl.when(tile < 2 * forward.count)
-            def _():
-                forward.run(tile)
-
-            return carried
-
-        lax.fori_loop(0, share, more, 0)
+        spread(index, ahead, forward.count, lambda tile: forward.run(forward.count + tile))
         return carried
 
     lax.fori_loop(0, ahead, both, 0)
+    for index in range(3):
+        forward.give(index).start()
     line.run(ahead, line.steps)
     line.drain()
+    for index in range(3):
+        forward.give(index).wait()
 
 
 def late_exchange(mid, weights, mixed, cotangent, gains, collective_id):
@@ -1145,8 +1190,8 @@
     low = jax.ShapeDtypeStruct((fsdp, tokens, units), LOW)
     return pl.pallas_call(
         functools.partial(late_kernel, fsdp),
-        in_specs=[VMEM_SPEC] * 4 + [ANY_SPEC],
-        out_specs=[VMEM_SPEC] * 6,
+        in_specs=[VMEM_SPEC] + [ANY_SPEC] * 4,
+        out_specs=[VMEM_SPEC] * 3 + [ANY_SPEC] * 3,
         out_shape=[
             jax.ShapeDtypeStruct(mid.shape, LOW),
             jax.ShapeDtypeStruct((tokens, width), LOW),
@@ -1158,26 +1203,34 @@
         scratch_shapes=[pltpu.VMEM(mid.shape, LOW)]
         + line_scratch(fsdp, tokens, width, True)
         + [
+            pltpu.VMEM((tokens, width), FULL),
+            pltpu.VMEM((tokens, width), LOW),
+            dma((2,)),
             pltpu.VMEM((2, rows, width), LOW),
             pltpu.VMEM((2, rows, units), LOW),
             pltpu.VMEM((2, 2, width, span), LOW),
             pltpu.VMEM((2, reach, units), LOW),
             dma((2,)),
             dma((2,)),
-        ],
+            dma((2, fsdp)),
+            dma((3,)),
+        ]
+        + [pltpu.VMEM((fsdp, tokens, units), LOW)] * 3,
         compiler_params=pltpu.CompilerParams(
             vmem_limit_bytes=VMEM_LIMIT, collective_id=collective_id
         ),
         name="late_exchange",
-    )(mid, mixed, cotangent, gains, weights)
+    )(gains, mid, mixed, cotangent, weights)
 
 
 class Backward:
-    def __init__(self, late, mid, weights, gate_factor, up_factor, part, grads, scratch):
-        self.weights, self.part, self.grads, self.mid = weights, part, grads, mid
-        self.factors = (gate_factor, up_factor)
-        self.late, self.turned, self.pairs, self.wide, self.tall, self.stage = scratch[:6]
-        self.wide_sem, self.tall_sem, self.stage_sem, self.mid_sem = scratch[6:]
+    def __init__(self, late, mid, weights, factors, part, grads, scratch):
+        self.weights, self.part, self.grads = weights, part, grads
+        self.late, self.mid, self.factors = late, mid, factors
+        self.rows_in, self.turned, self.pairs, self.wide, self.tall, self.stage = scratch[:6]
+        self.wide_sem, self.tall_sem, self.stage_sem, self.row_sem, self.factor_sem = scratch[6:11]
+        self.block, self.block_sem = scratch[11:13]
+        self.own_factors = scratch[13:]
         self.sequences, self.tokens, self.width = late.shape
         self.half = self.tokens // 2
         self.span, self.reach = self.wide.shape[2], self.tall.shape[2]
@@ -1186,36 +1239,64 @@
         self.ends = self.width // self.reach
         self.count = self.tiles + self.ends
         self.sums = 2 * self.units // self.stage.shape[2]
+        self.pieces = 2 * self.ends
+        self.work = self.sums * (self.width // 768)
+
+    def rows(self, half):
+        return pl.ds(pl.multiple_of(half * self.half, 16), self.half)
+
+    def fetch_rows(self, half, s):
+        return pltpu.make_async_copy(
+            self.late.at[s, self.rows(half)],
+            self.rows_in.at[half, pl.ds(s * self.half, self.half)],
+            self.row_sem.at[half, s],
+        )
+
+    def begin(self):
         for half in range(2):
-            for sequence in range(self.sequences):
-                rows = slice(sequence * self.half, (sequence + 1) * self.half)
-                self.late[half, rows, :] = late[sequence, half * self.half : (half + 1) * self.half, :]
-
-    def fetch_mid(self):
-        return [
-            pltpu.make_async_copy(
-                self.mid.at[s, pl.ds(half * self.half, self.half)],
-                self.late.at[half, pl.ds(s * self.half, self.half)],
-                self.mid_sem.at[half * self.sequences + s],
+            for s in range(self.sequences):
+                self.fetch_rows(half, s).start()
+        self.fetch(0)
+        self.fetch_block(0).start()
+
+    def fetch_block(self, piece):
+        half, block = piece // self.ends, piece % self.ends
+        span = pl.ds(pl.multiple_of(block * self.reach, self.reach), self.reach)
+        return Copies(
+            (
+                self.mid.at[s, self.rows(half), span],
+                self.block.at[piece % 2, pl.ds(s * self.half, self.half)],
+                self.block_sem.at[piece % 2, s],
             )
-            for half in range(2)
             for s in range(self.sequences)
-        ]
-
-    def turn(self):
+        )
+
+    def turn(self, piece):
+        @pl.when(piece + 1 < self.pieces)
+        def _():
+            self.fetch_block(piece + 1).start()
+
+        self.fetch_block(piece).wait()
         rows = self.sequences * self.half
-        for copy in self.fetch_mid():
-            copy.wait()
-        for half in range(2):
-            for first in range(0, self.width, self.reach):
-                block = self.late[half, :, first : first + self.reach]
-                self.turned[first : first + self.reach, half * rows : (half + 1) * rows] = block.T
+        half, block = piece // self.ends, piece % self.ends
+        span = pl.ds(pl.multiple_of(block * self.reach, self.reach), self.reach)
+        columns = pl.ds(pl.multiple_of(half * rows, 128), rows)
+        self.turned[span, columns] = self.block[piece % 2].T
 
     def fetch_wide(self, half, tile):
         slot = (half * self.tiles + tile) % 2
         columns = pl.ds(pl.multiple_of(tile * self.span, self.span), self.span)
-        return pltpu.make_async_copy(
-            self.weights.at[2, :, columns], self.wide.at[slot], self.wide_sem.at[slot]
+        rows = self.rows(half)
+        return Copies(
+            [(self.weights.at[2, :, columns], self.wide.at[slot], self.wide_sem.at[slot])]
+            + [
+                (
+                    self.factors[side].at[:, rows, columns],
+                    self.own_factors[side].at[:, rows, columns],
+                    self.factor_sem.at[slot, side],
+                )
+                for side in range(2)
+            ]
         )
 
     def fetch_tall(self, half, tile):
@@ -1238,19 +1319,24 @@
 
     def run(self, index):
         half, tile = index // self.count, index % self.count
-        rows = pl.ds(pl.multiple_of(half * self.half, 16), self.half)
+        rows = self.rows(half)
 
         @pl.when(index + 1 < 2 * self.count)
         def _():
             self.fetch(index + 1)
+
+        @pl.when(tile == 0)
+        def _():
+            for s in range(self.sequences):
+                self.fetch_rows(half, s).wait()
 
         @pl.when(tile < self.tiles)
         def _():
             self.fetch_wide(half, tile).wait()
             slot = (half * self.tiles + tile) % 2
-            hidden_grad = dot(self.late[half], self.wide[slot], 1, 0)
+            hidden_grad = dot(self.rows_in[half], self.wide[slot], 1, 0)
             columns = pl.ds(pl.multiple_of(tile * self.span, self.span), self.span)
-            for side, factor in enumerate(self.factors):
+            for side, factor in enumerate(self.own_factors):
                 target = pl.ds(
                     pl.multiple_of(side * self.units + tile * self.span, self.span), self.span
                 )
@@ -1278,29 +1364,35 @@
             self.stage.at[index % 2], self.grads.at[:, columns], self.stage_sem.at[index % 2]
         )
 
-    def sum(self, index):
-        @pl.when(index >= 2)
+    def sum(self, unit):
+        thirds = self.width // 768
+        index, third = unit // thirds, unit % thirds
+
+        @pl.when((third == 0) & (index >= 2))
         def _():
             self.put(index - 2).wait()
 
         span = self.stage.shape[2]
         columns = pl.ds(pl.multiple_of(index * span, span), span)
         rows = self.sequences * self.half
-        for first in range(0, self.width, 768):
-            own = slice(first, first + 768)
-            value = dot(self.turned[own, :rows], self.pairs[0, :, columns], 1, 0)
-            value = value + dot(self.turned[own, rows:], self.pairs[1, :, columns], 1, 0)
-            self.stage[index % 2, own, :] = value.astype(LOW)
-        self.put(index).start()
+        own = pl.ds(pl.multiple_of(third * 768, 768), 768)
+        value = dot(self.turned[own, :rows], self.pairs[0, :, columns], 1, 0)
+        value = value + dot(self.turned[own, rows:], self.pairs[1, :, columns], 1, 0)
+        self.stage[index % 2, own, :] = value.astype(LOW)
+
+        @pl.when(third == thirds - 1)
+        def _():
+            self.put(index).start()
 
 
 def mid_kernel(
-    size, late, mixed, branch, cotangent, gains, gate_factor, up_factor, mid, weights,
+    size, gains, late, mixed_in, branch_in, cotangent_in, gate_factor, up_factor, mid, weights,
     low, mixed_grad, gain, grads, *scratch
 ):
     at = lax.axis_index("fsdp")
     line_greet(at, size)
-    part = scratch[0]
+    part, line_parts, sides = scratch[0], scratch[1:8], scratch[8:11]
+    side_sem = scratch[11]
     line = LineExchange(
         at,
         size,
@@ -1308,59 +1400,44 @@
         part,
         low,
         lambda chunk, rows, total: mid_mid(
-            chunk, rows, total, (mixed, branch, cotangent), gains, (mixed_grad, gain)
+            chunk, rows, total, sides, gains, (mixed_grad, gain)
         ),
-        scratch[1:8],
-    )
-    backward = Backward(late, mid, weights, gate_factor, up_factor, part, grads, scratch[8:])
-    backward.fetch(0)
+        line_parts,
+    )
+    backward = Backward(late, mid, weights, (gate_factor, up_factor), part, grads, scratch[12:])
+    backward.begin()
+    copies = [
+        pltpu.make_async_copy(source, target, side_sem.at[index])
+        for index, (source, target) in enumerate(zip((mixed_in, branch_in, cotangent_in), sides))
+    ]
+    for copy in copies:
+        copy.start()
 
     def one(index, carried):
         backward.run(index)
+        spread(index, backward.count, backward.pieces, backward.turn)
         return carried
 
     lax.fori_loop(0, backward.count, one, 0)
-    ahead = line.chunks // 2 - 1
-    share = -(-backward.count // ahead)
+    for copy in copies:
+        copy.wait()
+    ahead = line.chunks // 2
 
     def both(index, carried):
         line.step(index)
-
-        def more(inner, carried):
-            tile = backward.count + index * share + inner
-
-            @pl.when(tile < 2 * backward.count)
-            def _():
-                backward.run(tile)
-
-            return carried
-
-        lax.fori_loop(0, share, more, 0)
+        spread(index, ahead, backward.count, lambda tile: backward.run(backward.count + tile))
         return carried
 
     lax.fori_loop(0, ahead, both, 0)
-    for copy in backward.fetch_mid():
-        copy.start()
-    line.run(ahead, ahead + 1)
-    backward.turn()
-    portion = -(-backward.sums // (line.steps - ahead - 1))
-
-    def rest(index, carried):
-        line.step(index)
-
-        def more(inner, carried):
-            tile = (index - ahead - 1) * portion + inner
-
-            @pl.when(tile < backward.sums)
-            def _():
-                backward.sum(tile)
-
-            return carried
-
-        lax.fori_loop(0, portion, more, 0)
+    busy = 6
+
+    def more(index, carried):
+        line.step(ahead + index)
+        spread(index, busy, backward.work, backward.sum)
         return carried
 
-    lax.fori_loop(ahead + 1, line.steps, rest, 0)
+    lax.fori_loop(0, busy, more, 0)
+    line.run(ahead + busy, line.steps)
     line.drain()
     backward.put(backward.sums - 2).wait()
     backward.put(backward.sums - 1).wait()
@@ -1376,7 +1453,7 @@
     dma = pltpu.SemaphoreType.DMA
     return pl.pallas_call(
         functools.partial(mid_kernel, fsdp),
-        in_specs=[VMEM_SPEC] * 7 + [ANY_SPEC] * 2,
+        in_specs=[VMEM_SPEC] + [ANY_SPEC] * 8,
         out_specs=[VMEM_SPEC] * 3 + [ANY_SPEC],
         out_shape=[
             jax.ShapeDtypeStruct(mid.shape, LOW),
@@ -1387,6 +1464,10 @@
         scratch_shapes=[pltpu.VMEM(mid.shape, LOW)]
         + line_scratch(fsdp, tokens, width, True)
         + [
+            pltpu.VMEM((tokens, width), FULL),
+            pltpu.VMEM((tokens, width), FULL),
+            pltpu.VMEM((tokens, width), LOW),
+            dma((3,)),
             pltpu.VMEM((2, rows, width), LOW),
             pltpu.VMEM((width, 2 * rows), LOW),
             pltpu.VMEM((2, rows, 2 * units), LOW),
@@ -1396,13 +1477,17 @@
             dma((2,)),
             dma((2,)),
             dma((2,)),
-            dma((2 * fsdp,)),
-        ],
+            dma((2, fsdp)),
+            dma((2, 2)),
+            pltpu.VMEM((2, rows, reach), LOW),
+            dma((2, fsdp)),
+        ]
+        + [pltpu.VMEM((fsdp, tokens, units), LOW)] * 2,
         compiler_params=pltpu.CompilerParams(
             vmem_limit_bytes=VMEM_LIMIT, collective_id=collective_id
         ),
         name="mid_exchange",
-    )(late, mixed, branch, cotangent, gains, gate_factor, up_factor, mid, weights)
+    )(gains, late, mixed, branch, cotangent, gate_factor, up_factor, mid, weights)
 
 
 def row_sum(values):
@@ -1510,7 +1595,7 @@
 
 
 def tail_kernel(
-    ctx, fsdp, in_part, out_part, pre_part, x, mixed_grad, gains, in_old, out_old, after, *refs
+    ctx, fsdp, in_part, out_part, pre_part, x, mixed_grad, gains, in_old, out_old, *refs
 ):
     at, line_at = lax.axis_index("ctx"), lax.axis_index("fsdp")
     in_new, out_new, update, gram, input_grad, gain = refs[:6]
@@ -1631,7 +1716,7 @@
     line.drain()
 
 
-def tail(in_part, out_part, pre_part, x, mixed_grad, gains, in_old, out_old, after):
+def tail(in_part, out_part, pre_part, x, mixed_grad, gains, in_old, out_old):
     _, stored, head = in_old.shape
     matrices = stored + out_old.shape[1]
     ctx, rows, in_width = in_part.shape
@@ -1642,7 +1727,7 @@
     dma = pltpu.SemaphoreType.DMA
     return pl.pallas_call(
         functools.partial(tail_kernel, ctx, fsdp),
-        in_specs=[VMEM_SPEC] * 8 + [ANY_SPEC],
+        in_specs=[VMEM_SPEC] * 8,
         out_specs=[VMEM_SPEC] * 6,
         out_shape=[
             jax.ShapeDtypeStruct(in_old.shape, FULL),
@@ -1664,7 +1749,7 @@
         + line_scratch(fsdp, tokens, width, False),
         compiler_params=pltpu.CompilerParams(vmem_limit_bytes=VMEM_LIMIT, collective_id=3),
         name="tail",
-    )(in_part, out_part, pre_part, x, mixed_grad, gains, in_old, out_old, after)
+    )(in_part, out_part, pre_part, x, mixed_grad, gains, in_old, out_old)
 
 
 def packed_rows(small, large):
@@ -1808,7 +1893,8 @@
     block_grams, head_grams = unpack_all(
         small, large, lambda first, count: gram[first : first + count, :]
     )
-    head_polys, block_polys = polys_of(head_grams), polys_of(block_grams)
+    polys = polys_of(head_grams + block_grams)
+    head_polys, block_polys = polys[:large], polys[large:]
     poly[edge:, :] = jnp.zeros((poly.shape[0] - edge, FBLK), FULL)
 
     def write(first, rows):
@@ -2103,7 +2189,6 @@
         norm_gains,
         momentum_in,
         momentum_out,
-        earlier[2][-1, :8],
     )
     input_grad = input_grad.reshape(inputs.shape)
     outputs = outputs.reshape(inputs.shape)

time: 688 us -> 678 us (0.985)
  Pallas kernels: 579 us -> 567 us
    pallas_call x1, Pallas kernels: 105 us -> 97.4 us  [mid_exchange(): pl.pallas_call(functools.partial(mid_kernel, fsdp), in_specs=[VMEM_SPEC]...]
where the time goes in v2:
time: 678 us; the launch traced here: 669 us
  Pallas kernels  567 us (84%)
  matrix products  44.5 us (7%)
  local copies, waits for them, and re-layouts  18.8 us (3%)
  waiting for transfers between devices  17.6 us (3%)
  between operations  14.6 us (2%)
    pallas_call x1, Pallas kernels, mid_exchange(): pl.pallas_call(functools.partial(mid_kernel, fsdp), in_specs=[VMEM_SPEC]...  97.4 us
    pallas_call x1, Pallas kernels, late_exchange(): pl.pallas_call(functools.partial(late_kernel, fsdp), in_specs=[VMEM_SPEC]...  90.4 us
    pallas_call x1, Pallas kernels, project(): pl.pallas_call(functools.partial(project_kernel, ctx, fsdp, tokens // chu...  88.4 us
    pallas_call x1, Pallas kernels, tail(): pl.pallas_call(functools.partial(tail_kernel, ctx, fsdp), in_specs=[VMEM_...  87.6 us
    pallas_call x1, Pallas kernels, exchange(): pl.pallas_call(functools.partial(exchange_kernel, mid, fsdp, len(ins)), i...  75.1 us
    pallas_call x1, Pallas kernels, newton(): pl.pallas_call(functools.partial(newton_kernel, ctx, fsdp, head_rate, ffn...  62.2 us
    dot_general x6, matrix products, dot(): lax.dot_general(left, right, (((left_dim,), (right_dim,)), ((), ())), pre...  28.2 us
    pallas_call x1, Pallas kernels, scatter_pairs(): pl.pallas_call(functools.partial(pair_sums_kernel, ctx), in_specs=[VMEM_S...  26.6 us
  transfers between devices with their start and end apart: 3, of which 2 were waited for; matrix products, arithmetic and copies ran while one was open for 6% of the time, Pallas kernels for 57%

profile of v2, /device:TPU:0, one launch (start us, length us, event | category | flops | bytes accessed | tf_op | source)
XLA Modules:
  0.0 668.6 jit_solution(9142378080916690605)
XLA Ops:
  7.2 0.0 all-gather.2.cloned.1.call-start
  7.2 25.0 %prepare.1 = (bf16[288,1024]{1,0:T(8,128)(2,1)}, bf16[8,288,512]{2,1,0:T(8,128)(2,1)}, bf16[3,288,2304]{2,1,0:T(8,128)(2,1)}, bf16[128,2304]{1,0:T(8,128)(2,1)}) custom-call(f32[288,4,256]{2,1,0:T(4,128)} %in_old.3, f32[288,2,256]{2,1,0:T(2,128)} %out_old.3, f32[3,288,2304]{2,1,0:T(8,128)} %bitcast.102, bf16[128,2304]{1,0:T(8,128)(2,1)} %bitcast.108, ...), custom_call_target="tpu_custom_call" | custom-call | tf_op jit(solution)/shard_map/prepare/pallas_call | solution.py:708
  32.2 0.0 copy-start.13
  32.2 0.0 all-gather.2.cloned.1.call-update
  32.2 0.0 reduce-scatter.5.cloned.1.call-start
  32.3 0.5 copy-done.13
  32.8 0.1 select_reduce_fusion.1
  32.9 1.0 fusion.16
  33.9 88.4 %project.1 = (bf16[4,128,2304]{2,1,0:T(8,128)(2,1)}, bf16[2304,1024]{1,0:T(8,128)(2,1)}, bf16[512,512]{1,0:T(8,128)(2,1)}, bf16[4,8,128,256]{3,2,1,0:T(8,128)(2,1)}, bf16[4,8,128,256]{3,2,1,0:T(8,128)(2,1)}) custom-call(bf16[128,2304]{1,0:T(8,128)(2,1)} %get-tuple-element.51.own, bf16[288,1024]{1,0:T(8,128)(2,1)} %get-tuple-element.52.mine, ...), custom_call_target="tpu_custom_call" | custom-call | tf_op jit(solution)/shard_map/project/pallas_call | solution.py:824
  122.3 0.1 select_reduce_fusion
  122.4 0.1 broadcast_compare_fusion
  122.6 1.2 fusion.37
  123.8 0.1 tile.10
  123.9 4.2 fusion
  128.0 0.0 copy-start.19
  128.1 1.6 fusion.38
  129.7 0.5 copy-done.19
  130.2 1.0 copy-done.15
  131.2 2.8 convolution_convert_fusion.3
  134.1 75.1 %branch_exchange.1 = (bf16[4,128,2304]{2,1,0:T(8,128)(2,1)}, f32[128,2304]{1,0:T(8,128)}, f32[128,2304]{1,0:T(8,128)}) custom-call(bf16[4,128,2304]{2,1,0:T(8,128)(2,1)} %bitcast.112, bf16[128,2304]{1,0:T(8,128)(2,1)} %bitcast.109, f32[4,2304]{1,0:T(4,128)} %gains.7), custom_call_target="tpu_custom_call" | custom-call | tf_op jit(solution)/shard_map/branch_exchange/pallas_call | solution.py:991
  209.2 4.1 all-gather.2.cloned.1.call-done.weights
  213.3 90.4 %late_exchange.1 = (bf16[4,128,2304]{2,1,0:T(8,128)(2,1)}, bf16[128,2304]{1,0:T(8,128)(2,1)}, f32[1,2304]{1,0:T(1,128)}, bf16[4,128,2304]{2,1,0:T(8,128)(2,1)}, ...) custom-call(f32[4,2304]{1,0:T(4,128)} %gains.7, bf16[4,128,2304]{2,1,0:T(8,128)(2,1)} %get-tuple-element.57.mid, ...), custom_call_target="tpu_custom_call" | custom-call | tf_op jit(solution)/shard_map/late_exchange/pallas_call | solution.py:1191
  303.6 10.4 %bitcast_convert_fusion = bf16[2304,2304]{1,0:T(8,128)(2,1)} fusion(bf16[4,128,2304]{2,1,0:T(8,128)(2,1)} %get-tuple-element.62.late, bf16[4,128,2304]{2,1,0:T(8,128)(2,1)} %get-tuple-element.74), kind=kOutput, calls=%fused_computation | convolution fusion | flops 5441126400 | bytes 15335424 | tf_op jit(solution)/shard_map/dot_general | solution.py:71
  314.0 0.0 reduce-scatter.5.cloned.1.call-update
  314.0 0.0 reduce-scatter.3.cloned.1.call-start
  314.1 97.4 %mid_exchange.1 = (bf16[4,128,2304]{2,1,0:T(8,128)(2,1)}, f32[128,2304]{1,0:T(8,128)}, f32[2,2304]{1,0:T(2,128)}, bf16[2304,4608]{1,0:T(8,128)(2,1)}) custom-call(f32[4,2304]{1,0:T(4,128)} %gains.7, bf16[4,128,2304]{2,1,0:T(8,128)(2,1)} %get-tuple-element.62.late, f32[128,2304]{1,0:T(8,128)} %get-tuple-element.58.mixed_in, ...), custom_call_target="tpu_custom_call" | custom-call | tf_op jit(solution)/shard_map/mid_exchange/pallas_call | solution.py:1454
  411.5 0.0 reduce-scatter.3.cloned.1.call-update
  411.5 0.0 copy-start.20
  411.5 3.9 fusion.39
  415.4 0.1 fusion.35
  415.5 0.2 multiply_reduce_fusion
  415.8 1.3 copy-done.18
  417.1 2.7 multiply_convert_fusion
  419.8 2.3 convolution_convert_fusion.5
  422.1 3.2 convolution_convert_fusion.4
  425.3 26.6 %scatter_pairs.1 = (f32[4,128,256]{2,1,0:T(8,128)}, f32[4,128,256]{2,1,0:T(8,128)}) custom-call(bf16[4,8,128,256]{3,2,1,0:T(8,128)(2,1)} %bitcast.105, bf16[4,8,128,256]{3,2,1,0:T(8,128)(2,1)} %bitcast.120), custom_call_target="tpu_custom_call" | custom-call | tf_op jit(solution)/shard_map/scatter_pairs/pallas_call | solution.py:1586
  452.0 0.0 copy-start.4
  452.0 1.1 convert.28
  453.1 2.3 fusion.40
  455.5 0.1 slice_multiply_fusion
  455.6 0.2 fusion.14
  456.1 1.0 copy-done.16
  457.1 2.8 convolution_convert_fusion.2
  460.0 0.0 copy-done.14
  460.0 4.3 convolution_convert_fusion
  464.3 3.9 convolution_convert_fusion.1
  468.2 87.6 %tail.1 = (f32[288,4,256]{2,1,0:T(4,128)}, f32[288,2,256]{2,1,0:T(2,128)}, bf16[6,288,256]{2,1,0:T(8,128)(2,1)}, f32[8,256,256]{2,1,0:T(8,128)}, f32[128,2304]{1,0:T(8,128)}, /*index=5*/f32[1,2304]{1,0:T(1,128)}) custom-call(bf16[8,288,1024]{2,1,0:T(8,128)(2,1)} %bitcast.111, bf16[8,288,512]{2,1,0:T(8,128)(2,1)} %bitcast.113, ...), custom_call_target="tpu_custom_call" | custom-call | tf_op jit(solution)/shard_map/tail/pallas_call | solution.py:1728
  555.9 0.0 copy-done.11
  555.9 0.0 copy-done.12
  555.9 1.3 pad_maximum_fusion.7.gains
  557.2 5.5 ffn_gram.2
  562.7 13.5 %reduce-scatter.3.cloned.1.call-done.grad_ref = bf16[288,4608]{1,0:T(8,128)(2,1)} async-done(((bf16[2304,4608]{1,0:T(8,128)(2,1)}), bf16[288,4608]{1,0:T(8,128)(2,1)}) %reduce-scatter.3.cloned.1.call-update) | async-done | bytes 2654224 | tf_op jit(solution)/shard_map/reduce_scatter | solution.py:2154
  576.2 8.7 %ffn_gram.3 = (f32[3,288,2304]{2,1,0:T(8,128)}, bf16[3,288,2304]{2,1,0:T(8,128)(2,1)}, f32[56,128,128]{2,1,0:T(8,128)}) custom-call(bf16[288,4608]{1,0:T(8,128)(2,1)} %reduce-scatter.3.cloned.1.call-done.grad_ref, f32[3,288,2304]{2,1,0:T(8,128)} %bitcast.101, ...), custom_call_target="tpu_custom_call", output_to_operand_aliasing={{0}: (2, {}), {1}: (3, {}), {2}: (4, {})} | custom-call | tf_op jit(solution)/shard_map/ffn_gram/pallas_call | solution.py:94
  584.9 62.2 %newton.1 = (f32[288,4,256]{2,1,0:T(4,128)}, f32[288,2,256]{2,1,0:T(2,128)}, f32[3,288,2304]{2,1,0:T(8,128)}, f32[8,4,2304]{2,1,0:T(4,128)}) custom-call(f32[8,1,256,256]{3,2,1,0:T(8,128)} %bitcast.117, f32[8,7,128,128]{3,2,1,0:T(8,128)} %bitcast.104, f32[4,2304]{1,0:T(4,128)} %pad_maximum_fusion.7.gains, ...), custom_call_target="tpu_custom_call" | custom-call | tf_op jit(solution)/shard_map/newton/pallas_call | solution.py:1992
  647.1 1.1 reduce_sum.49
  648.3 0.7 divide_subtract_fusion
  649.0 0.8 copy.51
  649.8 1.0 copy.52
  650.8 1.0 copy.53
  651.8 0.0 copy-done.7
  651.8 0.8 copy.54
  652.7 7.2 %copy.55 = f32[288,3,2304]{2,0,1:T(8,128)} copy(f32[288,3,2304]{2,0,1:T(8,128)} %bitcast.106) | data formatting | bytes 15925248
  659.8 1.0 copy.56
  660.8 0.8 copy.57
  (49 shorter events, 0.4 us)
Async XLA Ops:
  7.2 206.1 %all-gather.2.cloned.1.call-start = ((), (), s32[]{:S(2)}) async-start(), calls=%async_computation.2 | async-start | bytes 35831808 | tf_op jit(solution)/shard_map/all_gather | solution.py:2058
  32.2 0.7 copy-start.13
  32.2 525.0 %reduce-scatter.5.cloned.1.call-start = ((), (), s32[]{:S(2)}) async-start(), calls=%async_computation.4 | async-start | bytes 11943936 | tf_op jit(solution)/shard_map/reduce_scatter | solution.py:2140
  123.9 4.2 copy-start.17
  128.0 2.1 copy-start.19
  128.1 3.2 copy-start.15
  314.0 262.1 %reduce-scatter.3.cloned.1.call-start = ((), (), s32[]{:S(2)}) async-start(), calls=%async_computation.3 | async-start | bytes 23887872 | tf_op jit(solution)/shard_map/reduce_scatter | solution.py:2154
  411.5 4.2 copy-start.20
  415.4 1.6 copy-start.18
  452.0 3.6 copy-start.4
  452.0 3.6 copy-start.8
  455.4 1.7 copy-start.16
  457.1 2.9 copy-start.14
  457.1 7.2 %slice-start = ((s8[4718592]{0:T(1024)(128)(4,1)}), s8[4194304]{0:T(1024)(128)(4,1)S(1)}, s32[]{:S(2)}) async-start(s8[4718592]{0:T(1024)(128)(4,1)} %bitcast.145), calls=%async_computation.5 | async-start | bytes 8388608
  460.0 4.3 slice-start.1
  468.2 87.7 %copy-start.11 = (f32[2,2304]{1,0:T(2,128)S(1)}, f32[2,2304]{1,0:T(2,128)}, u32[]{:S(2)}) copy-start(f32[2,2304]{1,0:T(2,128)} %get-tuple-element.80) | copy-start | bytes 55300
  468.2 87.7 %copy-start.12 = (f32[1,2304]{1,0:T(1,128)S(1)}, f32[1,2304]{1,0:T(1,128)}, u32[]{:S(2)}) copy-start(f32[1,2304]{1,0:T(1,128)} %get-tuple-element.81) | copy-start | bytes 27652
  584.9 63.4 %copy-start = (f32[4,2304]{1,0:T(4,128)S(1)}, f32[4,2304]{1,0:T(4,128)}, u32[]{:S(2)}) copy-start(f32[4,2304]{1,0:T(4,128)} %gains.7) | copy-start | bytes 110596
  584.9 63.4 %copy-start.9 = (f32[4,2304]{1,0:T(4,128)S(1)}, f32[4,2304]{1,0:T(4,128)}, u32[]{:S(2)}) copy-start(f32[4,2304]{1,0:T(4,128)} %param.21) | copy-start | bytes 110596
  584.9 63.4 %copy-start.10 = (f32[4,2304]{1,0:T(4,128)S(1)}, f32[4,2304]{1,0:T(4,128)}, u32[]{:S(2)}) copy-start(f32[4,2304]{1,0:T(4,128)} %param.22) | copy-start | bytes 110596
  584.9 64.1 %copy-start.5 = (bf16[128,2304]{1,0:T(8,128)(2,1)S(1)}, bf16[128,2304]{1,0:T(8,128)(2,1)}, u32[]{:S(2)}) copy-start(bf16[128,2304]{1,0:T(8,128)(2,1)} %get-tuple-element.60) | copy-start | bytes 1769476
  584.9 64.9 %copy-start.2 = (f32[128,2304]{1,0:T(8,128)S(1)}, f32[128,2304]{1,0:T(8,128)}, u32[]{:S(2)}) copy-start(f32[128,2304]{1,0:T(8,128)} %get-tuple-element.71) | copy-start | bytes 3538948
  647.1 3.7 copy-start.3
  648.3 3.5 copy-start.7
  652.7 7.2 %copy-start.1 = (f32[288,4,256]{2,1,0:T(4,128)S(1)}, f32[288,4,256]{2,1,0:T(4,128)}, u32[]{:S(2)}) copy-start(f32[288,4,256]{2,1,0:T(4,128)} %get-tuple-element.137) | copy-start | bytes 3538948
  652.7 8.2 %copy-start.6 = (f32[288,2,256]{2,1,0:T(2,128)S(1)}, f32[288,2,256]{2,1,0:T(2,128)}, u32[]{:S(2)}) copy-start(f32[288,2,256]{2,1,0:T(2,128)} %get-tuple-element.138) | copy-start | bytes 1769476
Sparse Core Ops, SparseCore 0:
  32.3 180.8 all-gather.1
  314.1 80.3 reduce-scatter.4
  411.6 164.4 reduce-scatter.2

commit v3 on v2

--- a/solution.py
+++ b/solution.py
@@ -1598,12 +1598,13 @@
     ctx, fsdp, in_part, out_part, pre_part, x, mixed_grad, gains, in_old, out_old, *refs
 ):
     at, line_at = lax.axis_index("ctx"), lax.axis_index("fsdp")
-    in_new, out_new, update, gram, input_grad, gain = refs[:6]
+    in_new, out_new, update, head_sum, input_grad, gain = refs[:6]
     scratch = refs[6:]
     places = head_places(fsdp)
     mine = len(places[0])
     scratch, others = scratch[: 2 * SCATTER], scratch[2 * SCATTER :]
     mine_sum, arrived, move_send, move_receive, out_sum = others[:5]
+    gram, packed = others[10:12]
     head = arrived.shape[-1]
     greet(ctx_peers(at, ctx) + [("fsdp", (line_at + k) % fsdp) for k in range(1, fsdp)])
     ins = ctx_scatter(at, ctx, rows_of_ctx(in_part), scratch)
@@ -1703,6 +1704,30 @@
             paired = line_at * stored + index >= QUERY_HEADS
             grad = grad + jnp.where(paired, more, 0.0)
         step_of(index, grad, in_old, in_new, index)
+    large = gram.shape[0] // ctx
+    edge = large * 2 * FBLK
+
+    def pack_for(index, carried):
+        packed[index, edge:, :] = jnp.zeros((packed.shape[1] - edge, FBLK), FULL)
+
+        def write(first, rows):
+            packed[index, first : first + rows.shape[0], :] = rows
+
+        pack_all((0, None), (large, lambda i: gram[index * large + i]), write)
+        return carried
+
+    lax.fori_loop(0, ctx, pack_for, 0)
+    heads = ctx_scatter(at, ctx, rows_of_ctx(packed), others[12:])
+    heads.start()
+    heads.diagonal()
+    heads.neighbours()
+    heads.passing()
+
+    def store_head(block, rows, total):
+        head_sum[rows, :] = total
+
+    heads.finish(store_head)
+    heads.drain()
     for user in range(fsdp):
         for slot in range(mine):
             if places[user][slot][0] != user:
@@ -1719,6 +1744,7 @@
 def tail(in_part, out_part, pre_part, x, mixed_grad, gains, in_old, out_old):
     _, stored, head = in_old.shape
     matrices = stored + out_old.shape[1]
+    large = -(-matrices // in_part.shape[0])
     ctx, rows, in_width = in_part.shape
     out_width = out_part.shape[2]
     fsdp, tokens, width = pre_part.shape
@@ -1733,7 +1759,7 @@
             jax.ShapeDtypeStruct(in_old.shape, FULL),
             jax.ShapeDtypeStruct(out_old.shape, FULL),
             jax.ShapeDtypeStruct((matrices, rows, head), LOW),
-            jax.ShapeDtypeStruct((ctx * (-(-matrices // ctx)), head, head), FULL),
+            jax.ShapeDtypeStruct((packed_rows(0, large), FBLK), FULL),
             jax.ShapeDtypeStruct((tokens, width), FULL),
             jax.ShapeDtypeStruct((1, width), FULL),
         ],
@@ -1746,7 +1772,12 @@
             dma((stored, copies)),
             pltpu.VMEM((rows, out_width), FULL),
         ]
-        + line_scratch(fsdp, tokens, width, False),
+        + line_scratch(fsdp, tokens, width, False)
+        + [
+            pltpu.VMEM((ctx * large, head, head), FULL),
+            pltpu.VMEM((ctx, packed_rows(0, large), FBLK), FULL),
+        ]
+        + ctx_scatter_scratch(ctx, 1, packed_rows(0, large), FBLK, FULL),
         compiler_params=pltpu.CompilerParams(vmem_limit_bytes=VMEM_LIMIT, collective_id=3),
         name="tail",
     )(in_part, out_part, pre_part, x, mixed_grad, gains, in_old, out_old)
@@ -1823,14 +1854,21 @@
 
 
 def newton_kernel(
-    ctx, fsdp, head_rate, ffn_rate, heads, blocks, gains, head_update, in_old, out_old, ffn_update,
-    ffn_old, in_new, out_new, ffn_new, gains_all, *scratch
+    ctx, fsdp, large, head_rate, ffn_rate, heads, blocks, gains, head_update_in, in_old_in, out_old_in,
+    ffn_update, ffn_old, in_new, out_new, ffn_new, gains_all, *scratch
 ):
     at, line_at = lax.axis_index("ctx"), lax.axis_index("fsdp")
-    small, large = blocks.shape[1], heads.shape[1]
+    small = blocks.shape[1]
     packed, gram, poly, poly_all, gains_line, gains_sum, gain_send, gain_receive = scratch[:8]
     update, weights, update_sem, weight_sem, out_sem = scratch[8:13]
-    scratch = scratch[13:]
+    head_update, in_old, out_old, side_sem = scratch[13:17]
+    scratch = scratch[17:]
+    sides = [
+        pltpu.make_async_copy(source, target, side_sem.at[index])
+        for index, (source, target) in enumerate(
+            ((head_update_in, head_update), (in_old_in, in_old), (out_old_in, out_old))
+        )
+    ]
     matrices, _, width = weights.shape
     per_matrix = width // FBLK
     count = matrices * per_matrix
@@ -1856,7 +1894,7 @@
 
     for k in range(1, fsdp):
         gain_copy(k).start()
-    edge = packed_rows(small, large) - 16 * (-(-(-(-small // 2) + large) // 16))
+    edge = -(-small // 2) * FBLK
 
     def pack_for(index, carried):
         packed[index, edge:, :] = jnp.zeros((packed.shape[1] - edge, FBLK), FULL)
@@ -1864,7 +1902,7 @@
         def write(first, rows):
             packed[index, first : first + rows.shape[0], :] = rows
 
-        pack_all((small, lambda i: blocks[index, i]), (large, lambda i: heads[index, i]), write)
+        pack_all((small, lambda i: blocks[index, i]), (0, None), write)
         return carried
 
     lax.fori_loop(0, ctx, pack_for, 0)
@@ -1873,8 +1911,12 @@
     for matrix in range(matrices):
         for copy in fetches(matrix):
             copy.start()
+    for copy in sides:
+        copy.start()
     scatter.diagonal()
     scatter.neighbours()
+    _, head_grams = unpack_all(0, large, lambda first, count: heads[first : first + count, :])
+    head_polys = polys_of(head_grams)
     scatter.passing()
     total = gains[...]
     for k in range(1, fsdp):
@@ -1890,12 +1932,10 @@
 
     scatter.finish(store)
     gather_gains.start()
-    block_grams, head_grams = unpack_all(
-        small, large, lambda first, count: gram[first : first + count, :]
-    )
-    polys = polys_of(head_grams + block_grams)
-    head_polys, block_polys = polys[:large], polys[large:]
-    poly[edge:, :] = jnp.zeros((poly.shape[0] - edge, FBLK), FULL)
+    block_grams, _ = unpack_all(small, 0, lambda first, count: gram[first : first + count, :])
+    block_polys = polys_of(block_grams)
+    last = edge + large * 2 * FBLK
+    poly[last:, :] = jnp.zeros((poly.shape[0] - last, FBLK), FULL)
 
     def write(first, rows):
         poly[first : first + rows.shape[0], :] = rows
@@ -1960,6 +2000,8 @@
             device = square.device(j, turn, 1 - square.core)
             apply(reader(poly_all.at[device]), device)
     stored = in_old.shape[1]
+    for copy in sides:
+        copy.wait()
     for device in range(ctx):
         first = device * large
         if first < head_update.shape[0]:
@@ -1984,14 +2026,14 @@
 def newton(
     heads, blocks, gains, head_update, in_old, out_old, ffn_update, ffn_old, head_rate, ffn_rate, fsdp
 ):
-    ctx, large = heads.shape[:2]
-    small = blocks.shape[1]
-    rows = packed_rows(small, large)
+    ctx, small = blocks.shape[:2]
+    large = -(-head_update.shape[0] // ctx)
+    rows, block_rows = packed_rows(small, large), packed_rows(small, 0)
     dma = pltpu.SemaphoreType.DMA
     matrices = ffn_old.shape[0]
     return pl.pallas_call(
-        functools.partial(newton_kernel, ctx, fsdp, head_rate, ffn_rate),
-        in_specs=[VMEM_SPEC] * 6 + [ANY_SPEC] * 2,
+        functools.partial(newton_kernel, ctx, fsdp, large, head_rate, ffn_rate),
+        in_specs=[VMEM_SPEC] * 3 + [ANY_SPEC] * 5,
         out_specs=[VMEM_SPEC] * 2 + [ANY_SPEC, VMEM_SPEC],
         out_shape=[
             jax.ShapeDtypeStruct(in_old.shape, FULL),
@@ -2000,8 +2042,8 @@
             jax.ShapeDtypeStruct((ctx,) + gains.shape, FULL),
         ],
         scratch_shapes=[
-            pltpu.VMEM((ctx, rows, FBLK), FULL),
-            pltpu.VMEM((rows, FBLK), FULL),
+            pltpu.VMEM((ctx, block_rows, FBLK), FULL),
+            pltpu.VMEM((block_rows, FBLK), FULL),
             pltpu.VMEM((rows, FBLK), FULL),
             pltpu.VMEM((ctx, rows, FBLK), FULL),
             pltpu.VMEM((fsdp,) + gains.shape, FULL),
@@ -2013,8 +2055,12 @@
             dma((matrices,)),
             dma((matrices,)),
             dma((ctx * small,)),
+            pltpu.VMEM(head_update.shape, LOW),
+            pltpu.VMEM(in_old.shape, FULL),
+            pltpu.VMEM(out_old.shape, FULL),
+            dma((3,)),
         ]
-        + ctx_scatter_scratch(ctx, 1, rows, FBLK, FULL)
+        + ctx_scatter_scratch(ctx, 1, block_rows, FBLK, FULL)
         + ctx_gather_sems(ctx) * 2,
         compiler_params=pltpu.CompilerParams(vmem_limit_bytes=VMEM_LIMIT, collective_id=4),
         name="newton",
@@ -2180,7 +2226,7 @@
     momentum = jnp.transpose(ffn_momentum, (1, 0, 2))
     small = -(-3 * (ffn_local // FBLK) // ctx)
     earlier = ffn_gram(down_grads, momentum, 2, ctx * small, [])
-    momentum_new_in, momentum_new_out, head_update, head_gram, input_grad, gain_pre = tail(
+    momentum_new_in, momentum_new_out, head_update, head_sum, input_grad, gain_pre = tail(
         dot(normed_low, projected_grad, 0, 0).astype(LOW).reshape(ctx, local_rows, mine * head),
         dot(branch_low, attended_low, 0, 0).astype(LOW).reshape(ctx, local_rows, out_local * head),
         parts(dot(projected_grad, w_in, 1, 1)),
@@ -2196,7 +2242,7 @@
 
     new_ffn, ffn_update, block_gram = ffn_gram(pair_grads, momentum, 0, ctx * small, earlier)
     new_weights_in, new_weights_out, new_ffn_weights, gain_every = newton(
-        head_gram.reshape(ctx, -1, head, head),
+        head_sum,
         block_gram.reshape(ctx, small, FBLK, FBLK),
         gain_parts,
         head_update,

time: 678 us -> 675 us (level)
  waiting for transfers between devices: 17.6 us -> 8.28 us
    pallas_call x1, Pallas kernels: 87.6 us -> 101 us  [tail(): pl.pallas_call(functools.partial(tail_kernel, ctx, fsdp), in_specs=[VMEM_...]
    reduce_scatter x1, waiting for transfers between devices: 13.5 us -> 4.15 us  [local(): lax.psum_scatter(pair_part, 'ctx', scatter_dimension=0, tiled=True)]
    pallas_call x1, Pallas kernels: 62.2 us -> 54.1 us  [newton(): pl.pallas_call(functools.partial(newton_kernel, ctx, fsdp, large, head_ra...]
  transfers between devices with their start and end apart: 3 -> 3, of which waited for: 2 -> 2; matrix products, arithmetic and copies ran while one was open for 6% -> 6% of each run, Pallas kernels for 57% -> 59%
where the time goes in v3:
time: 675 us; the launch traced here: 665 us
  Pallas kernels  573 us (85%)
  matrix products  44.5 us (7%)
  local copies, waits for them, and re-layouts  18.8 us (3%)
  between operations  14.6 us (2%)
  waiting for transfers between devices  8.28 us (1%)
    pallas_call x1, Pallas kernels, tail(): pl.pallas_call(functools.partial(tail_kernel, ctx, fsdp), in_specs=[VMEM_...  101 us
    pallas_call x1, Pallas kernels, mid_exchange(): pl.pallas_call(functools.partial(mid_kernel, fsdp), in_specs=[VMEM_SPEC]...  97.4 us
    pallas_call x1, Pallas kernels, late_exchange(): pl.pallas_call(functools.partial(late_kernel, fsdp), in_specs=[VMEM_SPEC]...  90.4 us
    pallas_call x1, Pallas kernels, project(): pl.pallas_call(functools.partial(project_kernel, ctx, fsdp, tokens // chu...  88.4 us
    pallas_call x1, Pallas kernels, exchange(): pl.pallas_call(functools.partial(exchange_kernel, mid, fsdp, len(ins)), i...  75.1 us
    pallas_call x1, Pallas kernels, newton(): pl.pallas_call(functools.partial(newton_kernel, ctx, fsdp, large, head_ra...  54.1 us
    dot_general x6, matrix products, dot(): lax.dot_general(left, right, (((left_dim,), (right_dim,)), ((), ())), pre...  28.2 us
    pallas_call x1, Pallas kernels, scatter_pairs(): pl.pallas_call(functools.partial(pair_sums_kernel, ctx), in_specs=[VMEM_S...  26.6 us
  transfers between devices with their start and end apart: 3, of which 2 were waited for; matrix products, arithmetic and copies ran while one was open for 6% of the time, Pallas kernels for 59%

profile of v3, /device:TPU:0, one launch (start us, length us, event | category | flops | bytes accessed | tf_op | source)
XLA Modules:
  0.0 665.0 jit_solution(116358336437172645)
XLA Ops:
  7.2 0.0 all-gather.2.cloned.1.call-start
  7.2 25.0 %prepare.1 = (bf16[288,1024]{1,0:T(8,128)(2,1)}, bf16[8,288,512]{2,1,0:T(8,128)(2,1)}, bf16[3,288,2304]{2,1,0:T(8,128)(2,1)}, bf16[128,2304]{1,0:T(8,128)(2,1)}) custom-call(f32[288,4,256]{2,1,0:T(4,128)} %in_old_in.1, f32[288,2,256]{2,1,0:T(2,128)} %out_old_in.1, f32[3,288,2304]{2,1,0:T(8,128)} %bitcast.101, bf16[128,2304]{1,0:T(8,128)(2,1)} %bitcast.107, ...), custom_call_target="tpu_custom_call" | custom-call | tf_op jit(solution)/shard_map/prepare/pallas_call | solution.py:708
  32.2 0.0 copy-start.13
  32.2 0.0 all-gather.2.cloned.1.call-update
  32.2 0.0 reduce-scatter.5.cloned.1.call-start
  32.3 0.5 copy-done.13
  32.8 0.1 select_reduce_fusion.1
  32.9 1.0 fusion.16
  33.9 88.4 %project.1 = (bf16[4,128,2304]{2,1,0:T(8,128)(2,1)}, bf16[2304,1024]{1,0:T(8,128)(2,1)}, bf16[512,512]{1,0:T(8,128)(2,1)}, bf16[4,8,128,256]{3,2,1,0:T(8,128)(2,1)}, bf16[4,8,128,256]{3,2,1,0:T(8,128)(2,1)}) custom-call(bf16[128,2304]{1,0:T(8,128)(2,1)} %get-tuple-element.51.own, bf16[288,1024]{1,0:T(8,128)(2,1)} %get-tuple-element.52.mine, ...), custom_call_target="tpu_custom_call" | custom-call | tf_op jit(solution)/shard_map/project/pallas_call | solution.py:824
  122.3 0.1 select_reduce_fusion
  122.4 0.1 broadcast_compare_fusion
  122.6 1.2 fusion.37
  123.8 0.1 tile.10
  123.9 4.2 fusion
  128.0 0.0 copy-start.19
  128.1 0.0 copy-done.17
  128.1 0.0 copy-start.15
  128.1 1.6 fusion.38
  129.7 0.5 copy-done.19
  130.2 1.0 copy-done.15
  131.2 2.8 convolution_convert_fusion.3
  134.1 75.1 %branch_exchange.1 = (bf16[4,128,2304]{2,1,0:T(8,128)(2,1)}, f32[128,2304]{1,0:T(8,128)}, f32[128,2304]{1,0:T(8,128)}) custom-call(bf16[4,128,2304]{2,1,0:T(8,128)(2,1)} %bitcast.111, bf16[128,2304]{1,0:T(8,128)(2,1)} %bitcast.108, f32[4,2304]{1,0:T(4,128)} %gains.7), custom_call_target="tpu_custom_call" | custom-call | tf_op jit(solution)/shard_map/branch_exchange/pallas_call | solution.py:991
  209.2 4.1 all-gather.2.cloned.1.call-done.weights
  213.3 90.4 %late_exchange.1 = (bf16[4,128,2304]{2,1,0:T(8,128)(2,1)}, bf16[128,2304]{1,0:T(8,128)(2,1)}, f32[1,2304]{1,0:T(1,128)}, bf16[4,128,2304]{2,1,0:T(8,128)(2,1)}, ...) custom-call(f32[4,2304]{1,0:T(4,128)} %gains.7, bf16[4,128,2304]{2,1,0:T(8,128)(2,1)} %get-tuple-element.57.mid, ...), custom_call_target="tpu_custom_call" | custom-call | tf_op jit(solution)/shard_map/late_exchange/pallas_call | solution.py:1191
  303.6 10.4 %bitcast_convert_fusion = bf16[2304,2304]{1,0:T(8,128)(2,1)} fusion(bf16[4,128,2304]{2,1,0:T(8,128)(2,1)} %get-tuple-element.62.late, bf16[4,128,2304]{2,1,0:T(8,128)(2,1)} %get-tuple-element.74), kind=kOutput, calls=%fused_computation | convolution fusion | flops 5441126400 | bytes 15335424 | tf_op jit(solution)/shard_map/dot_general | solution.py:71
  314.0 0.0 reduce-scatter.5.cloned.1.call-update
  314.0 0.0 reduce-scatter.3.cloned.1.call-start
  314.1 97.4 %mid_exchange.1 = (bf16[4,128,2304]{2,1,0:T(8,128)(2,1)}, f32[128,2304]{1,0:T(8,128)}, f32[2,2304]{1,0:T(2,128)}, bf16[2304,4608]{1,0:T(8,128)(2,1)}) custom-call(f32[4,2304]{1,0:T(4,128)} %gains.7, bf16[4,128,2304]{2,1,0:T(8,128)(2,1)} %get-tuple-element.62.late, f32[128,2304]{1,0:T(8,128)} %get-tuple-element.58.mixed_in, ...), custom_call_target="tpu_custom_call" | custom-call | tf_op jit(solution)/shard_map/mid_exchange/pallas_call | solution.py:1454
  411.5 0.0 reduce-scatter.3.cloned.1.call-update
  411.5 0.0 copy-start.20
  411.5 3.9 fusion.39
  415.4 0.1 fusion.35
  415.5 0.2 multiply_reduce_fusion
  415.8 1.3 copy-done.18
  417.1 2.7 multiply_convert_fusion
  419.8 2.3 convolution_convert_fusion.5
  422.1 3.2 convolution_convert_fusion.4
  425.3 26.6 %scatter_pairs.1 = (f32[4,128,256]{2,1,0:T(8,128)}, f32[4,128,256]{2,1,0:T(8,128)}) custom-call(bf16[4,8,128,256]{3,2,1,0:T(8,128)(2,1)} %bitcast.104, bf16[4,8,128,256]{3,2,1,0:T(8,128)(2,1)} %bitcast.118), custom_call_target="tpu_custom_call" | custom-call | tf_op jit(solution)/shard_map/scatter_pairs/pallas_call | solution.py:1586
  452.0 0.0 copy-start.4
  452.0 0.0 copy-start.8
  452.0 1.1 convert.28
  453.1 2.3 fusion.40
  455.5 0.1 slice_multiply_fusion
  455.6 0.2 fusion.14
  456.1 1.0 copy-done.16
  457.1 2.8 convolution_convert_fusion.2
  460.0 0.0 copy-done.14
  460.0 4.3 convolution_convert_fusion
  464.3 3.9 convolution_convert_fusion.1
  468.2 101.5 %tail.1 = (f32[288,4,256]{2,1,0:T(4,128)}, f32[288,2,256]{2,1,0:T(2,128)}, bf16[6,288,256]{2,1,0:T(8,128)(2,1)}, f32[272,128]{1,0:T(8,128)}, f32[128,2304]{1,0:T(8,128)}, /*index=5*/f32[1,2304]{1,0:T(1,128)}) custom-call(bf16[8,288,1024]{2,1,0:T(8,128)(2,1)} %bitcast.110, bf16[8,288,512]{2,1,0:T(8,128)(2,1)} %bitcast.112, bf16[4,128,2304]{2,1,0:T(8,128)(2,1)} %bitcast.113, ...), custom_call_target="tpu_custom_call" | custom-call | tf_op jit(solution)/shard_map/tail/pallas_call | solution.py:1754
  569.7 1.3 pad_maximum_fusion.7.gains
  571.1 5.4 ffn_gram.2
  576.5 4.1 reduce-scatter.3.cloned.1.call-done.grad_ref
  580.7 8.7 %ffn_gram.3 = (f32[3,288,2304]{2,1,0:T(8,128)}, bf16[3,288,2304]{2,1,0:T(8,128)(2,1)}, f32[56,128,128]{2,1,0:T(8,128)}) custom-call(bf16[288,4608]{1,0:T(8,128)(2,1)} %reduce-scatter.3.cloned.1.call-done.grad_ref, f32[3,288,2304]{2,1,0:T(8,128)} %bitcast.100, ...), custom_call_target="tpu_custom_call", output_to_operand_aliasing={{0}: (2, {}), {1}: (3, {}), {2}: (4, {})} | custom-call | tf_op jit(solution)/shard_map/ffn_gram/pallas_call | solution.py:94
  589.4 54.1 %newton.1 = (f32[288,4,256]{2,1,0:T(4,128)}, f32[288,2,256]{2,1,0:T(2,128)}, f32[3,288,2304]{2,1,0:T(8,128)}, f32[8,4,2304]{2,1,0:T(4,128)}) custom-call(f32[272,128]{1,0:T(8,128)} %get-tuple-element.72.heads, f32[8,7,128,128]{3,2,1,0:T(8,128)} %bitcast.103, f32[4,2304]{1,0:T(4,128)} %pad_maximum_fusion.7.gains, ...), custom_call_target="tpu_custom_call" | custom-call | tf_op jit(solution)/shard_map/newton/pallas_call | solution.py:2034
  643.5 1.1 reduce_sum.49
  644.7 0.7 divide_subtract_fusion
  645.3 0.8 copy.51
  646.2 1.0 copy.52
  647.2 1.0 copy.53
  648.2 0.8 copy.54
  649.0 7.2 %copy.55 = f32[288,3,2304]{2,0,1:T(8,128)} copy(f32[288,3,2304]{2,0,1:T(8,128)} %bitcast.105) | data formatting | bytes 15925248
  656.2 1.0 copy.56
  657.2 0.8 copy.57
  (49 shorter events, 0.4 us)
Async XLA Ops:
  7.2 206.1 %all-gather.2.cloned.1.call-start = ((), (), s32[]{:S(2)}) async-start(), calls=%async_computation.2 | async-start | bytes 35831808 | tf_op jit(solution)/shard_map/all_gather | solution.py:2104
  32.2 0.7 copy-start.13
  32.2 538.8 %reduce-scatter.5.cloned.1.call-start = ((), (), s32[]{:S(2)}) async-start(), calls=%async_computation.4 | async-start | bytes 11943936 | tf_op jit(solution)/shard_map/reduce_scatter | solution.py:2186
  123.9 4.2 copy-start.17
  128.0 2.1 copy-start.19
  128.1 3.2 copy-start.15
  314.0 266.6 %reduce-scatter.3.cloned.1.call-start = ((), (), s32[]{:S(2)}) async-start(), calls=%async_computation.3 | async-start | bytes 23887872 | tf_op jit(solution)/shard_map/reduce_scatter | solution.py:2200
  411.5 4.2 copy-start.20
  415.4 1.6 copy-start.18
  452.0 3.6 copy-start.4
  452.0 3.6 copy-start.8
  455.4 1.7 copy-start.16
  457.1 2.9 copy-start.14
  457.1 7.2 %slice-start = ((s8[4718592]{0:T(1024)(128)(4,1)}), s8[4194304]{0:T(1024)(128)(4,1)S(1)}, s32[]{:S(2)}) async-start(s8[4718592]{0:T(1024)(128)(4,1)} %bitcast.143), calls=%async_computation.5 | async-start | bytes 8388608
  460.0 4.3 slice-start.1
  468.2 101.5 %copy-start.11 = (f32[2,2304]{1,0:T(2,128)S(1)}, f32[2,2304]{1,0:T(2,128)}, u32[]{:S(2)}) copy-start(f32[2,2304]{1,0:T(2,128)} %get-tuple-element.80) | copy-start | bytes 55300
  468.2 101.5 %copy-start.12 = (f32[1,2304]{1,0:T(1,128)S(1)}, f32[1,2304]{1,0:T(1,128)}, u32[]{:S(2)}) copy-start(f32[1,2304]{1,0:T(1,128)} %get-tuple-element.81) | copy-start | bytes 27652
  589.4 55.2 %copy-start = (f32[4,2304]{1,0:T(4,128)S(1)}, f32[4,2304]{1,0:T(4,128)}, u32[]{:S(2)}) copy-start(f32[4,2304]{1,0:T(4,128)} %gains.7) | copy-start | bytes 110596
  589.4 55.2 %copy-start.9 = (f32[4,2304]{1,0:T(4,128)S(1)}, f32[4,2304]{1,0:T(4,128)}, u32[]{:S(2)}) copy-start(f32[4,2304]{1,0:T(4,128)} %param.21) | copy-start | bytes 110596
  589.4 55.2 %copy-start.10 = (f32[4,2304]{1,0:T(4,128)S(1)}, f32[4,2304]{1,0:T(4,128)}, u32[]{:S(2)}) copy-start(f32[4,2304]{1,0:T(4,128)} %param.22) | copy-start | bytes 110596
  589.4 55.9 %copy-start.5 = (bf16[128,2304]{1,0:T(8,128)(2,1)S(1)}, bf16[128,2304]{1,0:T(8,128)(2,1)}, u32[]{:S(2)}) copy-start(bf16[128,2304]{1,0:T(8,128)(2,1)} %get-tuple-element.60) | copy-start | bytes 1769476
  589.4 56.8 %copy-start.2 = (f32[128,2304]{1,0:T(8,128)S(1)}, f32[128,2304]{1,0:T(8,128)}, u32[]{:S(2)}) copy-start(f32[128,2304]{1,0:T(8,128)} %get-tuple-element.71) | copy-start | bytes 3538948
  643.5 3.7 copy-start.3
  644.6 3.5 copy-start.7
  649.0 7.2 %copy-start.1 = (f32[288,4,256]{2,1,0:T(4,128)S(1)}, f32[288,4,256]{2,1,0:T(4,128)}, u32[]{:S(2)}) copy-start(f32[288,4,256]{2,1,0:T(4,128)} %get-tuple-element.137) | copy-start | bytes 3538948
  649.0 8.2 %copy-start.6 = (f32[288,2,256]{2,1,0:T(2,128)S(1)}, f32[288,2,256]{2,1,0:T(2,128)}, u32[]{:S(2)}) copy-start(f32[288,2,256]{2,1,0:T(2,128)} %get-tuple-element.138) | copy-start | bytes 1769476
Sparse Core Ops, SparseCore 0:
  32.3 180.8 all-gather.1
  314.1 80.3 reduce-scatter.4
  411.6 168.9 reduce-scatter.2

commit v4 on v3

--- a/solution.py
+++ b/solution.py
@@ -179,13 +179,17 @@
     )
 
 
-def greet(peers):
+def call(peers):
     barrier = pltpu.get_barrier_semaphore()
     for axis, to in peers:
         pl.semaphore_signal(
             barrier, inc=1, device_id={axis: to}, device_id_type=pl.DeviceIdType.MESH
         )
-    pl.semaphore_wait(barrier, len(peers))
+
+
+def greet(peers):
+    call(peers)
+    pl.semaphore_wait(pltpu.get_barrier_semaphore(), len(peers))
 
 
 def line_greet(at, size):
@@ -634,9 +638,11 @@
 ):
     at, line_at = lax.axis_index("ctx"), lax.axis_index("fsdp")
     in_low, out_low, wide, wide_sem, move_send, move_receive = scratch[:6]
+    cast, cast_sem = scratch[11:]
     places = head_places(fsdp)
     head = in_ref.shape[2]
-    greet(ctx_peers(at, ctx) + [("fsdp", (line_at + k) % fsdp) for k in range(1, fsdp)])
+    peers = ctx_peers(at, ctx) + [("fsdp", (line_at + k) % fsdp) for k in range(1, fsdp)]
+    call(peers)
 
     def move(user, slot):
         owner, index = places[user][slot]
@@ -654,9 +660,16 @@
             ffn_ref.at[matrix], wide.at[matrix % 2], wide_sem.at[matrix % 2]
         )
 
+    def give(matrix):
+        return pltpu.make_async_copy(cast.at[matrix], ffn_low.at[matrix], cast_sem.at[matrix])
+
     load(0).start()
+    load(1).start()
     for index in range(in_ref.shape[1]):
         in_low[index] = in_ref[:, index, :].astype(LOW)
+    for index in range(out_ref.shape[1]):
+        out_low[:, index * head : (index + 1) * head] = out_ref[:, index, :].astype(LOW)
+    pl.semaphore_wait(pltpu.get_barrier_semaphore(), len(peers))
     for user in range(fsdp):
         for slot in range(len(places[0])):
             owner, index = places[user][slot]
@@ -668,17 +681,16 @@
                 else:
                     move(user, slot).start()
 
-    for index in range(out_ref.shape[1]):
-        out_low[:, index * head : (index + 1) * head] = out_ref[:, index, :].astype(LOW)
     gather = CtxGather(at, ctx, out_low, lambda c: out_all.at[c], 0, scratch[6:11])
     gather.start()
+    for matrix in range(3):
+        load(matrix).wait()
+        cast[matrix] = wide[matrix % 2].astype(LOW)
+        give(matrix).start()
+        if matrix == 0:
+            load(2).start()
     x = x_ref[...].astype(FULL)
     normed[...] = (x * rms_scale(x) * (1.0 + gains[0:1, :])).astype(LOW)
-    for matrix in range(3):
-        load(matrix).wait()
-        if matrix < 2:
-            load(matrix + 1).start()
-        ffn_low[matrix] = wide[matrix % 2].astype(LOW)
     gather.forward()
     gather.rest()
     for user in range(fsdp):
@@ -698,6 +710,8 @@
                     move(user, slot).wait_send()
 
     gather.finish()
+    for matrix in range(3):
+        give(matrix).wait()
 
 
 def prepare(weights_in, weights_out, ffn, x, gains, ctx, fsdp):
@@ -708,7 +722,7 @@
     return pl.pallas_call(
         functools.partial(prepare_kernel, ctx, fsdp),
         in_specs=[VMEM_SPEC] * 2 + [ANY_SPEC] + [VMEM_SPEC] * 2,
-        out_specs=[VMEM_SPEC, ANY_SPEC, VMEM_SPEC, VMEM_SPEC],
+        out_specs=[VMEM_SPEC, ANY_SPEC, ANY_SPEC, VMEM_SPEC],
         out_shape=[
             jax.ShapeDtypeStruct((local_rows, mine * head), LOW),
             jax.ShapeDtypeStruct((ctx, local_rows, out_local * head), LOW),
@@ -723,7 +737,8 @@
             dma((fsdp, mine)),
             dma((mine,)),
         ]
-        + ctx_gather_sems(ctx),
+        + ctx_gather_sems(ctx)
+        + [pltpu.VMEM(ffn.shape, LOW), dma((3,))],
         compiler_params=pltpu.CompilerParams(vmem_limit_bytes=VMEM_LIMIT, collective_id=0),
         name="prepare",
     )(weights_in, weights_out, ffn, x, gains)

time: 675 us -> 671 us (level)
  transfers between devices with their start and end apart: 3 -> 3, of which waited for: 2 -> 2; matrix products, arithmetic and copies ran while one was open for 6% -> 6% of each run, Pallas kernels for 59% -> 60%
where the time goes in v4:
time: 671 us; the launch traced here: 661 us
  Pallas kernels  570 us (85%)
  matrix products  44.5 us (7%)
  local copies, waits for them, and re-layouts  18.8 us (3%)
  between operations  14.6 us (2%)
  waiting for transfers between devices  7.44 us (1%)
    pallas_call x1, Pallas kernels, tail(): pl.pallas_call(functools.partial(tail_kernel, ctx, fsdp), in_specs=[VMEM_...  101 us
    pallas_call x1, Pallas kernels, mid_exchange(): pl.pallas_call(functools.partial(mid_kernel, fsdp), in_specs=[VMEM_SPEC]...  97.3 us
    pallas_call x1, Pallas kernels, late_exchange(): pl.pallas_call(functools.partial(late_kernel, fsdp), in_specs=[VMEM_SPEC]...  90.4 us
    pallas_call x1, Pallas kernels, project(): pl.pallas_call(functools.partial(project_kernel, ctx, fsdp, tokens // chu...  88.9 us
    pallas_call x1, Pallas kernels, exchange(): pl.pallas_call(functools.partial(exchange_kernel, mid, fsdp, len(ins)), i...  75.4 us
    pallas_call x1, Pallas kernels, newton(): pl.pallas_call(functools.partial(newton_kernel, ctx, fsdp, large, head_ra...  54.1 us
    dot_general x6, matrix products, dot(): lax.dot_general(left, right, (((left_dim,), (right_dim,)), ((), ())), pre...  28.2 us
    pallas_call x1, Pallas kernels, scatter_pairs(): pl.pallas_call(functools.partial(pair_sums_kernel, ctx), in_specs=[VMEM_S...  26.7 us
  transfers between devices with their start and end apart: 3, of which 2 were waited for; matrix products, arithmetic and copies ran while one was open for 6% of the time, Pallas kernels for 60%

profile of v4, /device:TPU:0, one launch (start us, length us, event | category | flops | bytes accessed | tf_op | source)
XLA Modules:
  0.0 661.5 jit_solution(567203893017846597)
XLA Ops:
  7.2 0.0 all-gather.2.cloned.1.call-start
  7.2 21.4 %prepare.1 = (bf16[288,1024]{1,0:T(8,128)(2,1)}, bf16[8,288,512]{2,1,0:T(8,128)(2,1)}, bf16[3,288,2304]{2,1,0:T(8,128)(2,1)}, bf16[128,2304]{1,0:T(8,128)(2,1)}) custom-call(f32[288,4,256]{2,1,0:T(4,128)} %in_old_in.1, f32[288,2,256]{2,1,0:T(2,128)} %out_old_in.1, f32[3,288,2304]{2,1,0:T(8,128)} %bitcast.101, bf16[128,2304]{1,0:T(8,128)(2,1)} %bitcast.107, ...), custom_call_target="tpu_custom_call" | custom-call | tf_op jit(solution)/shard_map/prepare/pallas_call | solution.py:722
  28.7 0.0 copy-start.13
  28.7 0.0 all-gather.2.cloned.1.call-update
  28.7 0.0 reduce-scatter.5.cloned.1.call-start
  28.8 0.5 copy-done.13
  29.3 0.1 select_reduce_fusion.1
  29.4 1.0 fusion.16
  30.4 88.9 %project.1 = (bf16[4,128,2304]{2,1,0:T(8,128)(2,1)}, bf16[2304,1024]{1,0:T(8,128)(2,1)}, bf16[512,512]{1,0:T(8,128)(2,1)}, bf16[4,8,128,256]{3,2,1,0:T(8,128)(2,1)}, bf16[4,8,128,256]{3,2,1,0:T(8,128)(2,1)}) custom-call(bf16[128,2304]{1,0:T(8,128)(2,1)} %get-tuple-element.51.own, bf16[288,1024]{1,0:T(8,128)(2,1)} %get-tuple-element.52.mine, ...), custom_call_target="tpu_custom_call" | custom-call | tf_op jit(solution)/shard_map/project/pallas_call | solution.py:839
  119.3 0.1 select_reduce_fusion
  119.4 0.1 broadcast_compare_fusion
  119.6 1.2 fusion.37
  120.8 0.1 tile.10
  120.9 0.0 copy-start.17
  120.9 4.2 fusion
  125.1 0.0 copy-start.19
  125.1 1.6 fusion.38
  126.7 0.5 copy-done.19
  127.2 1.0 copy-done.15
  128.3 2.8 convolution_convert_fusion.3
  131.1 75.4 %branch_exchange.1 = (bf16[4,128,2304]{2,1,0:T(8,128)(2,1)}, f32[128,2304]{1,0:T(8,128)}, f32[128,2304]{1,0:T(8,128)}) custom-call(bf16[4,128,2304]{2,1,0:T(8,128)(2,1)} %bitcast.111, bf16[128,2304]{1,0:T(8,128)(2,1)} %bitcast.108, f32[4,2304]{1,0:T(4,128)} %gains.7), custom_call_target="tpu_custom_call" | custom-call | tf_op jit(solution)/shard_map/branch_exchange/pallas_call | solution.py:1006
  206.5 3.2 all-gather.2.cloned.1.call-done.weights
  209.7 90.4 %late_exchange.1 = (bf16[4,128,2304]{2,1,0:T(8,128)(2,1)}, bf16[128,2304]{1,0:T(8,128)(2,1)}, f32[1,2304]{1,0:T(1,128)}, bf16[4,128,2304]{2,1,0:T(8,128)(2,1)}, ...) custom-call(f32[4,2304]{1,0:T(4,128)} %gains.7, bf16[4,128,2304]{2,1,0:T(8,128)(2,1)} %get-tuple-element.57.mid, ...), custom_call_target="tpu_custom_call" | custom-call | tf_op jit(solution)/shard_map/late_exchange/pallas_call | solution.py:1206
  300.1 10.4 %bitcast_convert_fusion = bf16[2304,2304]{1,0:T(8,128)(2,1)} fusion(bf16[4,128,2304]{2,1,0:T(8,128)(2,1)} %get-tuple-element.62.late, bf16[4,128,2304]{2,1,0:T(8,128)(2,1)} %get-tuple-element.74), kind=kOutput, calls=%fused_computation | convolution fusion | flops 5441126400 | bytes 15335424 | tf_op jit(solution)/shard_map/dot_general | solution.py:71
  310.5 0.0 reduce-scatter.5.cloned.1.call-update
  310.5 0.0 reduce-scatter.3.cloned.1.call-start
  310.5 97.3 %mid_exchange.1 = (bf16[4,128,2304]{2,1,0:T(8,128)(2,1)}, f32[128,2304]{1,0:T(8,128)}, f32[2,2304]{1,0:T(2,128)}, bf16[2304,4608]{1,0:T(8,128)(2,1)}) custom-call(f32[4,2304]{1,0:T(4,128)} %gains.7, bf16[4,128,2304]{2,1,0:T(8,128)(2,1)} %get-tuple-element.62.late, f32[128,2304]{1,0:T(8,128)} %get-tuple-element.58.mixed_in, ...), custom_call_target="tpu_custom_call" | custom-call | tf_op jit(solution)/shard_map/mid_exchange/pallas_call | solution.py:1469
  407.9 0.0 reduce-scatter.3.cloned.1.call-update
  407.9 0.0 copy-start.20
  407.9 3.9 fusion.39
  411.8 0.0 copy-start.18
  411.8 0.1 fusion.35
  411.9 0.2 multiply_reduce_fusion
  412.1 1.3 copy-done.18
  413.5 2.7 multiply_convert_fusion
  416.2 2.3 convolution_convert_fusion.5
  418.5 3.2 convolution_convert_fusion.4
  421.7 26.7 %scatter_pairs.1 = (f32[4,128,256]{2,1,0:T(8,128)}, f32[4,128,256]{2,1,0:T(8,128)}) custom-call(bf16[4,8,128,256]{3,2,1,0:T(8,128)(2,1)} %bitcast.104, bf16[4,8,128,256]{3,2,1,0:T(8,128)(2,1)} %bitcast.118), custom_call_target="tpu_custom_call" | custom-call | tf_op jit(solution)/shard_map/scatter_pairs/pallas_call | solution.py:1601
  448.5 0.0 copy-start.4
  448.5 1.1 convert.28
  449.6 2.3 fusion.40
  451.9 0.0 copy-start.16
  451.9 0.1 slice_multiply_fusion
  452.0 0.0 copy-done.4
  452.0 0.2 fusion.14
  452.6 1.0 copy-done.16
  453.6 2.8 convolution_convert_fusion.2
  456.5 4.3 convolution_convert_fusion
  460.8 3.9 convolution_convert_fusion.1
  464.7 101.5 %tail.1 = (f32[288,4,256]{2,1,0:T(4,128)}, f32[288,2,256]{2,1,0:T(2,128)}, bf16[6,288,256]{2,1,0:T(8,128)(2,1)}, f32[272,128]{1,0:T(8,128)}, f32[128,2304]{1,0:T(8,128)}, /*index=5*/f32[1,2304]{1,0:T(1,128)}) custom-call(bf16[8,288,1024]{2,1,0:T(8,128)(2,1)} %bitcast.110, bf16[8,288,512]{2,1,0:T(8,128)(2,1)} %bitcast.112, bf16[4,128,2304]{2,1,0:T(8,128)(2,1)} %bitcast.113, ...), custom_call_target="tpu_custom_call" | custom-call | tf_op jit(solution)/shard_map/tail/pallas_call | solution.py:1769
  566.2 1.3 pad_maximum_fusion.7.gains
  567.6 5.4 ffn_gram.2
  573.0 4.2 reduce-scatter.3.cloned.1.call-done.grad_ref
  577.2 8.7 %ffn_gram.3 = (f32[3,288,2304]{2,1,0:T(8,128)}, bf16[3,288,2304]{2,1,0:T(8,128)(2,1)}, f32[56,128,128]{2,1,0:T(8,128)}) custom-call(bf16[288,4608]{1,0:T(8,128)(2,1)} %reduce-scatter.3.cloned.1.call-done.grad_ref, f32[3,288,2304]{2,1,0:T(8,128)} %bitcast.100, ...), custom_call_target="tpu_custom_call", output_to_operand_aliasing={{0}: (2, {}), {1}: (3, {}), {2}: (4, {})} | custom-call | tf_op jit(solution)/shard_map/ffn_gram/pallas_call | solution.py:94
  585.9 54.1 %newton.1 = (f32[288,4,256]{2,1,0:T(4,128)}, f32[288,2,256]{2,1,0:T(2,128)}, f32[3,288,2304]{2,1,0:T(8,128)}, f32[8,4,2304]{2,1,0:T(4,128)}) custom-call(f32[272,128]{1,0:T(8,128)} %get-tuple-element.72.heads, f32[8,7,128,128]{3,2,1,0:T(8,128)} %bitcast.103, f32[4,2304]{1,0:T(4,128)} %pad_maximum_fusion.7.gains, ...), custom_call_target="tpu_custom_call" | custom-call | tf_op jit(solution)/shard_map/newton/pallas_call | solution.py:2049
  640.0 1.1 reduce_sum.49
  641.2 0.7 divide_subtract_fusion
  641.9 0.8 copy.51
  642.7 1.0 copy.52
  643.7 1.0 copy.53
  644.7 0.8 copy.54
  645.5 7.2 %copy.55 = f32[288,3,2304]{2,0,1:T(8,128)} copy(f32[288,3,2304]{2,0,1:T(8,128)} %bitcast.105) | data formatting | bytes 15925248
  652.7 1.0 copy.56
  653.7 0.8 copy.57
  (49 shorter events, 0.4 us)
Async XLA Ops:
  7.2 202.5 %all-gather.2.cloned.1.call-start = ((), (), s32[]{:S(2)}) async-start(), calls=%async_computation.2 | async-start | bytes 35831808 | tf_op jit(solution)/shard_map/all_gather | solution.py:2119
  28.7 0.7 copy-start.13
  28.7 538.9 %reduce-scatter.5.cloned.1.call-start = ((), (), s32[]{:S(2)}) async-start(), calls=%async_computation.4 | async-start | bytes 11943936 | tf_op jit(solution)/shard_map/reduce_scatter | solution.py:2201
  120.9 4.2 copy-start.17
  125.1 2.1 copy-start.19
  125.1 3.2 copy-start.15
  310.5 266.7 %reduce-scatter.3.cloned.1.call-start = ((), (), s32[]{:S(2)}) async-start(), calls=%async_computation.3 | async-start | bytes 23887872 | tf_op jit(solution)/shard_map/reduce_scatter | solution.py:2215
  407.9 4.2 copy-start.20
  411.8 1.7 copy-start.18
  448.5 3.6 copy-start.4
  448.5 3.6 copy-start.8
  451.9 1.7 copy-start.16
  453.6 2.9 copy-start.14
  453.6 7.1 %slice-start = ((s8[4718592]{0:T(1024)(128)(4,1)}), s8[4194304]{0:T(1024)(128)(4,1)S(1)}, s32[]{:S(2)}) async-start(s8[4718592]{0:T(1024)(128)(4,1)} %bitcast.143), calls=%async_computation.5 | async-start | bytes 8388608
  456.5 4.3 slice-start.1
  464.7 101.5 %copy-start.11 = (f32[2,2304]{1,0:T(2,128)S(1)}, f32[2,2304]{1,0:T(2,128)}, u32[]{:S(2)}) copy-start(f32[2,2304]{1,0:T(2,128)} %get-tuple-element.80) | copy-start | bytes 55300
  464.7 101.5 %copy-start.12 = (f32[1,2304]{1,0:T(1,128)S(1)}, f32[1,2304]{1,0:T(1,128)}, u32[]{:S(2)}) copy-start(f32[1,2304]{1,0:T(1,128)} %get-tuple-element.81) | copy-start | bytes 27652
  585.9 55.2 %copy-start = (f32[4,2304]{1,0:T(4,128)S(1)}, f32[4,2304]{1,0:T(4,128)}, u32[]{:S(2)}) copy-start(f32[4,2304]{1,0:T(4,128)} %gains.7) | copy-start | bytes 110596
  585.9 55.2 %copy-start.9 = (f32[4,2304]{1,0:T(4,128)S(1)}, f32[4,2304]{1,0:T(4,128)}, u32[]{:S(2)}) copy-start(f32[4,2304]{1,0:T(4,128)} %param.21) | copy-start | bytes 110596
  585.9 55.3 %copy-start.10 = (f32[4,2304]{1,0:T(4,128)S(1)}, f32[4,2304]{1,0:T(4,128)}, u32[]{:S(2)}) copy-start(f32[4,2304]{1,0:T(4,128)} %param.22) | copy-start | bytes 110596
  585.9 56.0 %copy-start.5 = (bf16[128,2304]{1,0:T(8,128)(2,1)S(1)}, bf16[128,2304]{1,0:T(8,128)(2,1)}, u32[]{:S(2)}) copy-start(bf16[128,2304]{1,0:T(8,128)(2,1)} %get-tuple-element.60) | copy-start | bytes 1769476
  585.9 56.8 %copy-start.2 = (f32[128,2304]{1,0:T(8,128)S(1)}, f32[128,2304]{1,0:T(8,128)}, u32[]{:S(2)}) copy-start(f32[128,2304]{1,0:T(8,128)} %get-tuple-element.71) | copy-start | bytes 3538948
  640.0 3.7 copy-start.3
  641.2 3.5 copy-start.7
  645.5 7.2 %copy-start.1 = (f32[288,4,256]{2,1,0:T(4,128)S(1)}, f32[288,4,256]{2,1,0:T(4,128)}, u32[]{:S(2)}) copy-start(f32[288,4,256]{2,1,0:T(4,128)} %get-tuple-element.137) | copy-start | bytes 3538948
  645.5 8.2 %copy-start.6 = (f32[288,2,256]{2,1,0:T(2,128)S(1)}, f32[288,2,256]{2,1,0:T(2,128)}, u32[]{:S(2)}) copy-start(f32[288,2,256]{2,1,0:T(2,128)} %get-tuple-element.138) | copy-start | bytes 1769476
Sparse Core Ops, SparseCore 0:
  28.8 180.8 all-gather.1
  310.6 80.3 reduce-scatter.4
  408.0 169.1 reduce-scatter.2
